TPU v7x, 32 devices: a whole 2x2x4 slice. The times are simulated.
32 devices in a mesh: rep: 2 (over y), tp: 16 (over z, x, core).
Axes of the slice: x: 2, y: 2, z: 4, core: 2. Of those that a mesh axis runs over, the one named last changes fastest.
Arguments:
- tokens: bfloat16 [64, 8192], P('rep', 'tp'), parts along dimension 0, may hold values from -6 to 6
- attention_gain: bfloat16 [8192], replicated, may hold values from 0.5 to 1.5
- forward_gain: bfloat16 [8192], replicated, may hold values from 0.5 to 1.5
- query_weight: bfloat16 [8192, 8192], P(None, 'tp'), may hold values from -0.0625 to 0.0625
- key_matrix: bfloat16 [8192, 1024], P(None, 'tp'), may hold values from -0.0625 to 0.0625
- value_matrix: bfloat16 [8192, 1024], P(None, 'tp'), may hold values from -0.0625 to 0.0625
- output_weight: bfloat16 [8192, 8192], P('tp'), may hold values from -0.0625 to 0.0625
- gate_weight: bfloat16 [8192, 16384], P(None, 'tp'), may hold values from -0.0625 to 0.0625
- up_weight: bfloat16 [8192, 16384], P(None, 'tp'), may hold values from -0.0625 to 0.0625
- down_weight: bfloat16 [16384, 8192], P('tp'), may hold values from -0.046875 to 0.046875
- adapter_inputs: bfloat16 [32, 8192, 32], P(('rep', 'tp')), parts along dimension 0, may hold values from -0.0625 to 0.0625
- adapter_query: bfloat16 [32, 16, 8192], P('rep', None, 'tp'), parts along dimension 0, may hold values from -0.8984375 to 0.8984375
- adapter_upper: bfloat16 [32, 16, 16384], P('rep', None, 'tp'), parts along dimension 0, may hold values from -0.8984375 to 0.8984375
- adapter_place: int32 [32], P('rep'), parts along dimension 0, may hold values from 0 to 15, each once
- request_adapter: int32 [2], P('rep'), parts along dimension 0, may hold values from 0 to 15
- tree_parents: int32 [2, 32], P('rep'), parts along dimension 0, may hold values from 0 to 30, as said below
Outputs:
- layer_output: bfloat16 [64, 8192], P('rep', 'tp'), parts along dimension 0
There are 2 independent parts, one for each index of `rep`. A program takes and returns all parts, laid end to end along the dimension named above; an argument that names none is the same for every part. Nothing has to cross between parts.
Inputs may be any that keep to these rules, and one draw needn't show every extreme that they name: tree_parents[r, 0] = 0 and tree_parents[r, i] < i for i >= 1: each request's tokens form one tree rooted at its first token; in request 0 the last token's parent is token 30. `adapter_place`: a permutation of the pool rows. `request_adapter`: an adapter number for each request.
All inputs are finite; a program needn't handle non-finite values.
Results may differ from a plain program's by a relative error of at most 0.013.
Values may be sent and summed in bfloat16 or wider, within the bound.
No kernel may reach another device: no remote copies, remote signals or barrier semaphores. Data moves between devices by JAX's collectives and lax.ppermute only.
A program may use at most 192 MiB of HBM per device.

v0:
```python
import jax
import jax.numpy as jnp
from jax import lax
from jax.sharding import PartitionSpec as P

HEAD_SIZE = 128


EPS = 1e-05
ROPE_BASE = 500000.0


def broadcast(x, axis, root):
    mine = lax.axis_index(axis) == root
    return lax.psum(jnp.where(mine, x, jnp.zeros_like(x)), axis)


def partner_2(block, axis, distance):
    count = lax.axis_size(axis)
    route = []
    for low in range(count):
        high = low | 1 << distance
        if high != low and high < count:
            route += [(low, high), (high, low)]
    return lax.ppermute(block, axis, route)


def rms_scale(rows, gain):
    wide = rows.astype(jnp.float32)
    mean_sq = jnp.mean(wide * wide, axis=-1, keepdims=True)
    return (wide * lax.rsqrt(mean_sq + EPS) * gain.astype(jnp.float32)).astype(jnp.bfloat16)


def ancestry(parents):
    tree_width = parents.shape[-1]
    places = jnp.arange(tree_width, dtype=jnp.int32)
    links = (parents[:, :, None] == places[None, None, :]).astype(jnp.float32)
    reach = jnp.maximum(links, jnp.eye(tree_width, dtype=jnp.float32)[None])
    for step in range(int(tree_width).bit_length()):
        reach = jnp.minimum(
            jnp.einsum("rij,rjk->rik", reach, reach, precision=lax.Precision.HIGHEST), 1.0
        )
    tree_depth = jnp.sum(reach, axis=-1) - 1.0
    return (reach, tree_depth)


def apply_rotary(heads, tree_depth):
    half = heads.shape[-1] // 2
    freq = ROPE_BASE ** (-jnp.arange(half, dtype=jnp.float32) * 2.0 / heads.shape[-1])
    angle = tree_depth[:, :, None] * freq[None, None, :]
    cosine = jnp.cos(angle)[:, :, None, :]
    sine = jnp.sin(angle)[:, :, None, :]
    wide = heads.astype(jnp.float32)
    first = wide[..., :half]
    second = wide[..., half:]
    return jnp.concatenate(
        [first * cosine - second * sine, second * cosine + first * sine], axis=-1
    ).astype(jnp.bfloat16)


def join_pair(mine, theirs, flag):
    lower = jnp.concatenate([mine, theirs], axis=1)
    upper = jnp.concatenate([theirs, mine], axis=1)
    return jnp.where(flag == 1, upper, lower)


def body(
    tokens,
    attention_gain,
    forward_gain,
    query_weight,
    key_matrix,
    value_matrix,
    output_weight,
    gate_weight,
    up_weight,
    down_weight,
    adapter_inputs,
    adapter_query,
    adapter_upper,
    adapter_place,
    request_adapter,
    tree_parents,
):
    device = lax.axis_index("tp")
    rows = tokens.shape[0]
    request_list = request_adapter.shape[0]
    tree_width = rows // request_list
    rank = adapter_query.shape[1]
    pool_local = adapter_inputs.shape[0]
    head = HEAD_SIZE
    full_tokens = lax.all_gather(tokens, "tp", axis=1, tiled=True)
    normed = rms_scale(full_tokens, attention_gain)
    slots = adapter_place[request_adapter]
    owners = slots // pool_local
    local_slot = slots % pool_local
    grouped = normed.reshape(request_list, tree_width, -1)
    held = lax.dynamic_index_in_dim(adapter_inputs, local_slot[0], 0, keepdims=False)
    fetched = [broadcast(held, "tp", owners[0])]
    factors = jnp.stack(fetched)
    low_query = jnp.einsum(
        "rtd,rdk->rtk", grouped, factors[:, :, :rank], preferred_element_type=jnp.float32
    ).astype(jnp.bfloat16)
    lift = jnp.einsum(
        "rtk,rkc->rtc",
        low_query,
        adapter_query[request_adapter],
        preferred_element_type=jnp.float32,
    )
    query_local = (
        jnp.dot(normed, query_weight, preferred_element_type=jnp.float32) + lift.reshape(rows, -1)
    ).astype(jnp.bfloat16)
    key_local = jnp.dot(normed, key_matrix, preferred_element_type=jnp.float32).astype(jnp.bfloat16)
    value_local = jnp.dot(normed, value_matrix, preferred_element_type=jnp.float32).astype(
        jnp.bfloat16
    )
    query_cols = query_weight.shape[1]
    query_steps = max(0, (head // query_cols).bit_length() - 1)
    key_steps = (head // key_matrix.shape[1]).bit_length() - 1
    for bit in range(key_steps):
        flag = device >> bit & 1
        key_width = key_local.shape[1]
        with_query = bit < query_steps
        if with_query:
            query_width = query_local.shape[1]
            packed = jnp.concatenate([query_local, key_local, value_local], axis=1)
        else:
            query_width = 0
            packed = jnp.concatenate([key_local, value_local], axis=1)
        partner = partner_2(packed, "tp", bit)
        if with_query:
            query_local = join_pair(query_local, partner[:, :query_width], flag)
        key_other = partner[:, query_width : query_width + key_width]
        value_other = partner[:, query_width + key_width :]
        key_local = join_pair(key_local, key_other, flag)
        value_local = join_pair(value_local, value_other, flag)
    reach, tree_depth = ancestry(tree_parents)
    local_heads = query_local.shape[1] // head
    query_rotated = apply_rotary(
        query_local.reshape(request_list, tree_width, local_heads, head), tree_depth
    )
    key_rotated = apply_rotary(key_local.reshape(request_list, tree_width, 1, head), tree_depth)[
        :, :, 0, :
    ]
    heads_value = value_local.reshape(request_list, tree_width, head)
    scores = jnp.einsum(
        "rqhd,rkd->rhqk", query_rotated, key_rotated, preferred_element_type=jnp.float32
    ) * head ** (-0.5)
    weights = jnp.exp(scores) * reach[:, None, :, :]
    probs = (weights / jnp.sum(weights, axis=-1, keepdims=True)).astype(jnp.bfloat16)
    mixed = jnp.einsum(
        "rhqk,rkd->rqhd", probs, heads_value, preferred_element_type=jnp.float32
    ).astype(jnp.bfloat16)
    mixed = mixed.reshape(rows, local_heads * head)
    offset = (device & (1 << query_steps) - 1) * query_cols
    own_mixed = lax.dynamic_slice_in_dim(mixed, offset, query_cols, 1)
    partial_out = jnp.dot(own_mixed, output_weight, preferred_element_type=jnp.float32)
    feature_cols = tokens.shape[1]
    summed = lax.psum(partial_out, "tp")
    hidden_full = (full_tokens.astype(jnp.float32) + summed).astype(jnp.bfloat16)
    hidden = lax.dynamic_slice_in_dim(hidden_full, device * feature_cols, feature_cols, 1)
    normed_two = rms_scale(hidden_full, forward_gain)
    grouped_two = normed_two.reshape(request_list, tree_width, -1)
    low_up = jnp.einsum(
        "rtd,rdk->rtk", grouped_two, factors[:, :, rank:], preferred_element_type=jnp.float32
    ).astype(jnp.bfloat16)
    lift_up = jnp.einsum(
        "rtk,rkc->rtc", low_up, adapter_upper[request_adapter], preferred_element_type=jnp.float32
    )
    gate = jnp.dot(normed_two, gate_weight, preferred_element_type=jnp.float32)
    upper = jnp.dot(normed_two, up_weight, preferred_element_type=jnp.float32) + lift_up.reshape(
        rows, -1
    )
    active = (jax.nn.silu(gate) * upper).astype(jnp.bfloat16)
    forward = jnp.dot(active, down_weight, preferred_element_type=jnp.float32)
    forward_part = lax.psum_scatter(forward, "tp", scatter_dimension=1, tiled=True)
    return (hidden.astype(jnp.float32) + forward_part).astype(jnp.bfloat16)


def solution(mesh):
    return jax.shard_map(
        body,
        mesh=mesh,
        in_specs=(
            P("rep", "tp"),
            P(),
            P(),
            P(None, "tp"),
            P(None, "tp"),
            P(None, "tp"),
            P("tp", None),
            P(None, "tp"),
            P(None, "tp"),
            P("tp", None),
            P(("rep", "tp"), None, None),
            P("rep", None, "tp"),
            P("rep", None, "tp"),
            P("rep"),
            P("rep"),
            P("rep", None),
        ),
        out_specs=P("rep", "tp"),
        check_vma=False,
    )
```

profile of v0, /device:TPU:0, one launch (start us, length us, event | category | flops | bytes accessed | tf_op | source)
XLA Modules:
  0.0 297.1 jit_solution(12103147544704586909)
XLA Ops:
  7.3 1.3 dynamic-slice.8
  9.2 0.8 broadcast_select_fusion
  10.1 25.1 %all_gather.3 = bf16[32,8192]{1,0:T(8,128)(2,1)S(1)} all-gather(bf16[32,512]{1,0:T(8,128)(2,1)} %param.16), channel_id=1, replica_groups=mesh['rep'=2,'tp'=16] {'tp'}, dimensions={1}, use_global_device_ids=true | all-gather | bytes 557056 | tf_op jit(solution)/shard_map/all_gather | solution.py:92
  35.3 0.2 fusion.12
  35.5 0.7 convert_element_type.142
  36.3 0.5 convolution_convert_fusion.1
  36.7 1.7 convolution_convert_fusion.2
  38.5 0.4 collective-permute-start
  38.9 5.0 %fusion.71 = f32[32,512]{1,0:T(8,128)S(1)} fusion(bf16[8192,512]{1,0:T(8,128)(2,1)} %param.19, bf16[32,8192]{1,0:T(8,128)(2,1)S(1)} %all_gather.3, f32[8192]{0:T(1024)S(1)} %convert_element_type.142, f32[32]{0:T(128)S(1)} %add_rsqrt_fusion.1), kind=kOutput, calls=%fused_computation.104 | convolution fusion | flops 269484032 | bytes 9011328 | tf_op jit(solution)/shard_map/dot_general | solution.py:111
  44.0 0.2 convolution_minimum_fusion.5
  44.5 0.1 convolution_minimum_fusion.2
  44.8 0.2 fusion.78
  45.5 58.5 %all-reduce.3.cloned.1.call-done = bf16[1,8192,32]{1,2,0:T(8,128)(2,1)} async-done(((bf16[1,8192,32]{1,2,0:T(8,128)(2,1)}), bf16[1,8192,32]{1,2,0:T(8,128)(2,1)}) %all-reduce.3.cloned.1.call-update) | async-done | bytes 524304 | tf_op jit(solution)/shard_map/psum | solution.py:15
  103.9 1.4 fusion.6
  105.5 0.3 fusion.79
  105.8 0.2 fusion.7
  106.1 6.0 %fusion.25 = f32[32,8192]{1,0:T(8,128)} fusion(bf16[512,8192]{1,0:T(8,128)(2,1)} %param.22, bf16[4,8,4,128]{3,2,1,0:T(4,128)(2,1)S(1)} %bitcast.74), kind=kOutput, calls=%fused_computation.53 | convolution fusion | flops 268435456 | bytes 9469952 | tf_op jit(solution)/shard_map/dot_general | solution.py:157
  112.1 93.8 %all-reduce.5.cloned.1.call-done = f32[32,8192]{1,0:T(8,128)} async-done(((f32[32,8192]{1,0:T(8,128)}), f32[32,8192]{1,0:T(8,128)}) %all-reduce.5.cloned.1.call-update) | async-done | bytes 1048592 | tf_op jit(solution)/shard_map/psum | solution.py:159
  205.9 1.5 fusion.9
  207.4 8.8 %fusion.67 = f32[32,1024]{1,0:T(8,128)S(1)} fusion(bf16[8192,1024]{1,0:T(8,128)(2,1)} %param.23, bf16[32,8192]{1,0:T(8,128)(2,1)S(1)} %get-tuple-element.39, f32[8192]{0:T(1024)S(1)} %convert_element_type.160, f32[32]{0:T(128)S(1)} %add_rsqrt_fusion), kind=kOutput, calls=%fused_computation.103 | convolution fusion | flops 537919488 | bytes 17465472 | tf_op jit(solution)/shard_map/dot_general | solution.py:170
  216.3 1.4 fusion.8
  217.7 14.7 %fusion.16 = f32[32,8192]{1,0:T(8,128)} fusion(bf16[1024,8192]{1,0:T(8,128)(2,1)} %param.25, f32[32,1024]{1,0:T(8,128)S(1)} %fusion.8, bf16[8192,1024]{1,0:T(8,128)(2,1)} %param.24, f32[32,1024]{1,0:T(8,128)S(1)} %fusion.67, bf16[32,8192]{1,0:T(8,128)(2,1)S(1)} %get-tuple-element.39, f32[8192]{0:T(1024)S(1)} %convert_element_type.160, f32[32]{0:T(128)S(1)} %add_rsqrt_fusion), kind=kOutput, calls=%fused_computation.35 | convolution fusion | flops 1075019776 | bytes 35422336 | tf_op jit(solution)/shard_map/dot_general | solution.py:175
  232.3 56.7 %reduce-scatter.2.cloned.1.call-done = f32[32,512]{1,0:T(8,128)} async-done(((f32[32,8192]{1,0:T(8,128)}), f32[32,512]{1,0:T(8,128)}) %reduce-scatter.2.cloned.1.call-update) | async-done | bytes 65552 | tf_op jit(solution)/shard_map/reduce_scatter | solution.py:176
  289.1 1.5 add_convert_fusion
  (35 shorter events, 1.4 us)
Async XLA Ops:
  6.5 29.7 %copy-start = (bf16[8192,64]{0,1:T(8,128)(2,1)S(1)}, bf16[8192,64]{0,1:T(8,128)(2,1)}, u32[]{:S(2)}) copy-start(bf16[8192,64]{0,1:T(8,128)(2,1)} %param.21) | copy-start | bytes 3145732
  6.5 37.4 %copy-start.3 = (s32[1,32]{1,0:T(1,128)S(1)}, s32[1,32]{1,0:T(1,128)}, u32[]{:S(2)}) copy-start(s32[1,32]{1,0:T(1,128)} %param.31) | copy-start | bytes 388
  6.5 97.4 %all-reduce.3.cloned.1.call-start = ((), (), s32[]{:S(2)}) async-start(), calls=%async_computation.1 | async-start | bytes 1048576 | tf_op jit(solution)/shard_map/psum | solution.py:15
  10.1 195.8 %all-reduce.5.cloned.1.call-start = ((), (), s32[]{:S(2)}) async-start(), calls=%async_computation.2 | async-start | bytes 2097152 | tf_op jit(solution)/shard_map/psum | solution.py:159
  38.5 6.7 %collective-permute-start = (bf16[32,128]{1,0:T(8,128)(2,1)S(1)}, bf16[32,128]{1,0:T(8,128)(2,1)S(1)}, u32[]{:S(2)}, u32[]{:S(2)}) collective-permute-start(bf16[32,128]{1,0:T(8,128)(2,1)S(1)} %pad_maximum_fusion), channel_id=1, source_target_pairs={{0,1},{1,0},{2,3},{3,2},{4,5},{5,4},{6,7},{7,6},{8,9},{9,8},{10,11... | collective-permute-start | bytes 24584 | tf_op jit(solution)/shard_map/ppermute | solution.py:25
  38.9 73.2 %copy-start.2 = (bf16[8192]{0:T(1024)(128)(2,1)S(1)}, bf16[8192]{0:T(1024)(128)(2,1)}, u32[]{:S(2)}) copy-start(bf16[8192]{0:T(1024)(128)(2,1)} %param.18) | copy-start | bytes 49156
  112.0 104.3 %copy-start.4 = (bf16[1,8192,32]{1,2,0:T(8,128)(2,1)S(1)}, bf16[1,8192,32]{1,2,0:T(8,128)(2,1)}, u32[]{:S(2)}) copy-start(bf16[1,8192,32]{1,2,0:T(8,128)(2,1)} %all-reduce.3.cloned.1.call-done) | copy-start | bytes 1572868
  112.0 177.0 %reduce-scatter.2.cloned.1.call-start = ((), (), s32[]{:S(2)}) async-start(), calls=%async_computation.3 | async-start | bytes 1114112 | tf_op jit(solution)/shard_map/reduce_scatter | solution.py:176
  216.3 74.3 %copy-start.1 = (bf16[8192,64]{0,1:T(8,128)(2,1)S(1)}, bf16[8192,64]{0,1:T(8,128)(2,1)}, u32[]{:S(2)}) copy-start(bf16[8192,64]{0,1:T(8,128)(2,1)} %param.21) | copy-start | bytes 3145732
Sparse Core Ops, SparseCore 0:
  10.8 93.1 all-reduce.2
  112.2 93.7 all-reduce.4
  232.5 56.5 reduce-scatter.1
where the time goes:
time: 298 us; the launch traced here: 297 us
  waiting for transfers between devices  209 us (70%)
  matrix products  40.8 us (14%)
  blocking collectives  25.1 us (8%)
  between operations  14.7 us (5%)
  other arithmetic  5.37 us (2%)
    psum x1, waiting for transfers between devices, body(): summed = lax.psum(partial_out, 'tp')  93.8 us
    psum x1, waiting for transfers between devices, broadcast(): return lax.psum(jnp.where(mine, x, jnp.zeros_like(x)), axis)  58.5 us
    reduce_scatter x1, waiting for transfers between devices, body(): lax.psum_scatter(forward, 'tp', scatter_dimension=1, tiled=True)  56.7 us
    all_gather x1, blocking collectives, body(): full_tokens = lax.all_gather(tokens, 'tp', axis=1, tiled=True)  25.1 us
    dot_general x1, matrix products, body(): forward = jnp.dot(active, down_weight, preferred_element_type=jnp.float32)  14.7 us
    dot_general x1, matrix products, body(): gate = jnp.dot(normed_two, gate_weight, preferred_element_type=jnp.float32)  8.83 us
  transfers between devices with their start and end apart: 4, of which 3 were waited for; matrix products, arithmetic and copies ran while one was open for 3% of the time, Pallas kernels for 0%

commit v1 on v0

--- a/solution.py
+++ b/solution.py
@@ -10,9 +10,53 @@
 ROPE_BASE = 500000.0
 
 
-def broadcast(x, axis, root):
-    mine = lax.axis_index(axis) == root
-    return lax.psum(jnp.where(mine, x, jnp.zeros_like(x)), axis)
+def core_groups(axis):
+    count = lax.axis_size(axis)
+    return [list(range(core, count, 2)) for core in range(2)]
+
+
+def exchange(blocks, axis):
+    return lax.all_to_all(
+        blocks, axis, 0, 0, axis_index_groups=core_groups(axis), tiled=True
+    )
+
+
+def by_core(mine, theirs, core):
+    even = jnp.where(core == 0, mine, theirs)
+    odd = jnp.where(core == 0, theirs, mine)
+    return jnp.stack([even, odd], axis=1)
+
+
+def gather_features(part, axis):
+    chips = lax.axis_size(axis) // 2
+    core = lax.axis_index(axis) & 1
+    mine = exchange(jnp.broadcast_to(part[None], (chips,) + part.shape), axis)
+    theirs = partner_2(mine, axis, 0)
+    both = by_core(mine, theirs, core).reshape((2 * chips,) + part.shape)
+    return jnp.moveaxis(both, 0, 1).reshape(part.shape[0], -1)
+
+
+def sum_features(partial, axis):
+    count = lax.axis_size(axis)
+    core = lax.axis_index(axis) & 1
+    rows = partial.shape[0]
+    split = partial.reshape(rows, count // 2, 2, -1)
+    even = split[:, :, 0]
+    odd = split[:, :, 1]
+    mine = jnp.where(core == 0, even, odd)
+    theirs = jnp.where(core == 0, odd, even).astype(jnp.bfloat16)
+    pair = (mine + partner_2(theirs, axis, 0).astype(jnp.float32)).astype(jnp.bfloat16)
+    got = exchange(jnp.moveaxis(pair, 1, 0), axis)
+    return jnp.sum(got.astype(jnp.float32), axis=0)
+
+
+def from_owner(mine, owner, axis):
+    core = lax.axis_index(axis) & 1
+    held = jnp.where(lax.axis_index(axis) == owner, mine, jnp.zeros_like(mine))
+    held = held + partner_2(held, axis, 0)
+    chips = lax.axis_size(axis) // 2
+    got = exchange(jnp.broadcast_to(held[None], (chips,) + held.shape), axis)
+    return lax.dynamic_index_in_dim(got, owner >> 1, 0, keepdims=False)
 
 
 def partner_2(block, axis, distance):
@@ -89,18 +133,15 @@
     rank = adapter_query.shape[1]
     pool_local = adapter_inputs.shape[0]
     head = HEAD_SIZE
-    full_tokens = lax.all_gather(tokens, "tp", axis=1, tiled=True)
+    full_tokens = gather_features(tokens, "tp")
     normed = rms_scale(full_tokens, attention_gain)
     slots = adapter_place[request_adapter]
-    owners = slots // pool_local
-    local_slot = slots % pool_local
-    grouped = normed.reshape(request_list, tree_width, -1)
-    held = lax.dynamic_index_in_dim(adapter_inputs, local_slot[0], 0, keepdims=False)
-    fetched = [broadcast(held, "tp", owners[0])]
-    factors = jnp.stack(fetched)
-    low_query = jnp.einsum(
-        "rtd,rdk->rtk", grouped, factors[:, :, :rank], preferred_element_type=jnp.float32
-    ).astype(jnp.bfloat16)
+    owner = slots[0] // pool_local
+    factors = lax.dynamic_index_in_dim(adapter_inputs, slots[0] % pool_local, 0, keepdims=False)
+    low_held = jnp.dot(normed, factors[:, :rank], preferred_element_type=jnp.float32).astype(
+        jnp.bfloat16
+    )
+    low_query = from_owner(low_held, owner, "tp")[None]
     lift = jnp.einsum(
         "rtk,rkc->rtc",
         low_query,
@@ -155,15 +196,14 @@
     offset = (device & (1 << query_steps) - 1) * query_cols
     own_mixed = lax.dynamic_slice_in_dim(mixed, offset, query_cols, 1)
     partial_out = jnp.dot(own_mixed, output_weight, preferred_element_type=jnp.float32)
-    feature_cols = tokens.shape[1]
-    summed = lax.psum(partial_out, "tp")
-    hidden_full = (full_tokens.astype(jnp.float32) + summed).astype(jnp.bfloat16)
-    hidden = lax.dynamic_slice_in_dim(hidden_full, device * feature_cols, feature_cols, 1)
+    summed = sum_features(partial_out, "tp")
+    hidden = (tokens.astype(jnp.float32) + summed).astype(jnp.bfloat16)
+    hidden_full = gather_features(hidden, "tp")
     normed_two = rms_scale(hidden_full, forward_gain)
-    grouped_two = normed_two.reshape(request_list, tree_width, -1)
-    low_up = jnp.einsum(
-        "rtd,rdk->rtk", grouped_two, factors[:, :, rank:], preferred_element_type=jnp.float32
-    ).astype(jnp.bfloat16)
+    low_held_two = jnp.dot(normed_two, factors[:, rank:], preferred_element_type=jnp.float32).astype(
+        jnp.bfloat16
+    )
+    low_up = from_owner(low_held_two, owner, "tp")[None]
     lift_up = jnp.einsum(
         "rtk,rkc->rtc", low_up, adapter_upper[request_adapter], preferred_element_type=jnp.float32
     )
@@ -173,7 +213,7 @@
     )
     active = (jax.nn.silu(gate) * upper).astype(jnp.bfloat16)
     forward = jnp.dot(active, down_weight, preferred_element_type=jnp.float32)
-    forward_part = lax.psum_scatter(forward, "tp", scatter_dimension=1, tiled=True)
+    forward_part = sum_features(forward, "tp")
     return (hidden.astype(jnp.float32) + forward_part).astype(jnp.bfloat16)
 
 

time: 298 us -> 141 us (0.47)
  waiting for transfers between devices: 209 us -> 18.8 us
  local copies, waits for them, and re-layouts: 1.54 us -> 21.5 us
  starting transfers between devices: 0.44 us -> 15.4 us
  blocking collectives: 25.1 us -> 39.4 us
  between operations: 14.7 us -> 2.31 us
    psum x2 -> x0, waiting for transfers between devices: 152 us -> none  [the longest x1 93.8 us: body(): summed = lax.psum(partial_out, 'tp')]
    reduce_scatter x1 -> x0, waiting for transfers between devices: 56.7 us -> none  [body(): lax.psum_scatter(forward, 'tp', scatter_dimension=1, tiled=True)]
    all_to_all x0 -> x3, blocking collectives: none -> 39.4 us  [exchange(): lax.all_to_all(blocks, axis, 0, 0, axis_index_groups=core_groups(axis), t...]
    all_gather x1 -> x0, blocking collectives: 25.1 us -> none  [body(): full_tokens = lax.all_gather(tokens, 'tp', axis=1, tiled=True)]
    all_to_all x0 -> x3, starting transfers between devices: none -> 14.4 us  [exchange(): lax.all_to_all(blocks, axis, 0, 0, axis_index_groups=core_groups(axis), t...]
    all_to_all x0 -> x3, waiting for transfers between devices: none -> 13.3 us  [exchange(): lax.all_to_all(blocks, axis, 0, 0, axis_index_groups=core_groups(axis), t...]
    dot_general x0 -> x1, local copies, waits for them, and re-layouts: none -> 12 us  [body(): jnp.dot(own_mixed, output_weight, preferred_element_type=jnp.float32)]
    ppermute x1 -> x7, waiting for transfers between devices: 0.01 us -> 5.51 us  [partner_2(): return lax.ppermute(block, axis, route)]
  transfers between devices with their start and end apart: 4 -> 10, of which waited for: 3 -> 6; matrix products, arithmetic and copies ran while one was open for 3% -> 22% of each run, Pallas kernels for 0% -> 0%
where the time goes in v1:
time: 141 us; the launch traced here: 140 us
  blocking collectives  39.4 us (28%)
  matrix products  37.9 us (27%)
  local copies, waits for them, and re-layouts  21.5 us (15%)
  waiting for transfers between devices  18.8 us (13%)
  starting transfers between devices  15.4 us (11%)
  other arithmetic  5.07 us (4%)
  between operations  2.31 us (2%)
    all_to_all x3, blocking collectives, exchange(): lax.all_to_all(blocks, axis, 0, 0, axis_index_groups=core_groups(axis), t...  39.4 us
    all_to_all x3, starting transfers between devices, exchange(): lax.all_to_all(blocks, axis, 0, 0, axis_index_groups=core_groups(axis), t...  14.4 us
    dot_general x1, matrix products, body(): forward = jnp.dot(active, down_weight, preferred_element_type=jnp.float32)  13.7 us
    all_to_all x3, waiting for transfers between devices, exchange(): lax.all_to_all(blocks, axis, 0, 0, axis_index_groups=core_groups(axis), t...  13.3 us
    dot_general x1, local copies, waits for them, and re-layouts, body(): jnp.dot(own_mixed, output_weight, preferred_element_type=jnp.float32)  12 us
    dot_general x1, matrix products, body(): gate = jnp.dot(normed_two, gate_weight, preferred_element_type=jnp.float32)  8.74 us
    dot_general x1, matrix products, body(): jnp.dot(own_mixed, output_weight, preferred_element_type=jnp.float32)  5.9 us
    ppermute x7, waiting for transfers between devices, partner_2(): return lax.ppermute(block, axis, route)  5.51 us
  transfers between devices with their start and end apart: 10, of which 6 were waited for; matrix products, arithmetic and copies ran while one was open for 22% of the time, Pallas kernels for 0%

profile of v1, /device:TPU:0, one launch (start us, length us, event | category | flops | bytes accessed | tf_op | source)
XLA Modules:
  0.0 140.4 jit_solution(16458479389300838250)
XLA Ops:
  0.0 1.6 %broadcast_in_dim.10 = bf16[8,32,512]{2,1,0:T(8,128)(2,1)} broadcast(bf16[32,512]{1,0:T(8,128)(2,1)} %param.16), dimensions={1,2} | broadcast | bytes 294912 | tf_op jit(solution)/shard_map/broadcast_in_dim | solution.py:33
  1.6 7.3 %all-to-all-start = ((bf16[8,32,512]{2,1,0:T(8,128)(2,1)}), bf16[8,32,512]{2,1,0:T(8,128)(2,1)S(1)}, u32[]{:S(2)}, u32[]{:S(2)}) async-start(bf16[8,32,512]{2,1,0:T(8,128)(2,1)} %broadcast_in_dim.10), calls=%async_computation | async-start | bytes 524288 | tf_op jit(solution)/shard_map/all_to_all | solution.py:19
  8.9 0.8 fusion.46
  10.7 7.1 %all-to-all-done = bf16[8,32,512]{2,1,0:T(8,128)(2,1)S(1)} async-done(((bf16[8,32,512]{2,1,0:T(8,128)(2,1)}), bf16[8,32,512]{2,1,0:T(8,128)(2,1)S(1)}, u32[]{:S(2)}, u32[]{:S(2)}) %all-to-all-start) | async-done | bytes 262176 | tf_op jit(solution)/shard_map/all_to_all | solution.py:19
  18.5 1.2 dynamic-slice.8
  21.8 12.0 %copy.64 = bf16[8192,512]{1,0:T(8,128)(2,1)} copy(bf16[8192,512]{0,1:T(8,128)(2,1)} %bitcast.149) | data formatting | bytes 16777216 | tf_op jit(solution)/shard_map/dot_general | solution.py:198
  35.4 4.9 %fusion.76 = f32[32,512]{1,0:T(8,128)S(1)} fusion(bf16[32,8192]{1,0:T(8,128)(2,1)S(1)} %multiply_convert_fusion.1, bf16[8192,512]{1,0:T(8,128)(2,1)} %param.19), kind=kOutput, calls=%fused_computation.127 | convolution fusion | flops 268435456 | bytes 8978432 | tf_op jit(solution)/shard_map/dot_general | solution.py:152
  42.0 3.6 %all-to-all-start.1 = ((bf16[8,2,256]{2,1,0:T(2,128)(2,1)}), bf16[8,2,256]{2,1,0:T(2,128)(2,1)S(1)}, u32[]{:S(2)}, u32[]{:S(2)}) async-start(bf16[8,2,256]{2,1,0:T(2,128)(2,1)} %reshape.570), calls=%async_computation.1 | async-start | bytes 16384 | tf_op jit(solution)/shard_map/all_to_all | solution.py:19
  45.9 6.2 %all-to-all-done.1 = bf16[8,2,256]{2,1,0:T(2,128)(2,1)S(1)} async-done(((bf16[8,2,256]{2,1,0:T(2,128)(2,1)}), bf16[8,2,256]{2,1,0:T(2,128)(2,1)S(1)}, u32[]{:S(2)}, u32[]{:S(2)}) %all-to-all-start.1) | async-done | bytes 8224 | tf_op jit(solution)/shard_map/all_to_all | solution.py:19
  52.2 0.9 fusion.6
  53.8 5.9 %fusion.34 = f32[32,8,2,512]{3,0,2,1:T(8,128)S(1)} fusion(bf16[8,2,512,512]{3,2,1,0:T(8,128)(2,1)} %bitcast.148, bf16[32,512,1,1]{1,0,2,3:T(8,128)(2,1)S(1)} %reshape.568), kind=kOutput, calls=%fused_computation.71 | convolution fusion | flops 268435456 | bytes 9469952 | tf_op jit(solution)/shard_map/dot_general | solution.py:198
  59.9 1.5 %collective-permute-done.3 = bf16[32,8,512]{2,0,1:T(8,128)(2,1)S(1)} collective-permute-done((bf16[32,8,512]{2,0,1:T(8,128)(2,1)S(1)}, bf16[32,8,512]{2,0,1:T(8,128)(2,1)S(1)}, u32[]{:S(2)}, u32[]{:S(2)}) %collective-permute-start.3) | collective-permute-done | bytes 262176 | tf_op jit(solution)/shard_map/ppermute | solution.py:69
  61.5 11.9 %all_to_all.30 = bf16[8,32,512]{2,1,0:T(8,128)(2,1)S(1)} all-to-all(bf16[8,32,512]{2,1,0:T(8,128)(2,1)S(1)} %fusion.18), channel_id=1, replica_groups={{0,2,4,6,8,10,12,14},{1,3,5,7,9,11,13,15},{16,18,20,22,24,26,28,30},{17..., dimensions={0} | all-to-all | bytes 524288 | tf_op jit(solution)/shard_map/all_to_all | solution.py:19
  73.5 12.4 %all_to_all.31 = bf16[8,32,512]{2,1,0:T(8,128)(2,1)S(1)} all-to-all(bf16[8,32,512]{2,1,0:T(8,128)(2,1)S(1)} %broadcast_in_dim.13), channel_id=1, replica_groups={{0,2,4,6,8,10,12,14},{1,3,5,7,9,11,13,15},{16,18,20,22,24,26,28,30},{17..., dimensions={0} | all-to-all | bytes 524288 | tf_op jit(solution)/shard_map/all_to_all | solution.py:19
  86.0 1.5 %collective-permute-done.4 = bf16[8,32,512]{2,1,0:T(8,128)(2,1)S(1)} collective-permute-done((bf16[8,32,512]{2,1,0:T(8,128)(2,1)S(1)}, bf16[8,32,512]{2,1,0:T(8,128)(2,1)S(1)}, u32[]{:S(2)}, u32[]{:S(2)}) %collective-permute-start.4) | collective-permute-done | bytes 262176 | tf_op jit(solution)/shard_map/ppermute | solution.py:69
  88.6 1.0 collective-permute-done.5
  90.4 3.6 %all-to-all-start.4 = ((bf16[8,2,256]{2,1,0:T(2,128)(2,1)}), bf16[8,2,256]{2,1,0:T(2,128)(2,1)S(1)}, u32[]{:S(2)}, u32[]{:S(2)}) async-start(bf16[8,2,256]{2,1,0:T(2,128)(2,1)} %reshape.572), calls=%async_computation.4 | async-start | bytes 16384 | tf_op jit(solution)/shard_map/all_to_all | solution.py:19
  94.0 8.7 %fusion.77 = f32[32,1024]{1,0:T(8,128)S(1)} fusion(bf16[32,8192]{1,0:T(8,128)(2,1)S(1)} %multiply_convert_fusion, bf16[8192,1024]{1,0:T(8,128)(2,1)} %param.23), kind=kOutput, calls=%fused_computation.128 | convolution fusion | flops 536870912 | bytes 17432576 | tf_op jit(solution)/shard_map/dot_general | solution.py:210
  102.8 0.9 fusion.32
  103.8 13.7 %fusion.10 = f32[32,8192]{1,0:T(8,128)S(1)} fusion(bf16[1024,8192]{1,0:T(8,128)(2,1)} %param.25, f32[32,1024]{1,0:T(8,128)S(1)} %fusion.32, bf16[32,8192]{1,0:T(8,128)(2,1)S(1)} %multiply_convert_fusion, bf16[8192,1024]{1,0:T(8,128)(2,1)} %param.24, f32[32,1024]{1,0:T(8,128)S(1)} %fusion.77), kind=kOutput, calls=%fused_computation.28 | convolution fusion | flops 1073971200 | bytes 35389440 | tf_op jit(solution)/shard_map/dot_general | solution.py:215
  117.5 1.9 %reshape.497 = f32[32,8,2,512]{3,2,1,0:T(2,128)} reshape(f32[32,8192]{1,0:T(8,128)S(1)} %fusion.10) | data formatting | bytes 2097152 | tf_op jit(solution)/shard_map/reshape | solution.py:43
  119.3 2.6 %fusion.71 = (f32[32,8,1,512]{3,2,1,0:T(1,128)S(1)}, f32[32,8,1,512]{3,2,1,0:T(1,128)S(1)}) fusion(f32[32,8,2,512]{3,2,1,0:T(2,128)} %reshape.497), kind=kLoop, calls=%fused_computation.120 | loop fusion | bytes 2097152 | tf_op jit(solution)/shard_map/slice | solution.py:45
  122.7 1.4 %collective-permute-done.6 = bf16[32,8,512]{2,0,1:T(8,128)(2,1)S(1)} collective-permute-done((bf16[32,8,512]{2,0,1:T(8,128)(2,1)S(1)}, bf16[32,8,512]{2,0,1:T(8,128)(2,1)S(1)}, u32[]{:S(2)}, u32[]{:S(2)}) %collective-permute-start.6) | collective-permute-done | bytes 262176 | tf_op jit(solution)/shard_map/ppermute | solution.py:69
  124.7 15.0 %all_to_all.32 = bf16[8,32,512]{2,1,0:T(8,128)(2,1)S(1)} all-to-all(bf16[8,32,512]{2,1,0:T(8,128)(2,1)S(1)} %fusion.17), channel_id=1, replica_groups={{0,2,4,6,8,10,12,14},{1,3,5,7,9,11,13,15},{16,18,20,22,24,26,28,30},{17..., dimensions={0} | all-to-all | bytes 524288 | tf_op jit(solution)/shard_map/all_to_all | solution.py:19
  (80 shorter events, 10.3 us)
Async XLA Ops:
  0.0 40.3 %copy-start = (bf16[8192,64]{0,1:T(8,128)(2,1)S(1)}, bf16[8192,64]{0,1:T(8,128)(2,1)}, u32[]{:S(2)}) copy-start(bf16[8192,64]{0,1:T(8,128)(2,1)} %param.21) | copy-start | bytes 3145732
  0.0 34.6 %copy-start.3 = (bf16[1,8192,32]{1,2,0:T(8,128)(2,1)S(1)}, bf16[1,8192,32]{1,2,0:T(8,128)(2,1)}, u32[]{:S(2)}) copy-start(bf16[1,8192,32]{1,2,0:T(8,128)(2,1)} %param.26) | copy-start | bytes 1572868
  1.6 16.2 %all-to-all-start = ((bf16[8,32,512]{2,1,0:T(8,128)(2,1)}), bf16[8,32,512]{2,1,0:T(8,128)(2,1)S(1)}, u32[]{:S(2)}, u32[]{:S(2)}) async-start(bf16[8,32,512]{2,1,0:T(8,128)(2,1)} %broadcast_in_dim.10), calls=%async_computation | async-start | bytes 524288 | tf_op jit(solution)/shard_map/all_to_all | solution.py:19
  17.8 16.2 %collective-permute-start = (bf16[8,32,512]{2,1,0:T(8,128)(2,1)S(1)}, bf16[8,32,512]{2,1,0:T(8,128)(2,1)S(1)}, u32[]{:S(2)}, u32[]{:S(2)}) collective-permute-start(bf16[8,32,512]{2,1,0:T(8,128)(2,1)S(1)} %all-to-all-done), channel_id=1, source_target_pairs={{0,1},{1,0},{2,3},{3,2},{4,5},{5,4},{6,7},{7,6},{8,9},{9,8},{10,11... | collective-permute-start | bytes 786440 | tf_op jit(solution)/shard_map/ppermute | solution.py:69
  33.8 7.0 %copy-start.2 = (bf16[8192,64]{0,1:T(8,128)(2,1)S(1)}, bf16[8192,64]{0,1:T(8,128)(2,1)}, u32[]{:S(2)}) copy-start(bf16[8192,64]{0,1:T(8,128)(2,1)} %param.20) | copy-start | bytes 3145732
  34.9 38.6 %copy-start.4 = (bf16[32,512]{1,0:T(8,128)(2,1)S(1)}, bf16[32,512]{1,0:T(8,128)(2,1)}, u32[]{:S(2)}) copy-start(bf16[32,512]{1,0:T(8,128)(2,1)} %param.16) | copy-start | bytes 98308
  34.9 51.1 %copy-start.5 = (bf16[8192]{0:T(1024)(128)(2,1)S(1)}, bf16[8192]{0:T(1024)(128)(2,1)}, u32[]{:S(2)}) copy-start(bf16[8192]{0:T(1024)(128)(2,1)} %param.18) | copy-start | bytes 49156
  34.9 6.4 %collective-permute-start.2 = (bf16[32,16]{0,1:T(8,128)(2,1)S(1)}, bf16[32,16]{0,1:T(8,128)(2,1)S(1)}, u32[]{:S(2)}, u32[]{:S(2)}) collective-permute-start(bf16[32,16]{0,1:T(8,128)(2,1)S(1)} %fusion.8), channel_id=1, source_target_pairs={{0,1},{1,0},{2,3},{3,2},{4,5},{5,4},{6,7},{7,6},{8,9},{9,8},{10,11... | collective-permute-start | bytes 3080 | tf_op jit(solution)/shard_map/ppermute | solution.py:69
  41.3 4.3 %collective-permute-start.1 = (bf16[32,128]{1,0:T(8,128)(2,1)S(1)}, bf16[32,128]{1,0:T(8,128)(2,1)S(1)}, u32[]{:S(2)}, u32[]{:S(2)}) collective-permute-start(bf16[32,128]{1,0:T(8,128)(2,1)S(1)} %pad_maximum_fusion), channel_id=1, source_target_pairs={{0,1},{1,0},{2,3},{3,2},{4,5},{5,4},{6,7},{7,6},{8,9},{9,8},{10,11... | collective-permute-start | bytes 24584 | tf_op jit(solution)/shard_map/ppermute | solution.py:69
  42.0 10.1 %all-to-all-start.1 = ((bf16[8,2,256]{2,1,0:T(2,128)(2,1)}), bf16[8,2,256]{2,1,0:T(2,128)(2,1)S(1)}, u32[]{:S(2)}, u32[]{:S(2)}) async-start(bf16[8,2,256]{2,1,0:T(2,128)(2,1)} %reshape.570), calls=%async_computation.1 | async-start | bytes 16384 | tf_op jit(solution)/shard_map/all_to_all | solution.py:19
  59.8 1.6 %collective-permute-start.3 = (bf16[32,8,512]{2,0,1:T(8,128)(2,1)S(1)}, bf16[32,8,512]{2,0,1:T(8,128)(2,1)S(1)}, u32[]{:S(2)}, u32[]{:S(2)}) collective-permute-start(bf16[32,8,512]{2,0,1:T(8,128)(2,1)S(1)} %fusion.15), channel_id=1, source_target_pairs={{0,1},{1,0},{2,3},{3,2},{4,5},{5,4},{6,7},{7,6},{8,9},{9,8},{10,11... | collective-permute-start | bytes 786440 | tf_op jit(solution)/shard_map/ppermute | solution.py:69
  86.0 1.5 %collective-permute-start.4 = (bf16[8,32,512]{2,1,0:T(8,128)(2,1)S(1)}, bf16[8,32,512]{2,1,0:T(8,128)(2,1)S(1)}, u32[]{:S(2)}, u32[]{:S(2)}) collective-permute-start(bf16[8,32,512]{2,1,0:T(8,128)(2,1)S(1)} %all_to_all.31), channel_id=1, source_target_pairs={{0,1},{1,0},{2,3},{3,2},{4,5},{5,4},{6,7},{7,6},{8,9},{9,8},{10,11... | collective-permute-start | bytes 786440 | tf_op jit(solution)/shard_map/ppermute | solution.py:69
  88.5 1.2 collective-permute-start.5
  90.4 12.3 %all-to-all-start.4 = ((bf16[8,2,256]{2,1,0:T(2,128)(2,1)}), bf16[8,2,256]{2,1,0:T(2,128)(2,1)S(1)}, u32[]{:S(2)}, u32[]{:S(2)}) async-start(bf16[8,2,256]{2,1,0:T(2,128)(2,1)} %reshape.572), calls=%async_computation.4 | async-start | bytes 16384 | tf_op jit(solution)/shard_map/all_to_all | solution.py:19
  103.8 36.6 %copy-start.1 = (bf16[8192,64]{0,1:T(8,128)(2,1)S(1)}, bf16[8192,64]{0,1:T(8,128)(2,1)}, u32[]{:S(2)}) copy-start(bf16[8192,64]{0,1:T(8,128)(2,1)} %param.21) | copy-start | bytes 3145732
  122.5 1.6 %collective-permute-start.6 = (bf16[32,8,512]{2,0,1:T(8,128)(2,1)S(1)}, bf16[32,8,512]{2,0,1:T(8,128)(2,1)S(1)}, u32[]{:S(2)}, u32[]{:S(2)}) collective-permute-start(bf16[32,8,512]{2,0,1:T(8,128)(2,1)S(1)} %fusion.16), channel_id=1, source_target_pairs={{0,1},{1,0},{2,3},{3,2},{4,5},{5,4},{6,7},{7,6},{8,9},{9,8},{10,11... | collective-permute-start | bytes 786440 | tf_op jit(solution)/shard_map/ppermute | solution.py:69

commit v2 on v1

--- a/solution.py
+++ b/solution.py
@@ -1,6 +1,9 @@
 import jax
 import jax.numpy as jnp
+import numpy as np
 from jax import lax
+from jax.experimental import pallas as pl
+from jax.experimental.pallas import tpu as pltpu
 from jax.sharding import PartitionSpec as P
 
 HEAD_SIZE = 128
@@ -108,7 +111,7 @@
     return jnp.where(flag == 1, upper, lower)
 
 
-def body(
+def general_body(
     tokens,
     attention_gain,
     forward_gain,
@@ -217,6 +220,381 @@
     return (hidden.astype(jnp.float32) + forward_part).astype(jnp.bfloat16)
 
 
+VMEM = pltpu.VMEM
+WHOLE = pl.BlockSpec(memory_space=pltpu.VMEM)
+SCALAR = pl.BlockSpec(memory_space=pltpu.SMEM)
+FAR = pl.BlockSpec(memory_space=pltpu.HBM)
+ROW_DOT = (((1,), (1,)), ((), ()))
+LANES = 128
+CHUNK = 1024
+
+
+def dot(a, b):
+    return jnp.dot(a, b, preferred_element_type=jnp.float32)
+
+
+def dot_rows(a, b):
+    return lax.dot_general(a, b, ROW_DOT, preferred_element_type=jnp.float32)
+
+
+def call(kernel, name, outs, args, weights=(), ahead=(), scratch=(), limit=6):
+    outs = tuple(VMEM(o.shape, o.dtype) for o in outs)
+    size = sum(w.size for w in weights)
+
+    def run(*refs):
+        kernel(*refs[: len(args) + len(weights)], *refs[len(args) + len(weights) + len(ahead) :])
+
+    return pl.pallas_call(
+        run,
+        out_shape=outs,
+        in_specs=[WHOLE] * (len(args) + len(weights)) + [FAR] * len(ahead),
+        out_specs=(WHOLE,) * len(outs),
+        scratch_shapes=list(scratch),
+        name=name,
+        cost_estimate=pl.CostEstimate(
+            flops=64 * size, bytes_accessed=2 * size, transcendentals=0
+        ),
+        compiler_params=pltpu.CompilerParams(vmem_limit_bytes=limit << 20),
+    )(
+        *args,
+        *[pltpu.with_memory_space_constraint(w, VMEM) for w in weights],
+        *[pltpu.with_memory_space_constraint(w, pltpu.HBM) for w in ahead],
+    )
+
+
+def stage(tokens, gains, lifts, parents, place, request, ahead, chips):
+    rows, cols = tokens.shape
+    outs = (
+        VMEM((chips, rows, cols), tokens.dtype),
+        VMEM(tokens.shape, tokens.dtype),
+        *[VMEM(g.shape, g.dtype) for g in gains],
+        *[VMEM(a.shape[1:], a.dtype) for a in lifts],
+        VMEM(parents.shape, parents.dtype),
+        VMEM((8, LANES), jnp.int32),
+    )
+    count = len(outs) - 1 + chips - 1
+
+    def kernel(place_ref, request_ref, *refs):
+        ins, outs, sem = refs[:6], refs[6 + len(ahead) : -1], refs[-1]
+        token_ref, parent_ref = ins[0], ins[5]
+        pairs = [(token_ref, outs[0].at[chip]) for chip in range(chips)]
+        pairs += [(token_ref, outs[1])]
+        pairs += [(ins[1], outs[2]), (ins[2], outs[3])]
+        pairs += [(ins[k].at[request_ref[0]], outs[k + 1]) for k in (3, 4)]
+        pairs += [(parent_ref, outs[6])]
+        copies = [
+            pltpu.make_async_copy(src, dst, sem.at[k]) for k, (src, dst) in enumerate(pairs)
+        ]
+        for copy in copies:
+            copy.start()
+        outs[7][...] = jnp.full(outs[7].shape, place_ref[request_ref[0]], jnp.int32)
+        for copy in copies:
+            copy.wait()
+
+    args = (tokens, *gains, *lifts, parents, *ahead)
+    return pl.pallas_call(
+        kernel,
+        out_shape=outs,
+        in_specs=[SCALAR] * 2 + [FAR] * len(args),
+        out_specs=(WHOLE,) * len(outs),
+        scratch_shapes=[pltpu.SemaphoreType.DMA((count + 1,))],
+        name="stage",
+        compiler_params=pltpu.CompilerParams(vmem_limit_bytes=2 << 20),
+    )(place, request, *[pltpu.with_memory_space_constraint(a, pltpu.HBM) for a in args])
+
+
+def dot_chunks(left, weight_ref):
+    depth = weight_ref.shape[0]
+    step = min(depth, CHUNK)
+    total = dot(left[:, :step], weight_ref[:step, :])
+    for at in range(step, depth, step):
+        total = total + dot(left[:, at : at + step], weight_ref[at : at + step, :])
+    return total
+
+
+def gain_block(gain_ref, index, cols):
+    count = cols // LANES
+    lines = [gain_ref[index * count + j : index * count + j + 1, :] for j in range(count)]
+    return jnp.concatenate([line.astype(jnp.float32) for line in lines], axis=1)
+
+
+def core_index():
+    return lax.axis_index("tp") & 1
+
+
+def in_order(mine, theirs, flag):
+    mine = mine.astype(jnp.float32)
+    theirs = theirs.astype(jnp.float32)
+    return jnp.where(flag, mine, theirs), jnp.where(flag, theirs, mine)
+
+
+def norm_blocks(mine_ref, theirs_ref, gain_ref, scratch, cols):
+    chips = mine_ref.shape[0]
+    first = core_index() == 0
+    squares = jnp.zeros((mine_ref.shape[1], cols), jnp.float32)
+    for chip in range(chips):
+        for ref in (mine_ref, theirs_ref):
+            wide = ref[chip, :, :cols].astype(jnp.float32)
+            squares = squares + wide * wide
+    mean_sq = jnp.sum(squares, axis=-1, keepdims=True) / (2 * chips * cols)
+    scale = lax.rsqrt(mean_sq + EPS)
+    for chip in range(chips):
+        pair = in_order(mine_ref[chip, :, :cols], theirs_ref[chip, :, :cols], first)
+        for side in range(2):
+            low = (2 * chip + side) * cols
+            gain = gain_block(gain_ref, 2 * chip + side, cols)
+            scratch[:, low : low + cols] = (pair[side] * scale * gain).astype(jnp.bfloat16)
+    return scale
+
+
+def project_kernel(
+    mine_ref, theirs_ref, gain_ref, query_ref, key_ref, value_ref, factor_ref,
+    query_out, pair_out, payload_out, scratch,
+):
+    chips, rows, cols = mine_ref.shape
+    norm_blocks(mine_ref, theirs_ref, gain_ref, scratch, cols)
+    normed = scratch[...]
+    rank = factor_ref.shape[0] // 2
+    low = dot_rows(normed, factor_ref[:rank, :])
+    query_out[...] = dot_chunks(normed, query_ref)
+    half = key_ref.shape[0]
+    pair_out[:, :half] = dot_rows(normed, key_ref[...]).astype(jnp.bfloat16)
+    pair_out[:, half:] = dot_rows(normed, value_ref[...]).astype(jnp.bfloat16)
+    padded = jnp.concatenate([low, jnp.zeros((rows, LANES - rank), jnp.float32)], axis=1)
+    padded = padded.astype(jnp.bfloat16)
+    for chip in range(chips):
+        for side in range(2):
+            at = (2 * chip + side) * cols
+            payload_out[chip, side * rank : (side + 1) * rank, :cols] = factor_ref[
+                rank:, at : at + cols
+            ]
+        payload_out[chip, :, cols:] = padded
+
+
+def pick_kernel(owner_ref, got_ref, out_ref):
+    owner = owner_ref[:1, :1] - core_index()
+    piece = jnp.zeros(out_ref.shape, jnp.float32)
+    for chip in range(got_ref.shape[0]):
+        piece = piece + jnp.where(owner == 2 * chip, got_ref[chip].astype(jnp.float32), 0.0)
+    out_ref[...] = piece.astype(jnp.bfloat16)
+
+
+def joined(mine_ref, theirs_ref):
+    return mine_ref[...].astype(jnp.float32) + theirs_ref[...].astype(jnp.float32)
+
+
+def split_product(left, weight_ref, mine_out, theirs_out):
+    chips, _, cols = mine_out.shape
+    core = core_index()
+    for chip in range(chips):
+        at = pl.multiple_of((2 * chip + 1 - core) * cols, cols)
+        theirs_out[chip] = dot(left, weight_ref[:, pl.ds(at, cols)]).astype(jnp.bfloat16)
+        at = pl.multiple_of((2 * chip + core) * cols, cols)
+        mine_out[chip] = dot(left, weight_ref[:, pl.ds(at, cols)])
+
+
+def attend_kernel(
+    query_ref, pair_mine, pair_theirs, piece_mine, piece_theirs,
+    lift_ref, parent_ref, freq_ref, output_ref, mine_out, theirs_out,
+):
+    rows, query_cols = query_ref.shape
+    head = HEAD_SIZE
+    heads = query_cols // head
+    half = head // 2
+    rank = lift_ref.shape[0]
+    first = core_index() == 0
+    own = lax.broadcasted_iota(jnp.int32, (rows, rows), 0)
+    other = lax.broadcasted_iota(jnp.int32, (rows, rows), 1)
+    eye = jnp.where(own == other, 1.0, 0.0)
+    links = jnp.where(parent_ref[...] == own, 1.0, 0.0)
+    reach = dot_rows(eye.astype(jnp.bfloat16), jnp.maximum(links, eye).astype(jnp.bfloat16))
+    for _ in range((rows - 1).bit_length()):
+        square = reach.astype(jnp.bfloat16)
+        reach = jnp.minimum(dot(square, square), 1.0)
+    angle = (jnp.sum(reach, axis=-1, keepdims=True) - 1.0) * freq_ref[...]
+    lane = lax.broadcasted_iota(jnp.int32, (rows, head), 1)
+    cosine = jnp.cos(angle)
+    sine = jnp.sin(angle)
+    sine = jnp.where(lane < half, -sine, sine)
+
+    def rotate(wide):
+        return (wide * cosine + pltpu.roll(wide, half, 1) * sine).astype(jnp.bfloat16)
+
+    even, odd = in_order(pair_mine[...], pair_theirs[...], first)
+    key = rotate(jnp.where(lane < half, even, pltpu.roll(odd, half, 1)))
+    value = jnp.where(lane < half, pltpu.roll(even, half, 1), odd).astype(jnp.bfloat16)
+    piece = joined(piece_mine, piece_theirs)
+    cols = piece.shape[1] - LANES
+    low = piece[:, cols : cols + rank].astype(jnp.bfloat16)
+    query = query_ref[...] + dot(low, lift_ref[...])
+    query = query.astype(jnp.bfloat16).astype(jnp.float32)
+    stacked = jnp.concatenate(
+        [rotate(query[:, h * head : (h + 1) * head]) for h in range(heads)], axis=0
+    )
+    scores = dot_rows(stacked, key) * head ** (-0.5)
+    weights = jnp.exp(scores) * jnp.concatenate([reach] * heads, axis=0)
+    probs = (weights / jnp.sum(weights, axis=-1, keepdims=True)).astype(jnp.bfloat16)
+    mixed = dot(probs, value).astype(jnp.bfloat16)
+    mixed = jnp.concatenate([mixed[h * rows : (h + 1) * rows] for h in range(heads)], axis=1)
+    split_product(mixed, output_ref, mine_out, theirs_out)
+
+
+def hidden_kernel(
+    got_ref, token_ref, gain_ref, piece_mine, piece_theirs,
+    hidden_out, payload_out,
+):
+    chips, rows, cols = got_ref.shape
+    total = token_ref[...].astype(jnp.float32)
+    added = got_ref[0].astype(jnp.float32)
+    for chip in range(1, chips):
+        added = added + got_ref[chip].astype(jnp.float32)
+    hidden = (total + added).astype(jnp.bfloat16)
+    hidden_out[...] = hidden
+    piece = joined(piece_mine, piece_theirs)
+    rank = piece.shape[0] // 2
+    factor = jnp.where(core_index() == 0, piece[:rank, :cols], piece[rank:, :cols])
+    device = lax.axis_index("tp")
+    gain = gain_block(gain_ref, 0, cols)
+    for index in range(1, 2 * chips):
+        gain = jnp.where(device == index, gain_block(gain_ref, index, cols), gain)
+    gained = hidden.astype(jnp.float32) * gain
+    low = dot_rows(gained.astype(jnp.bfloat16), factor.astype(jnp.bfloat16))
+    padded = jnp.concatenate([low, jnp.zeros((rows, LANES - rank), jnp.float32)], axis=1)
+    padded = padded.astype(jnp.bfloat16)
+    for chip in range(chips):
+        payload_out[chip, :, :cols] = hidden
+        payload_out[chip, :, cols:] = padded
+
+
+def forward_kernel(
+    mine_ref, theirs_ref, gain_ref, lift_ref, gate_ref, up_ref, active_out, scratch,
+):
+    cols = mine_ref.shape[2] - LANES
+    rank = lift_ref.shape[0]
+    scale = norm_blocks(mine_ref, theirs_ref, gain_ref, scratch, cols)
+    low = jnp.zeros((mine_ref.shape[1], LANES), jnp.float32)
+    for chip in range(mine_ref.shape[0]):
+        for ref in (mine_ref, theirs_ref):
+            low = low + ref[chip, :, cols:].astype(jnp.float32)
+    low = (low * scale)[:, :rank].astype(jnp.bfloat16)
+    normed = scratch[...]
+    gate = dot_chunks(normed, gate_ref)
+    upper = dot_chunks(normed, up_ref) + dot(low, lift_ref[...])
+    active_out[...] = (gate * jax.nn.sigmoid(gate) * upper).astype(jnp.bfloat16)
+
+
+def down_kernel(active_ref, down_ref, mine_out, theirs_out):
+    split_product(active_ref[...], down_ref, mine_out, theirs_out)
+
+
+def fast_body(
+    tokens,
+    attention_gain,
+    forward_gain,
+    query_weight,
+    key_matrix,
+    value_matrix,
+    output_weight,
+    gate_weight,
+    up_weight,
+    down_weight,
+    adapter_inputs,
+    adapter_query,
+    adapter_upper,
+    adapter_place,
+    request_adapter,
+    tree_parents,
+):
+    rows, cols = tokens.shape
+    chips = lax.axis_size("tp") // 2
+    width = query_weight.shape[0]
+    half = HEAD_SIZE // 2
+    freq = ROPE_BASE ** (-np.arange(half, dtype=np.float32) * np.float32(2.0 / HEAD_SIZE))
+    freq = jnp.asarray(np.concatenate([freq, freq])[None].astype(np.float32))
+    shape = jax.ShapeDtypeStruct
+    bf16, f32 = jnp.bfloat16, jnp.float32
+    attention_gain = attention_gain.reshape(-1, LANES)
+    forward_gain = forward_gain.reshape(-1, LANES)
+    wide = cols + LANES
+    split_out = (shape((chips, rows, cols), f32), shape((chips, rows, cols), bf16))
+
+    heavy = (gate_weight, up_weight, down_weight)
+    spread, kept_tokens, gain_one, gain_two, query_lift, up_lift, parents, owner = stage(
+        tokens,
+        (attention_gain, forward_gain),
+        (adapter_query, adapter_upper),
+        tree_parents,
+        adapter_place,
+        request_adapter,
+        heavy,
+        chips,
+    )
+    mine = exchange(spread, "tp")
+    theirs = partner_2(mine, "tp", 0)
+    query, pair, payload = call(
+        project_kernel,
+        "project",
+        (
+            shape((rows, query_weight.shape[1]), f32),
+            shape((rows, 2 * key_matrix.shape[1]), bf16),
+            shape((chips, rows, wide), bf16),
+        ),
+        (mine, theirs, gain_one),
+        (query_weight, key_matrix.T, value_matrix.T, adapter_inputs[0].T),
+        heavy,
+        [VMEM((rows, width), bf16)],
+    )
+    pair_theirs = partner_2(pair, "tp", 0)
+    got = exchange(payload, "tp")
+    (piece,) = call(pick_kernel, "pick", (shape((rows, wide), bf16),), (owner, got), (), heavy)
+    piece_theirs = partner_2(piece, "tp", 0)
+    kept, sent = call(
+        attend_kernel,
+        "attend",
+        split_out,
+        (query, pair, pair_theirs, piece, piece_theirs, query_lift, parents, freq),
+        (output_weight,),
+        heavy,
+    )
+    chip_sum = (kept + partner_2(sent, "tp", 0).astype(f32)).astype(bf16)
+    hidden, payload = call(
+        hidden_kernel,
+        "hidden",
+        (shape((rows, cols), bf16), shape((chips, rows, wide), bf16)),
+        (exchange(chip_sum, "tp"), kept_tokens, gain_two, piece, piece_theirs),
+        (),
+        heavy,
+    )
+    mine = exchange(payload, "tp")
+    theirs = partner_2(mine, "tp", 0)
+    (active,) = call(
+        forward_kernel,
+        "forward",
+        (shape((rows, gate_weight.shape[1]), bf16),),
+        (mine, theirs, gain_two, up_lift),
+        (gate_weight, up_weight),
+        (query_weight, output_weight, down_weight),
+        [VMEM((rows, width), bf16)],
+    )
+    kept, sent = call(down_kernel, "down", split_out, (active,), (down_weight,))
+    chip_sum = (kept + partner_2(sent, "tp", 0).astype(f32)).astype(bf16)
+    added = jnp.sum(exchange(chip_sum, "tp").astype(f32), axis=0)
+    return (hidden.astype(f32) + added).astype(bf16)
+
+
+def body(*args):
+    tokens, key_matrix, query_weight = args[0], args[4], args[3]
+    fits = (
+        tokens.shape[1] % LANES == 0
+        and query_weight.shape[1] % HEAD_SIZE == 0
+        and key_matrix.shape[1] * 2 == HEAD_SIZE
+        and args[10].shape[0] == 1
+        and args[14].shape[0] == 1
+        and args[10].shape[2] == tokens.shape[0]
+    )
+    return fast_body(*args) if fits else general_body(*args)
+
+
 def solution(mesh):
     return jax.shard_map(
         body,

time: 141 us -> 102 us (0.72)
  matrix products: 37.9 us -> 0 us
  blocking collectives: 39.4 us -> 69.7 us
  Pallas kernels: 0 us -> 16.2 us
  local copies, waits for them, and re-layouts: 21.5 us -> 6.48 us
  starting transfers between devices: 15.4 us -> 1.08 us
  waiting for transfers between devices: 18.8 us -> 6.58 us
  other arithmetic: 5.07 us -> 0.82 us
  between operations: 2.31 us -> 0.84 us
    dot_general x18 -> x0, matrix products: 37.9 us -> none  [the longest x1 13.7 us: body(): forward = jnp.dot(active, down_weight, preferred_element_type=jnp.float32)]
    all_to_all x3 -> x5, blocking collectives: 39.4 us -> 69.7 us  [exchange(): lax.all_to_all(blocks, axis, 0, 0, axis_index_groups=core_groups(axis), t...]
    pallas_call x0 -> x7, Pallas kernels: none -> 16.2 us  [the longest x6 14.3 us: call(): pl.pallas_call(run, out_shape=outs, in_specs=[WHOLE] * (len(args) + len(w...]
    all_to_all x3 -> x0, starting transfers between devices: 14.4 us -> none  [exchange(): lax.all_to_all(blocks, axis, 0, 0, axis_index_groups=core_groups(axis), t...]
    all_to_all x3 -> x0, waiting for transfers between devices: 13.3 us -> none  [exchange(): lax.all_to_all(blocks, axis, 0, 0, axis_index_groups=core_groups(axis), t...]
    dot_general x1 -> x0, local copies, waits for them, and re-layouts: 12 us -> none  [body(): jnp.dot(own_mixed, output_weight, preferred_element_type=jnp.float32)]
    unnamed x18 -> x34, local copies, waits for them, and re-layouts: 1.62 us -> 6.48 us
    slice x3 -> x0, local copies, waits for them, and re-layouts: 2.8 us -> none  [the longest x1 2.63 us: sum_features(): odd = split[:, :, 1]]
  transfers between devices with their start and end apart: 10 -> 6, of which waited for: 6 -> 5; matrix products, arithmetic and copies ran while one was open for 22% -> 0% of each run, Pallas kernels for 0% -> 0%
where the time goes in v2:
time: 102 us
  blocking collectives  69.7 us (68%)
  Pallas kernels  16.2 us (16%)
  waiting for transfers between devices  6.58 us (6%)
  local copies, waits for them, and re-layouts  6.48 us (6%)
  starting transfers between devices  1.08 us (1%)
    all_to_all x5, blocking collectives, exchange(): lax.all_to_all(blocks, axis, 0, 0, axis_index_groups=core_groups(axis), t...  69.7 us
    pallas_call x6, Pallas kernels, call(): pl.pallas_call(run, out_shape=outs, in_specs=[WHOLE] * (len(args) + len(w...  14.3 us
    ppermute x6, waiting for transfers between devices, partner_2(): return lax.ppermute(block, axis, route)  6.58 us
    unnamed x34, local copies, waits for them, and re-layouts  6.48 us
  transfers between devices with their start and end apart: 6, of which 5 were waited for; matrix products, arithmetic and copies ran while one was open for 0% of the time, Pallas kernels for 0%

profile of v2, /device:TPU:0, one launch (start us, length us, event | category | flops | bytes accessed | tf_op | source)
XLA Modules:
  0.0 101.7 jit_solution(9009232807871866664)
XLA Ops:
  0.7 0.6 copy-done.5
  1.3 1.8 %stage.1 = (bf16[8,32,512]{2,1,0:T(8,128)(2,1)S(1)}, bf16[32,512]{1,0:T(8,128)(2,1)S(1)}, bf16[64,128]{1,0:T(8,128)(2,1)S(1)}, bf16[64,128]{1,0:T(8,128)(2,1)S(1...) custom-call(s32[16]{0:T(128)S(1)} %copy-done.5, ...), custom_call_target="tpu_custom_call" | custom-call | tf_op jit(solution)/shard_map/stage/pallas_call | solution.py:295
  3.2 16.2 %all_to_all.25.refs_0_ = bf16[8,32,512]{2,1,0:T(8,128)(2,1)S(1)} all-to-all(bf16[8,32,512]{2,1,0:T(8,128)(2,1)S(1)} %get-tuple-element.22), channel_id=1, replica_groups={{0,2,4,6,8,10,12,14},{1,3,5,7,9,11,13,15},{16,18,20,22,24,26,28,30},{17..., dimensions={0} | all-to-all | bytes 524288 | tf_op jit(solution)/shard_map/all_to_all | solution.py:22
  19.4 1.5 %collective-permute-done.refs_1_ = bf16[8,32,512]{2,1,0:T(8,128)(2,1)S(1)} collective-permute-done((bf16[8,32,512]{2,1,0:T(8,128)(2,1)S(1)}, bf16[8,32,512]{2,1,0:T(8,128)(2,1)S(1)}, u32[]{:S(2)}, u32[]{:S(2)}) %collective-permute-start) | collective-permute-done | bytes 262176 | tf_op jit(solution)/shard_map/ppermute | solution.py:72
  21.0 2.1 %project.1 = (f32[32,512]{1,0:T(8,128)S(1)}, bf16[32,128]{1,0:T(8,128)(2,1)S(1)}, bf16[8,32,640]{2,1,0:T(8,128)(2,1)S(1)}) custom-call(bf16[8,32,512]{2,1,0:T(8,128)(2,1)S(1)} %all_to_all.25.refs_0_, bf16[8,32,512]{2,1,0:T(8,128)(2,1)S(1)} %collective-permute-done.refs_1_, bf16[64,128]{1,0:T(8,128)(2,1)S(1)} %get-tuple-element.23.refs_2_, ...), custom_call_target="tpu_custom_call" | custom-call | flops 352321536 | bytes 11010048 | tf_op jit(solution)/shard_map/project/pallas_call | solution.py:247
  23.1 14.6 %all_to_all.26.refs_1_ = bf16[8,32,640]{2,1,0:T(8,128)(2,1)S(1)} all-to-all(bf16[8,32,640]{2,1,0:T(8,128)(2,1)S(1)} %get-tuple-element.27), channel_id=1, replica_groups={{0,2,4,6,8,10,12,14},{1,3,5,7,9,11,13,15},{16,18,20,22,24,26,28,30},{17..., dimensions={0} | all-to-all | bytes 655360 | tf_op jit(solution)/shard_map/all_to_all | solution.py:22
  37.7 0.1 pick.1.refs_3_
  37.9 0.5 collective-permute-start.1
  38.4 0.8 collective-permute-done.1.refs_2_
  39.3 2.8 %attend.1 = (f32[8,32,512]{2,1,0:T(8,128)S(1)}, bf16[8,32,512]{2,1,0:T(8,128)(2,1)S(1)}) custom-call(f32[32,512]{1,0:T(8,128)S(1)} %get-tuple-element.24.refs_0_, bf16[32,128]{1,0:T(8,128)(2,1)S(1)} %get-tuple-element.25.refs_1_, bf16[32,128]{1,0:T(8,128)(2,1)S(1)} %collective-permute-done.1.refs_2_, bf16[32,640]{1,0:T(8,128)(2,1)S(1)} %pick.1.refs_3_, ...), custom_call_target="tpu_custom_call" | custom-call | flops 268435456 | bytes 8388608 | tf_op jit(solution)/shard_map/attend/pallas_call | solution.py:247
  42.1 0.4 collective-permute-start.3
  42.4 1.2 %collective-permute-done.3 = bf16[8,32,512]{2,1,0:T(8,128)(2,1)S(1)} collective-permute-done((bf16[8,32,512]{2,1,0:T(8,128)(2,1)S(1)}, bf16[8,32,512]{2,1,0:T(8,128)(2,1)S(1)}, u32[]{:S(2)}, u32[]{:S(2)}) %collective-permute-start.3) | collective-permute-done | bytes 262176 | tf_op jit(solution)/shard_map/ppermute | solution.py:72
  43.7 12.2 %all_to_all.27.refs_0_ = bf16[8,32,512]{2,1,0:T(8,128)(2,1)S(1)} all-to-all(bf16[8,32,512]{2,1,0:T(8,128)(2,1)S(1)} %add_convert_fusion.1), channel_id=1, replica_groups={{0,2,4,6,8,10,12,14},{1,3,5,7,9,11,13,15},{16,18,20,22,24,26,28,30},{17..., dimensions={0} | all-to-all | bytes 524288 | tf_op jit(solution)/shard_map/all_to_all | solution.py:22
  55.9 0.2 hidden.1
  56.2 14.6 %all_to_all.28.refs_0_ = bf16[8,32,640]{2,1,0:T(8,128)(2,1)S(1)} all-to-all(bf16[8,32,640]{2,1,0:T(8,128)(2,1)S(1)} %get-tuple-element.35), channel_id=1, replica_groups={{0,2,4,6,8,10,12,14},{1,3,5,7,9,11,13,15},{16,18,20,22,24,26,28,30},{17..., dimensions={0} | all-to-all | bytes 655360 | tf_op jit(solution)/shard_map/all_to_all | solution.py:22
  70.8 1.6 %collective-permute-done.4.refs_1_ = bf16[8,32,640]{2,1,0:T(8,128)(2,1)S(1)} collective-permute-done((bf16[8,32,640]{2,1,0:T(8,128)(2,1)S(1)}, bf16[8,32,640]{2,1,0:T(8,128)(2,1)S(1)}, u32[]{:S(2)}, u32[]{:S(2)}) %collective-permute-start.4) | collective-permute-done | bytes 327712 | tf_op jit(solution)/shard_map/ppermute | solution.py:72
  72.5 5.8 %copy-done = bf16[8192,1024]{1,0:T(8,128)(2,1)S(1)} copy-done((bf16[8192,1024]{1,0:T(8,128)(2,1)S(1)}, bf16[8192,1024]{1,0:T(8,128)(2,1)}, u32[]{:S(2)}) %copy-start) | copy-done | bytes 16777240
  78.2 6.1 %forward.1.refs_0_ = bf16[32,1024]{1,0:T(8,128)(2,1)S(1)} custom-call(bf16[8,32,640]{2,1,0:T(8,128)(2,1)S(1)} %all_to_all.28.refs_0_, bf16[8,32,640]{2,1,0:T(8,128)(2,1)S(1)} %collective-permute-done.4.refs_1_, bf16[64,128]{1,0:T(8,128)(2,1)S(1)} %get-tuple-element.33.refs_2_, bf16[16,1024]{1,0:T(8,128)(2,1)S(1)} %get-tuple-element.36.refs_3_, ...), custom_call_target="tpu_custom_call" | custom-call | flops 1073741824 | bytes 33554432 | tf_op jit(solution)/shard_map/forward/pallas_call | solution.py:247
  84.4 3.0 %down.1 = (f32[8,32,512]{2,1,0:T(8,128)S(1)}, bf16[8,32,512]{2,1,0:T(8,128)(2,1)S(1)}) custom-call(bf16[32,1024]{1,0:T(8,128)(2,1)S(1)} %forward.1.refs_0_, bf16[1024,8192]{1,0:T(8,128)(2,1)S(1)} %bitcast.8), custom_call_target="tpu_custom_call" | custom-call | flops 536870912 | bytes 16777216 | tf_op jit(solution)/shard_map/down/pallas_call | solution.py:247
  87.4 0.1 collective-permute-start.5
  87.5 1.4 %collective-permute-done.5 = bf16[8,32,512]{2,1,0:T(8,128)(2,1)S(1)} collective-permute-done((bf16[8,32,512]{2,1,0:T(8,128)(2,1)S(1)}, bf16[8,32,512]{2,1,0:T(8,128)(2,1)S(1)}, u32[]{:S(2)}, u32[]{:S(2)}) %collective-permute-start.5) | collective-permute-done | bytes 262176 | tf_op jit(solution)/shard_map/ppermute | solution.py:72
  88.9 0.1 add_convert_fusion
  89.0 12.0 %all_to_all.29 = bf16[8,32,512]{2,1,0:T(8,128)(2,1)S(1)} all-to-all(bf16[8,32,512]{2,1,0:T(8,128)(2,1)S(1)} %add_convert_fusion), channel_id=1, replica_groups={{0,2,4,6,8,10,12,14},{1,3,5,7,9,11,13,15},{16,18,20,22,24,26,28,30},{17..., dimensions={0} | all-to-all | bytes 524288 | tf_op jit(solution)/shard_map/all_to_all | solution.py:22
  101.0 0.6 add_convert_fusion.2
  (41 shorter events, 0.3 us)
Async XLA Ops:
  0.7 0.7 copy-start.5
  1.3 19.6 %copy-start.1 = (bf16[8192,512]{1,0:T(8,128)(2,1)S(1)}, bf16[8192,512]{1,0:T(8,128)(2,1)}, u32[]{:S(2)}) copy-start(bf16[8192,512]{1,0:T(8,128)(2,1)} %refs_6_.5) | copy-start | bytes 25165828
  1.3 19.6 %copy-start.2 = (bf16[8192,64]{0,1:T(8,128)(2,1)S(1)}, bf16[8192,64]{0,1:T(8,128)(2,1)}, u32[]{:S(2)}) copy-start(bf16[8192,64]{0,1:T(8,128)(2,1)} %param.21) | copy-start | bytes 3145732
  1.3 19.6 %copy-start.3 = (bf16[8192,64]{0,1:T(8,128)(2,1)S(1)}, bf16[8192,64]{0,1:T(8,128)(2,1)}, u32[]{:S(2)}) copy-start(bf16[8192,64]{0,1:T(8,128)(2,1)} %param.22) | copy-start | bytes 3145732
  1.3 19.6 %copy-start.4 = (bf16[1,8192,32]{1,2,0:T(8,128)(2,1)S(1)}, bf16[1,8192,32]{1,2,0:T(8,128)(2,1)}, u32[]{:S(2)}) copy-start(bf16[1,8192,32]{1,2,0:T(8,128)(2,1)} %param.27) | copy-start | bytes 1572868
  1.3 37.9 %slice-start.8 = ((s8[8388608]{0:T(1024)(128)(4,1)}), s8[4194304]{0:T(1024)(128)(4,1)S(1)}, s32[]{:S(2)}) async-start(s8[8388608]{0:T(1024)(128)(4,1)} %bitcast.11), calls=%async_computation.13 | async-start | bytes 8388608
  19.4 1.5 %collective-permute-start = (bf16[8,32,512]{2,1,0:T(8,128)(2,1)S(1)}, bf16[8,32,512]{2,1,0:T(8,128)(2,1)S(1)}, u32[]{:S(2)}, u32[]{:S(2)}) collective-permute-start(bf16[8,32,512]{2,1,0:T(8,128)(2,1)S(1)} %all_to_all.25.refs_0_), channel_id=1, source_target_pairs={{0,1},{1,0},{2,3},{3,2},{4,5},{5,4},{6,7},{7,6},{8,9},{9,8},{10,11... | collective-permute-start | bytes 786440 | tf_op jit(solution)/shard_map/ppermute | solution.py:72
  21.0 18.3 %slice-start.9 = ((s8[8388608]{0:T(1024)(128)(4,1)}), s8[4194304]{0:T(1024)(128)(4,1)S(1)}, s32[]{:S(2)}) async-start(s8[8388608]{0:T(1024)(128)(4,1)} %bitcast.11), calls=%async_computation.14 | async-start | bytes 8388608
  37.7 1.5 %copy-start.6 = (f32[1,128]{1,0:T(1,128)S(1)}, f32[1,128]{1,0:T(1,128)}, u32[]{:S(2)}) copy-start(f32[1,128]{1,0:T(1,128)} %constant.4.clone.refs_7_) | copy-start | bytes 1540
  37.8 1.4 %collective-permute-start.2 = (bf16[32,640]{1,0:T(8,128)(2,1)S(1)}, bf16[32,640]{1,0:T(8,128)(2,1)S(1)}, u32[]{:S(2)}, u32[]{:S(2)}) collective-permute-start(bf16[32,640]{1,0:T(8,128)(2,1)S(1)} %pick.1.refs_3_), channel_id=1, source_target_pairs={{0,1},{1,0},{2,3},{3,2},{4,5},{5,4},{6,7},{7,6},{8,9},{9,8},{10,11... | collective-permute-start | bytes 122888 | tf_op jit(solution)/shard_map/ppermute | solution.py:72
  37.9 1.3 %collective-permute-start.1 = (bf16[32,128]{1,0:T(8,128)(2,1)S(1)}, bf16[32,128]{1,0:T(8,128)(2,1)S(1)}, u32[]{:S(2)}, u32[]{:S(2)}) collective-permute-start(bf16[32,128]{1,0:T(8,128)(2,1)S(1)} %get-tuple-element.25.refs_1_), channel_id=1, source_target_pairs={{0,1},{1,0},{2,3},{3,2},{4,5},{5,4},{6,7},{7,6},{8,9},{9,8},{10,11... | collective-permute-start | bytes 24584 | tf_op jit(solution)/shard_map/ppermute | solution.py:72
  39.3 33.2 %slice-start.4 = ((s8[16777216]{0:T(1024)(128)(4,1)}), s8[4194304]{0:T(1024)(128)(4,1)S(1)}, s32[]{:S(2)}) async-start(s8[16777216]{0:T(1024)(128)(4,1)} %bitcast.9), calls=%async_computation.9 | async-start | bytes 8388608
  39.3 33.2 %slice-start.5 = ((s8[16777216]{0:T(1024)(128)(4,1)}), s8[4194304]{0:T(1024)(128)(4,1)S(1)}, s32[]{:S(2)}) async-start(s8[16777216]{0:T(1024)(128)(4,1)} %bitcast.9), calls=%async_computation.10 | async-start | bytes 8388608
  39.3 33.2 %slice-start.6 = ((s8[16777216]{0:T(1024)(128)(4,1)}), s8[4194304]{0:T(1024)(128)(4,1)S(1)}, s32[]{:S(2)}) async-start(s8[16777216]{0:T(1024)(128)(4,1)} %bitcast.9), calls=%async_computation.11 | async-start | bytes 8388608
  42.1 1.5 %collective-permute-start.3 = (bf16[8,32,512]{2,1,0:T(8,128)(2,1)S(1)}, bf16[8,32,512]{2,1,0:T(8,128)(2,1)S(1)}, u32[]{:S(2)}, u32[]{:S(2)}) collective-permute-start(bf16[8,32,512]{2,1,0:T(8,128)(2,1)S(1)} %get-tuple-element.31), channel_id=1, source_target_pairs={{0,1},{1,0},{2,3},{3,2},{4,5},{5,4},{6,7},{7,6},{8,9},{9,8},{10,11... | collective-permute-start | bytes 786440 | tf_op jit(solution)/shard_map/ppermute | solution.py:72
  55.9 16.5 %slice-start.7 = ((s8[16777216]{0:T(1024)(128)(4,1)}), s8[4194304]{0:T(1024)(128)(4,1)S(1)}, s32[]{:S(2)}) async-start(s8[16777216]{0:T(1024)(128)(4,1)} %bitcast.9), calls=%async_computation.12 | async-start | bytes 8388608
  55.9 28.4 %slice-start = ((s8[16777216]{0:T(1024)(128)(4,1)}), s8[4194304]{0:T(1024)(128)(4,1)S(1)}, s32[]{:S(2)}) async-start(s8[16777216]{0:T(1024)(128)(4,1)} %bitcast.7), calls=%async_computation.5 | async-start | bytes 8388608
  55.9 28.4 %slice-start.1 = ((s8[16777216]{0:T(1024)(128)(4,1)}), s8[4194304]{0:T(1024)(128)(4,1)S(1)}, s32[]{:S(2)}) async-start(s8[16777216]{0:T(1024)(128)(4,1)} %bitcast.7), calls=%async_computation.6 | async-start | bytes 8388608
  70.8 1.6 %collective-permute-start.4 = (bf16[8,32,640]{2,1,0:T(8,128)(2,1)S(1)}, bf16[8,32,640]{2,1,0:T(8,128)(2,1)S(1)}, u32[]{:S(2)}, u32[]{:S(2)}) collective-permute-start(bf16[8,32,640]{2,1,0:T(8,128)(2,1)S(1)} %all_to_all.28.refs_0_), channel_id=1, source_target_pairs={{0,1},{1,0},{2,3},{3,2},{4,5},{5,4},{6,7},{7,6},{8,9},{9,8},{10,11... | collective-permute-start | bytes 983048 | tf_op jit(solution)/shard_map/ppermute | solution.py:72
  72.4 5.8 %copy-start = (bf16[8192,1024]{1,0:T(8,128)(2,1)S(1)}, bf16[8192,1024]{1,0:T(8,128)(2,1)}, u32[]{:S(2)}) copy-start(bf16[8192,1024]{1,0:T(8,128)(2,1)} %refs_4_.5) | copy-start | bytes 50331652
  78.2 6.1 %slice-start.2 = ((s8[16777216]{0:T(1024)(128)(4,1)}), s8[4194304]{0:T(1024)(128)(4,1)S(1)}, s32[]{:S(2)}) async-start(s8[16777216]{0:T(1024)(128)(4,1)} %bitcast.7), calls=%async_computation.7 | async-start | bytes 8388608
  78.2 6.1 %slice-start.3 = ((s8[16777216]{0:T(1024)(128)(4,1)}), s8[4194304]{0:T(1024)(128)(4,1)S(1)}, s32[]{:S(2)}) async-start(s8[16777216]{0:T(1024)(128)(4,1)} %bitcast.7), calls=%async_computation.8 | async-start | bytes 8388608
  87.4 1.6 %collective-permute-start.5 = (bf16[8,32,512]{2,1,0:T(8,128)(2,1)S(1)}, bf16[8,32,512]{2,1,0:T(8,128)(2,1)S(1)}, u32[]{:S(2)}, u32[]{:S(2)}) collective-permute-start(bf16[8,32,512]{2,1,0:T(8,128)(2,1)S(1)} %get-tuple-element.38), channel_id=1, source_target_pairs={{0,1},{1,0},{2,3},{3,2},{4,5},{5,4},{6,7},{7,6},{8,9},{9,8},{10,11... | collective-permute-start | bytes 786440 | tf_op jit(solution)/shard_map/ppermute | solution.py:72

commit v3 on v2

--- a/solution.py
+++ b/solution.py
@@ -237,17 +237,18 @@
     return lax.dot_general(a, b, ROW_DOT, preferred_element_type=jnp.float32)
 
 
-def call(kernel, name, outs, args, weights=(), ahead=(), scratch=(), limit=6):
+def call(kernel, name, outs, args, weights=(), ahead=(), scratch=(), limit=6, far=()):
     outs = tuple(VMEM(o.shape, o.dtype) for o in outs)
-    size = sum(w.size for w in weights)
+    size = sum(w.size for w in weights + far)
+    used = len(args) + len(weights) + len(far)
 
     def run(*refs):
-        kernel(*refs[: len(args) + len(weights)], *refs[len(args) + len(weights) + len(ahead) :])
+        kernel(*refs[:used], *refs[used + len(ahead) :])
 
     return pl.pallas_call(
         run,
         out_shape=outs,
-        in_specs=[WHOLE] * (len(args) + len(weights)) + [FAR] * len(ahead),
+        in_specs=[WHOLE] * (len(args) + len(weights)) + [FAR] * len(far + ahead),
         out_specs=(WHOLE,) * len(outs),
         scratch_shapes=list(scratch),
         name=name,
@@ -256,9 +257,8 @@
         ),
         compiler_params=pltpu.CompilerParams(vmem_limit_bytes=limit << 20),
     )(
-        *args,
-        *[pltpu.with_memory_space_constraint(w, VMEM) for w in weights],
-        *[pltpu.with_memory_space_constraint(w, pltpu.HBM) for w in ahead],
+        *[pltpu.with_memory_space_constraint(w, VMEM) for w in args + weights],
+        *[pltpu.with_memory_space_constraint(w, pltpu.HBM) for w in far + ahead],
     )
 
 
@@ -467,9 +467,20 @@
 
 
 def forward_kernel(
-    mine_ref, theirs_ref, gain_ref, lift_ref, gate_ref, up_ref, active_out, scratch,
+    mine_ref, theirs_ref, gain_ref, lift_ref, gate_ref, up_ref, down_ref,
+    mine_out, theirs_out, scratch, active, held, sem,
 ):
+    chips = mine_ref.shape[0]
     cols = mine_ref.shape[2] - LANES
+
+    def down_copy(chip):
+        part = pl.ds(pl.multiple_of(2 * cols * chip, 2 * cols), 2 * cols)
+        return pltpu.make_async_copy(down_ref.at[:, part], held.at[:, part], sem.at[chip])
+
+    @pl.loop(0, chips)
+    def _(chip):
+        down_copy(chip).start()
+
     rank = lift_ref.shape[0]
     scale = norm_blocks(mine_ref, theirs_ref, gain_ref, scratch, cols)
     low = jnp.zeros((mine_ref.shape[1], LANES), jnp.float32)
@@ -480,11 +491,15 @@
     normed = scratch[...]
     gate = dot_chunks(normed, gate_ref)
     upper = dot_chunks(normed, up_ref) + dot(low, lift_ref[...])
-    active_out[...] = (gate * jax.nn.sigmoid(gate) * upper).astype(jnp.bfloat16)
-
-
-def down_kernel(active_ref, down_ref, mine_out, theirs_out):
-    split_product(active_ref[...], down_ref, mine_out, theirs_out)
+    active[...] = (gate * jax.nn.sigmoid(gate) * upper).astype(jnp.bfloat16)
+    core = core_index()
+
+    @pl.loop(0, chips)
+    def _(chip):
+        down_copy(chip).wait()
+        for side, out in ((1 - core, theirs_out), (core, mine_out)):
+            at = pl.multiple_of((2 * chip + side) * cols, cols)
+            out[chip] = dot(active[...], held[:, pl.ds(at, cols)]).astype(out.dtype)
 
 
 def fast_body(
@@ -519,6 +534,7 @@
     split_out = (shape((chips, rows, cols), f32), shape((chips, rows, cols), bf16))
 
     heavy = (gate_weight, up_weight, down_weight)
+    most = heavy + (query_weight, output_weight)
     spread, kept_tokens, gain_one, gain_two, query_lift, up_lift, parents, owner = stage(
         tokens,
         (attention_gain, forward_gain),
@@ -546,7 +562,7 @@
     )
     pair_theirs = partner_2(pair, "tp", 0)
     got = exchange(payload, "tp")
-    (piece,) = call(pick_kernel, "pick", (shape((rows, wide), bf16),), (owner, got), (), heavy)
+    (piece,) = call(pick_kernel, "pick", (shape((rows, wide), bf16),), (owner, got), (), most)
     piece_theirs = partner_2(piece, "tp", 0)
     kept, sent = call(
         attend_kernel,
@@ -554,7 +570,7 @@
         split_out,
         (query, pair, pair_theirs, piece, piece_theirs, query_lift, parents, freq),
         (output_weight,),
-        heavy,
+        heavy + (query_weight,),
     )
     chip_sum = (kept + partner_2(sent, "tp", 0).astype(f32)).astype(bf16)
     hidden, payload = call(
@@ -563,20 +579,26 @@
         (shape((rows, cols), bf16), shape((chips, rows, wide), bf16)),
         (exchange(chip_sum, "tp"), kept_tokens, gain_two, piece, piece_theirs),
         (),
-        heavy,
+        most,
     )
     mine = exchange(payload, "tp")
     theirs = partner_2(mine, "tp", 0)
-    (active,) = call(
+    kept, sent = call(
         forward_kernel,
         "forward",
-        (shape((rows, gate_weight.shape[1]), bf16),),
+        split_out,
         (mine, theirs, gain_two, up_lift),
         (gate_weight, up_weight),
-        (query_weight, output_weight, down_weight),
-        [VMEM((rows, width), bf16)],
-    )
-    kept, sent = call(down_kernel, "down", split_out, (active,), (down_weight,))
+        (query_weight, output_weight),
+        [
+            VMEM((rows, width), bf16),
+            VMEM((rows, gate_weight.shape[1]), bf16),
+            VMEM(down_weight.shape, bf16),
+            pltpu.SemaphoreType.DMA((chips,)),
+        ],
+        far=(down_weight,),
+        limit=18,
+    )
     chip_sum = (kept + partner_2(sent, "tp", 0).astype(f32)).astype(bf16)
     added = jnp.sum(exchange(chip_sum, "tp").astype(f32), axis=0)
     return (hidden.astype(f32) + added).astype(bf16)

time: 102 us -> 98 us (0.961)
  local copies, waits for them, and re-layouts: 6.48 us -> 1.37 us
    unnamed x34 -> x32, local copies, waits for them, and re-layouts: 6.48 us -> 1.37 us
    pallas_call x6 -> x5, Pallas kernels: 14.3 us -> 15.3 us  [call(): pl.pallas_call(run, out_shape=outs, in_specs=[WHOLE] * (len(args) + len(w...]
where the time goes in v3:
time: 98 us; the launch traced here: 97.7 us
  blocking collectives  69.8 us (71%)
  Pallas kernels  17.2 us (18%)
  waiting for transfers between devices  6.93 us (7%)
  local copies, waits for them, and re-layouts  1.37 us (1%)
    all_to_all x5, blocking collectives, exchange(): lax.all_to_all(blocks, axis, 0, 0, axis_index_groups=core_groups(axis), t...  69.8 us
    pallas_call x5, Pallas kernels, call(): pl.pallas_call(run, out_shape=outs, in_specs=[WHOLE] * (len(args) + len(w...  15.3 us
    ppermute x6, waiting for transfers between devices, partner_2(): return lax.ppermute(block, axis, route)  6.93 us
  transfers between devices with their start and end apart: 6, of which 5 were waited for; matrix products, arithmetic and copies ran while one was open for 0% of the time, Pallas kernels for 0%

profile of v3, /device:TPU:0, one launch (start us, length us, event | category | flops | bytes accessed | tf_op | source)
XLA Modules:
  0.0 97.7 jit_solution(18252124523999940894)
XLA Ops:
  0.7 0.6 copy-done.5
  1.3 1.8 %stage.1 = (bf16[8,32,512]{2,1,0:T(8,128)(2,1)S(1)}, bf16[32,512]{1,0:T(8,128)(2,1)S(1)}, bf16[64,128]{1,0:T(8,128)(2,1)S(1)}, bf16[64,128]{1,0:T(8,128)(2,1)S(1...) custom-call(s32[16]{0:T(128)S(1)} %copy-done.5, ...), custom_call_target="tpu_custom_call" | custom-call | tf_op jit(solution)/shard_map/stage/pallas_call | solution.py:295
  3.2 16.2 %all_to_all.25.refs_0_ = bf16[8,32,512]{2,1,0:T(8,128)(2,1)S(1)} all-to-all(bf16[8,32,512]{2,1,0:T(8,128)(2,1)S(1)} %get-tuple-element.22), channel_id=1, replica_groups={{0,2,4,6,8,10,12,14},{1,3,5,7,9,11,13,15},{16,18,20,22,24,26,28,30},{17..., dimensions={0} | all-to-all | bytes 524288 | tf_op jit(solution)/shard_map/all_to_all | solution.py:22
  19.4 1.5 %collective-permute-done.refs_1_ = bf16[8,32,512]{2,1,0:T(8,128)(2,1)S(1)} collective-permute-done((bf16[8,32,512]{2,1,0:T(8,128)(2,1)S(1)}, bf16[8,32,512]{2,1,0:T(8,128)(2,1)S(1)}, u32[]{:S(2)}, u32[]{:S(2)}) %collective-permute-start) | collective-permute-done | bytes 262176 | tf_op jit(solution)/shard_map/ppermute | solution.py:72
  21.0 2.1 %project.1 = (f32[32,512]{1,0:T(8,128)S(1)}, bf16[32,128]{1,0:T(8,128)(2,1)S(1)}, bf16[8,32,640]{2,1,0:T(8,128)(2,1)S(1)}) custom-call(bf16[8,32,512]{2,1,0:T(8,128)(2,1)S(1)} %all_to_all.25.refs_0_, bf16[8,32,512]{2,1,0:T(8,128)(2,1)S(1)} %collective-permute-done.refs_1_, bf16[64,128]{1,0:T(8,128)(2,1)S(1)} %get-tuple-element.23.refs_2_, ...), custom_call_target="tpu_custom_call" | custom-call | flops 352321536 | bytes 11010048 | tf_op jit(solution)/shard_map/project/pallas_call | solution.py:248
  23.1 14.6 %all_to_all.26.refs_1_ = bf16[8,32,640]{2,1,0:T(8,128)(2,1)S(1)} all-to-all(bf16[8,32,640]{2,1,0:T(8,128)(2,1)S(1)} %get-tuple-element.27), channel_id=1, replica_groups={{0,2,4,6,8,10,12,14},{1,3,5,7,9,11,13,15},{16,18,20,22,24,26,28,30},{17..., dimensions={0} | all-to-all | bytes 655360 | tf_op jit(solution)/shard_map/all_to_all | solution.py:22
  37.7 0.1 pick.1.refs_3_
  37.8 0.1 collective-permute-start.2
  37.9 0.5 collective-permute-start.1
  38.4 0.8 collective-permute-done.1.refs_2_
  39.2 0.7 slice-done.9
  39.9 2.8 %attend.1 = (f32[8,32,512]{2,1,0:T(8,128)S(1)}, bf16[8,32,512]{2,1,0:T(8,128)(2,1)S(1)}) custom-call(f32[32,512]{1,0:T(8,128)S(1)} %get-tuple-element.24.refs_0_, bf16[32,128]{1,0:T(8,128)(2,1)S(1)} %get-tuple-element.25.refs_1_, bf16[32,128]{1,0:T(8,128)(2,1)S(1)} %collective-permute-done.1.refs_2_, bf16[32,640]{1,0:T(8,128)(2,1)S(1)} %pick.1.refs_3_, ...), custom_call_target="tpu_custom_call" | custom-call | flops 268435456 | bytes 8388608 | tf_op jit(solution)/shard_map/attend/pallas_call | solution.py:248
  42.7 1.5 %collective-permute-done.3 = bf16[8,32,512]{2,1,0:T(8,128)(2,1)S(1)} collective-permute-done((bf16[8,32,512]{2,1,0:T(8,128)(2,1)S(1)}, bf16[8,32,512]{2,1,0:T(8,128)(2,1)S(1)}, u32[]{:S(2)}, u32[]{:S(2)}) %collective-permute-start.3) | collective-permute-done | bytes 262176 | tf_op jit(solution)/shard_map/ppermute | solution.py:72
  44.2 0.1 add_convert_fusion.1
  44.4 12.4 %all_to_all.27.refs_0_ = bf16[8,32,512]{2,1,0:T(8,128)(2,1)S(1)} all-to-all(bf16[8,32,512]{2,1,0:T(8,128)(2,1)S(1)} %add_convert_fusion.1), channel_id=1, replica_groups={{0,2,4,6,8,10,12,14},{1,3,5,7,9,11,13,15},{16,18,20,22,24,26,28,30},{17..., dimensions={0} | all-to-all | bytes 524288 | tf_op jit(solution)/shard_map/all_to_all | solution.py:22
  56.8 0.2 hidden.1
  57.0 14.6 %all_to_all.28.refs_0_ = bf16[8,32,640]{2,1,0:T(8,128)(2,1)S(1)} all-to-all(bf16[8,32,640]{2,1,0:T(8,128)(2,1)S(1)} %get-tuple-element.35), channel_id=1, replica_groups={{0,2,4,6,8,10,12,14},{1,3,5,7,9,11,13,15},{16,18,20,22,24,26,28,30},{17..., dimensions={0} | all-to-all | bytes 655360 | tf_op jit(solution)/shard_map/all_to_all | solution.py:22
  71.6 1.6 %collective-permute-done.4.refs_1_ = bf16[8,32,640]{2,1,0:T(8,128)(2,1)S(1)} collective-permute-done((bf16[8,32,640]{2,1,0:T(8,128)(2,1)S(1)}, bf16[8,32,640]{2,1,0:T(8,128)(2,1)S(1)}, u32[]{:S(2)}, u32[]{:S(2)}) %collective-permute-start.4) | collective-permute-done | bytes 327712 | tf_op jit(solution)/shard_map/ppermute | solution.py:72
  73.3 10.1 %forward.1 = (f32[8,32,512]{2,1,0:T(8,128)S(1)}, bf16[8,32,512]{2,1,0:T(8,128)(2,1)S(1)}) custom-call(bf16[8,32,640]{2,1,0:T(8,128)(2,1)S(1)} %all_to_all.28.refs_0_, bf16[8,32,640]{2,1,0:T(8,128)(2,1)S(1)} %collective-permute-done.4.refs_1_, bf16[64,128]{1,0:T(8,128)(2,1)S(1)} %get-tuple-element.33.refs_2_, bf16[16,1024]{1,0:T(8,128)(2,1)S(1)} %get-tuple-element.36.refs_3_, ...), custom_call_target="tpu_custom_call" | custom-call | flops 1610612736 | bytes 50331648 | tf_op jit(solution)/shard_map/forward/pallas_call | solution.py:248
  83.4 0.2 collective-permute-start.5
  83.6 1.4 %collective-permute-done.5 = bf16[8,32,512]{2,1,0:T(8,128)(2,1)S(1)} collective-permute-done((bf16[8,32,512]{2,1,0:T(8,128)(2,1)S(1)}, bf16[8,32,512]{2,1,0:T(8,128)(2,1)S(1)}, u32[]{:S(2)}, u32[]{:S(2)}) %collective-permute-start.5) | collective-permute-done | bytes 262176 | tf_op jit(solution)/shard_map/ppermute | solution.py:72
  85.0 0.1 add_convert_fusion
  85.0 12.0 %all_to_all.29 = bf16[8,32,512]{2,1,0:T(8,128)(2,1)S(1)} all-to-all(bf16[8,32,512]{2,1,0:T(8,128)(2,1)S(1)} %add_convert_fusion), channel_id=1, replica_groups={{0,2,4,6,8,10,12,14},{1,3,5,7,9,11,13,15},{16,18,20,22,24,26,28,30},{17..., dimensions={0} | all-to-all | bytes 524288 | tf_op jit(solution)/shard_map/all_to_all | solution.py:22
  97.1 0.6 add_convert_fusion.2
  (38 shorter events, 0.1 us)
Async XLA Ops:
  0.7 0.7 copy-start.5
  1.3 19.6 %copy-start = (bf16[8192,512]{1,0:T(8,128)(2,1)S(1)}, bf16[8192,512]{1,0:T(8,128)(2,1)}, u32[]{:S(2)}) copy-start(bf16[8192,512]{1,0:T(8,128)(2,1)} %refs_7_.8) | copy-start | bytes 25165828
  1.3 19.6 %copy-start.1 = (bf16[8192,64]{0,1:T(8,128)(2,1)S(1)}, bf16[8192,64]{0,1:T(8,128)(2,1)}, u32[]{:S(2)}) copy-start(bf16[8192,64]{0,1:T(8,128)(2,1)} %param.21) | copy-start | bytes 3145732
  1.3 19.6 %copy-start.2 = (bf16[8192,64]{0,1:T(8,128)(2,1)S(1)}, bf16[8192,64]{0,1:T(8,128)(2,1)}, u32[]{:S(2)}) copy-start(bf16[8192,64]{0,1:T(8,128)(2,1)} %param.22) | copy-start | bytes 3145732
  1.3 19.6 %copy-start.3 = (bf16[1,8192,32]{1,2,0:T(8,128)(2,1)S(1)}, bf16[1,8192,32]{1,2,0:T(8,128)(2,1)}, u32[]{:S(2)}) copy-start(bf16[1,8192,32]{1,2,0:T(8,128)(2,1)} %param.27) | copy-start | bytes 1572868
  19.4 1.5 %collective-permute-start = (bf16[8,32,512]{2,1,0:T(8,128)(2,1)S(1)}, bf16[8,32,512]{2,1,0:T(8,128)(2,1)S(1)}, u32[]{:S(2)}, u32[]{:S(2)}) collective-permute-start(bf16[8,32,512]{2,1,0:T(8,128)(2,1)S(1)} %all_to_all.25.refs_0_), channel_id=1, source_target_pairs={{0,1},{1,0},{2,3},{3,2},{4,5},{5,4},{6,7},{7,6},{8,9},{9,8},{10,11... | collective-permute-start | bytes 786440 | tf_op jit(solution)/shard_map/ppermute | solution.py:72
  20.9 18.3 %slice-start.8 = ((s8[8388608]{0:T(1024)(128)(4,1)}), s8[4194304]{0:T(1024)(128)(4,1)S(1)}, s32[]{:S(2)}) async-start(s8[8388608]{0:T(1024)(128)(4,1)} %bitcast.11), calls=%async_computation.13 | async-start | bytes 8388608
  37.7 2.2 %slice-start.9 = ((s8[8388608]{0:T(1024)(128)(4,1)}), s8[4194304]{0:T(1024)(128)(4,1)S(1)}, s32[]{:S(2)}) async-start(s8[8388608]{0:T(1024)(128)(4,1)} %bitcast.11), calls=%async_computation.14 | async-start | bytes 8388608
  37.7 2.2 %copy-start.4 = (f32[1,128]{1,0:T(1,128)S(1)}, f32[1,128]{1,0:T(1,128)}, u32[]{:S(2)}) copy-start(f32[1,128]{1,0:T(1,128)} %constant.4.clone.refs_7_) | copy-start | bytes 1540
  37.8 1.4 %collective-permute-start.2 = (bf16[32,640]{1,0:T(8,128)(2,1)S(1)}, bf16[32,640]{1,0:T(8,128)(2,1)S(1)}, u32[]{:S(2)}, u32[]{:S(2)}) collective-permute-start(bf16[32,640]{1,0:T(8,128)(2,1)S(1)} %pick.1.refs_3_), channel_id=1, source_target_pairs={{0,1},{1,0},{2,3},{3,2},{4,5},{5,4},{6,7},{7,6},{8,9},{9,8},{10,11... | collective-permute-start | bytes 122888 | tf_op jit(solution)/shard_map/ppermute | solution.py:72
  37.9 1.3 %collective-permute-start.1 = (bf16[32,128]{1,0:T(8,128)(2,1)S(1)}, bf16[32,128]{1,0:T(8,128)(2,1)S(1)}, u32[]{:S(2)}, u32[]{:S(2)}) collective-permute-start(bf16[32,128]{1,0:T(8,128)(2,1)S(1)} %get-tuple-element.25.refs_1_), channel_id=1, source_target_pairs={{0,1},{1,0},{2,3},{3,2},{4,5},{5,4},{6,7},{7,6},{8,9},{9,8},{10,11... | collective-permute-start | bytes 24584 | tf_op jit(solution)/shard_map/ppermute | solution.py:72
  39.9 33.3 %slice-start = ((s8[16777216]{0:T(1024)(128)(4,1)}), s8[4194304]{0:T(1024)(128)(4,1)S(1)}, s32[]{:S(2)}) async-start(s8[16777216]{0:T(1024)(128)(4,1)} %bitcast.7), calls=%async_computation.5 | async-start | bytes 8388608
  39.9 33.3 %slice-start.1 = ((s8[16777216]{0:T(1024)(128)(4,1)}), s8[4194304]{0:T(1024)(128)(4,1)S(1)}, s32[]{:S(2)}) async-start(s8[16777216]{0:T(1024)(128)(4,1)} %bitcast.7), calls=%async_computation.6 | async-start | bytes 8388608
  39.9 33.3 %slice-start.4 = ((s8[16777216]{0:T(1024)(128)(4,1)}), s8[4194304]{0:T(1024)(128)(4,1)S(1)}, s32[]{:S(2)}) async-start(s8[16777216]{0:T(1024)(128)(4,1)} %bitcast.9), calls=%async_computation.9 | async-start | bytes 8388608
  39.9 33.3 %slice-start.5 = ((s8[16777216]{0:T(1024)(128)(4,1)}), s8[4194304]{0:T(1024)(128)(4,1)S(1)}, s32[]{:S(2)}) async-start(s8[16777216]{0:T(1024)(128)(4,1)} %bitcast.9), calls=%async_computation.10 | async-start | bytes 8388608
  42.7 1.5 %collective-permute-start.3 = (bf16[8,32,512]{2,1,0:T(8,128)(2,1)S(1)}, bf16[8,32,512]{2,1,0:T(8,128)(2,1)S(1)}, u32[]{:S(2)}, u32[]{:S(2)}) collective-permute-start(bf16[8,32,512]{2,1,0:T(8,128)(2,1)S(1)} %get-tuple-element.31), channel_id=1, source_target_pairs={{0,1},{1,0},{2,3},{3,2},{4,5},{5,4},{6,7},{7,6},{8,9},{9,8},{10,11... | collective-permute-start | bytes 786440 | tf_op jit(solution)/shard_map/ppermute | solution.py:72
  44.3 28.9 %slice-start.2 = ((s8[16777216]{0:T(1024)(128)(4,1)}), s8[4194304]{0:T(1024)(128)(4,1)S(1)}, s32[]{:S(2)}) async-start(s8[16777216]{0:T(1024)(128)(4,1)} %bitcast.7), calls=%async_computation.7 | async-start | bytes 8388608
  44.3 28.9 %slice-start.6 = ((s8[16777216]{0:T(1024)(128)(4,1)}), s8[4194304]{0:T(1024)(128)(4,1)S(1)}, s32[]{:S(2)}) async-start(s8[16777216]{0:T(1024)(128)(4,1)} %bitcast.9), calls=%async_computation.11 | async-start | bytes 8388608
  56.8 16.4 %slice-start.3 = ((s8[16777216]{0:T(1024)(128)(4,1)}), s8[4194304]{0:T(1024)(128)(4,1)S(1)}, s32[]{:S(2)}) async-start(s8[16777216]{0:T(1024)(128)(4,1)} %bitcast.7), calls=%async_computation.8 | async-start | bytes 8388608
  56.8 16.5 %slice-start.7 = ((s8[16777216]{0:T(1024)(128)(4,1)}), s8[4194304]{0:T(1024)(128)(4,1)S(1)}, s32[]{:S(2)}) async-start(s8[16777216]{0:T(1024)(128)(4,1)} %bitcast.9), calls=%async_computation.12 | async-start | bytes 8388608
  71.6 1.6 %collective-permute-start.4 = (bf16[8,32,640]{2,1,0:T(8,128)(2,1)S(1)}, bf16[8,32,640]{2,1,0:T(8,128)(2,1)S(1)}, u32[]{:S(2)}, u32[]{:S(2)}) collective-permute-start(bf16[8,32,640]{2,1,0:T(8,128)(2,1)S(1)} %all_to_all.28.refs_0_), channel_id=1, source_target_pairs={{0,1},{1,0},{2,3},{3,2},{4,5},{5,4},{6,7},{7,6},{8,9},{9,8},{10,11... | collective-permute-start | bytes 983048 | tf_op jit(solution)/shard_map/ppermute | solution.py:72
  83.4 1.6 %collective-permute-start.5 = (bf16[8,32,512]{2,1,0:T(8,128)(2,1)S(1)}, bf16[8,32,512]{2,1,0:T(8,128)(2,1)S(1)}, u32[]{:S(2)}, u32[]{:S(2)}) collective-permute-start(bf16[8,32,512]{2,1,0:T(8,128)(2,1)S(1)} %get-tuple-element.38), channel_id=1, source_target_pairs={{0,1},{1,0},{2,3},{3,2},{4,5},{5,4},{6,7},{7,6},{8,9},{9,8},{10,11... | collective-permute-start | bytes 786440 | tf_op jit(solution)/shard_map/ppermute | solution.py:72

commit v4 on v3

--- a/solution.py
+++ b/solution.py
@@ -262,45 +262,94 @@
     )
 
 
-def stage(tokens, gains, lifts, parents, place, request, ahead, chips):
-    rows, cols = tokens.shape
-    outs = (
-        VMEM((chips, rows, cols), tokens.dtype),
-        VMEM(tokens.shape, tokens.dtype),
-        *[VMEM(g.shape, g.dtype) for g in gains],
-        *[VMEM(a.shape[1:], a.dtype) for a in lifts],
-        VMEM(parents.shape, parents.dtype),
-        VMEM((8, LANES), jnp.int32),
-    )
-    count = len(outs) - 1 + chips - 1
-
-    def kernel(place_ref, request_ref, *refs):
-        ins, outs, sem = refs[:6], refs[6 + len(ahead) : -1], refs[-1]
-        token_ref, parent_ref = ins[0], ins[5]
-        pairs = [(token_ref, outs[0].at[chip]) for chip in range(chips)]
-        pairs += [(token_ref, outs[1])]
-        pairs += [(ins[1], outs[2]), (ins[2], outs[3])]
-        pairs += [(ins[k].at[request_ref[0]], outs[k + 1]) for k in (3, 4)]
-        pairs += [(parent_ref, outs[6])]
+def near(x):
+    return pltpu.with_memory_space_constraint(x, VMEM)
+
+
+def distant(x):
+    return pltpu.with_memory_space_constraint(x, pltpu.HBM)
+
+
+def spread(tokens, kept, ahead, chips):
+    outs = (VMEM((chips,) + tokens.shape, tokens.dtype),)
+    outs += tuple(VMEM(a.shape, a.dtype) for a in (tokens, *kept))
+    used = 1 + len(kept)
+
+    def kernel(*refs):
+        ins, outs, sem = refs[:used], refs[used + len(ahead) : -1], refs[-1]
+        pairs = [(ins[0], outs[0].at[chip]) for chip in range(chips)]
+        pairs += [(ins[k], outs[1 + k]) for k in range(used)]
         copies = [
             pltpu.make_async_copy(src, dst, sem.at[k]) for k, (src, dst) in enumerate(pairs)
         ]
         for copy in copies:
             copy.start()
-        outs[7][...] = jnp.full(outs[7].shape, place_ref[request_ref[0]], jnp.int32)
         for copy in copies:
             copy.wait()
 
-    args = (tokens, *gains, *lifts, parents, *ahead)
     return pl.pallas_call(
         kernel,
         out_shape=outs,
-        in_specs=[SCALAR] * 2 + [FAR] * len(args),
+        in_specs=[FAR] * (used + len(ahead)),
         out_specs=(WHOLE,) * len(outs),
-        scratch_shapes=[pltpu.SemaphoreType.DMA((count + 1,))],
-        name="stage",
+        scratch_shapes=[pltpu.SemaphoreType.DMA((chips + used,))],
+        name="spread",
         compiler_params=pltpu.CompilerParams(vmem_limit_bytes=2 << 20),
-    )(place, request, *[pltpu.with_memory_space_constraint(a, pltpu.HBM) for a in args])
+    )(*[distant(a) for a in (tokens, *kept, *ahead)])
+
+
+def table_kernel(
+    request_ref, place_ref, query_ref, up_ref, parent_ref, after_ref,
+    query_out, up_out, owner_out, cosine_out, sine_out, reach_out, place, sem,
+):
+    request = request_ref[0]
+    copies = [
+        pltpu.make_async_copy(place_ref, place, sem.at[0]),
+        pltpu.make_async_copy(query_ref.at[request], query_out, sem.at[1]),
+        pltpu.make_async_copy(up_ref.at[request], up_out, sem.at[2]),
+    ]
+    for copy in copies:
+        copy.start()
+    rows, head = cosine_out.shape
+    half = head // 2
+    own = lax.broadcasted_iota(jnp.int32, (rows, rows), 0)
+    other = lax.broadcasted_iota(jnp.int32, (rows, rows), 1)
+    eye = jnp.where(own == other, 1.0, 0.0)
+    links = jnp.where(parent_ref[...] == own, 1.0, 0.0)
+    reach = dot_rows(eye.astype(jnp.bfloat16), jnp.maximum(links, eye).astype(jnp.bfloat16))
+    for _ in range((rows - 1).bit_length()):
+        square = reach.astype(jnp.bfloat16)
+        reach = jnp.minimum(dot(square, square), 1.0)
+    reach_out[...] = reach
+    lane = lax.broadcasted_iota(jnp.int32, (rows, head), 1)
+    place_in_half = jnp.where(lane < half, lane, lane - half).astype(jnp.float32)
+    freq = jnp.exp(place_in_half * np.float32(-2.0 / head * np.log(ROPE_BASE)))
+    angle = (jnp.sum(reach, axis=-1, keepdims=True) - 1.0) * freq
+    sine = jnp.sin(angle)
+    cosine_out[...] = jnp.cos(angle)
+    sine_out[...] = jnp.where(lane < half, -sine, sine)
+    for copy in copies:
+        copy.wait()
+    owner_out[...] = jnp.full(owner_out.shape, place[request], jnp.int32)
+
+
+def tables(request, place, lifts, parents, after):
+    rows = parents.shape[1]
+    shapes = [(a.shape[1:], a.dtype) for a in lifts]
+    shapes += [((8, LANES), jnp.int32)]
+    shapes += [((rows, HEAD_SIZE), jnp.float32)] * 2 + [((rows, rows), jnp.float32)]
+    return pl.pallas_call(
+        table_kernel,
+        out_shape=tuple(VMEM(*a) for a in shapes),
+        in_specs=[SCALAR] + [FAR] * 3 + [WHOLE] * 2,
+        out_specs=(WHOLE,) * len(shapes),
+        scratch_shapes=[
+            pltpu.SMEM(place.shape, jnp.int32),
+            pltpu.SemaphoreType.DMA((3,)),
+        ],
+        name="tables",
+        compiler_params=pltpu.CompilerParams(vmem_limit_bytes=2 << 20),
+    )(request, *[distant(a) for a in (place, *lifts)], near(parents), near(after))
 
 
 def dot_chunks(left, weight_ref):
@@ -348,39 +397,33 @@
 
 
 def project_kernel(
-    mine_ref, theirs_ref, gain_ref, query_ref, key_ref, value_ref, factor_ref,
-    query_out, pair_out, payload_out, scratch,
+    mine_ref, theirs_ref, gain_ref, owner_ref, other_ref, query_ref, key_ref, value_ref,
+    factor_ref, query_out, pair_out, payload_out, scratch,
 ):
     chips, rows, cols = mine_ref.shape
+    core = core_index()
     norm_blocks(mine_ref, theirs_ref, gain_ref, scratch, cols)
     normed = scratch[...]
     rank = factor_ref.shape[0] // 2
-    low = dot_rows(normed, factor_ref[:rank, :])
+    here = (owner_ref[:1, :1] & 1) == core
+    low = jnp.where(
+        here, dot_rows(normed, factor_ref[:rank, :]), dot_rows(normed, other_ref[:rank, :])
+    )
     query_out[...] = dot_chunks(normed, query_ref)
     half = key_ref.shape[0]
     pair_out[:, :half] = dot_rows(normed, key_ref[...]).astype(jnp.bfloat16)
     pair_out[:, half:] = dot_rows(normed, value_ref[...]).astype(jnp.bfloat16)
+    parts = rows // rank
     padded = jnp.concatenate([low, jnp.zeros((rows, LANES - rank), jnp.float32)], axis=1)
     padded = padded.astype(jnp.bfloat16)
     for chip in range(chips):
-        for side in range(2):
-            at = (2 * chip + side) * cols
-            payload_out[chip, side * rank : (side + 1) * rank, :cols] = factor_ref[
-                rank:, at : at + cols
-            ]
-        payload_out[chip, :, cols:] = padded
-
-
-def pick_kernel(owner_ref, got_ref, out_ref):
-    owner = owner_ref[:1, :1] - core_index()
-    piece = jnp.zeros(out_ref.shape, jnp.float32)
-    for chip in range(got_ref.shape[0]):
-        piece = piece + jnp.where(owner == 2 * chip, got_ref[chip].astype(jnp.float32), 0.0)
-    out_ref[...] = piece.astype(jnp.bfloat16)
-
-
-def joined(mine_ref, theirs_ref):
-    return mine_ref[...].astype(jnp.float32) + theirs_ref[...].astype(jnp.float32)
+        at = pl.multiple_of((2 * chip + core) * cols, cols)
+        own = factor_ref[rank:, pl.ds(at, cols)].astype(jnp.float32)
+        other = other_ref[rank:, pl.ds(at, cols)].astype(jnp.float32)
+        payload_out[chip, :, :cols] = jnp.where(here, own, other).astype(jnp.bfloat16)
+        for part in range(parts):
+            lanes = slice(cols + part * LANES, cols + (part + 1) * LANES)
+            payload_out[chip, :, lanes] = padded[part * rank : (part + 1) * rank]
 
 
 def split_product(left, weight_ref, mine_out, theirs_out):
@@ -394,45 +437,42 @@
 
 
 def attend_kernel(
-    query_ref, pair_mine, pair_theirs, piece_mine, piece_theirs,
-    lift_ref, parent_ref, freq_ref, output_ref, mine_out, theirs_out,
+    query_ref, pair_mine, pair_theirs, owner_ref, got_ref, lift_ref, cosine_ref, sine_ref,
+    reach_ref, output_ref, mine_out, theirs_out, piece_out,
 ):
     rows, query_cols = query_ref.shape
+    chips, _, cols = mine_out.shape
     head = HEAD_SIZE
     heads = query_cols // head
     half = head // 2
     rank = lift_ref.shape[0]
-    first = core_index() == 0
-    own = lax.broadcasted_iota(jnp.int32, (rows, rows), 0)
-    other = lax.broadcasted_iota(jnp.int32, (rows, rows), 1)
-    eye = jnp.where(own == other, 1.0, 0.0)
-    links = jnp.where(parent_ref[...] == own, 1.0, 0.0)
-    reach = dot_rows(eye.astype(jnp.bfloat16), jnp.maximum(links, eye).astype(jnp.bfloat16))
-    for _ in range((rows - 1).bit_length()):
-        square = reach.astype(jnp.bfloat16)
-        reach = jnp.minimum(dot(square, square), 1.0)
-    angle = (jnp.sum(reach, axis=-1, keepdims=True) - 1.0) * freq_ref[...]
+    owner = owner_ref[:1, :1]
+    piece = jnp.zeros(got_ref.shape[1:], jnp.float32)
+    for chip in range(chips):
+        sent = got_ref[chip].astype(jnp.float32)
+        piece = piece + jnp.where((owner >> 1) == chip, sent, 0.0)
+    piece_out[...] = piece.astype(jnp.bfloat16)
+    low = jnp.concatenate(
+        [piece[:, at : at + LANES] for at in range(cols, piece.shape[1], LANES)], axis=0
+    )
     lane = lax.broadcasted_iota(jnp.int32, (rows, head), 1)
-    cosine = jnp.cos(angle)
-    sine = jnp.sin(angle)
-    sine = jnp.where(lane < half, -sine, sine)
+    cosine = cosine_ref[...]
+    sine = sine_ref[...]
 
     def rotate(wide):
         return (wide * cosine + pltpu.roll(wide, half, 1) * sine).astype(jnp.bfloat16)
 
+    first = core_index() == 0
     even, odd = in_order(pair_mine[...], pair_theirs[...], first)
     key = rotate(jnp.where(lane < half, even, pltpu.roll(odd, half, 1)))
     value = jnp.where(lane < half, pltpu.roll(even, half, 1), odd).astype(jnp.bfloat16)
-    piece = joined(piece_mine, piece_theirs)
-    cols = piece.shape[1] - LANES
-    low = piece[:, cols : cols + rank].astype(jnp.bfloat16)
-    query = query_ref[...] + dot(low, lift_ref[...])
+    query = query_ref[...] + dot(low[:, :rank].astype(jnp.bfloat16), lift_ref[...])
     query = query.astype(jnp.bfloat16).astype(jnp.float32)
     stacked = jnp.concatenate(
         [rotate(query[:, h * head : (h + 1) * head]) for h in range(heads)], axis=0
     )
     scores = dot_rows(stacked, key) * head ** (-0.5)
-    weights = jnp.exp(scores) * jnp.concatenate([reach] * heads, axis=0)
+    weights = jnp.exp(scores) * jnp.concatenate([reach_ref[...]] * heads, axis=0)
     probs = (weights / jnp.sum(weights, axis=-1, keepdims=True)).astype(jnp.bfloat16)
     mixed = dot(probs, value).astype(jnp.bfloat16)
     mixed = jnp.concatenate([mixed[h * rows : (h + 1) * rows] for h in range(heads)], axis=1)
@@ -440,7 +480,7 @@
 
 
 def hidden_kernel(
-    got_ref, token_ref, gain_ref, piece_mine, piece_theirs,
+    got_ref, token_ref, gain_ref, piece_ref,
     hidden_out, payload_out,
 ):
     chips, rows, cols = got_ref.shape
@@ -450,15 +490,14 @@
         added = added + got_ref[chip].astype(jnp.float32)
     hidden = (total + added).astype(jnp.bfloat16)
     hidden_out[...] = hidden
-    piece = joined(piece_mine, piece_theirs)
-    rank = piece.shape[0] // 2
-    factor = jnp.where(core_index() == 0, piece[:rank, :cols], piece[rank:, :cols])
+    factor = piece_ref[:, :cols]
+    rank = factor.shape[0]
     device = lax.axis_index("tp")
     gain = gain_block(gain_ref, 0, cols)
     for index in range(1, 2 * chips):
         gain = jnp.where(device == index, gain_block(gain_ref, index, cols), gain)
     gained = hidden.astype(jnp.float32) * gain
-    low = dot_rows(gained.astype(jnp.bfloat16), factor.astype(jnp.bfloat16))
+    low = dot_rows(gained.astype(jnp.bfloat16), factor)
     padded = jnp.concatenate([low, jnp.zeros((rows, LANES - rank), jnp.float32)], axis=1)
     padded = padded.astype(jnp.bfloat16)
     for chip in range(chips):
@@ -523,52 +562,50 @@
     rows, cols = tokens.shape
     chips = lax.axis_size("tp") // 2
     width = query_weight.shape[0]
-    half = HEAD_SIZE // 2
-    freq = ROPE_BASE ** (-np.arange(half, dtype=np.float32) * np.float32(2.0 / HEAD_SIZE))
-    freq = jnp.asarray(np.concatenate([freq, freq])[None].astype(np.float32))
     shape = jax.ShapeDtypeStruct
     bf16, f32 = jnp.bfloat16, jnp.float32
-    attention_gain = attention_gain.reshape(-1, LANES)
-    forward_gain = forward_gain.reshape(-1, LANES)
     wide = cols + LANES
-    split_out = (shape((chips, rows, cols), f32), shape((chips, rows, cols), bf16))
-
     heavy = (gate_weight, up_weight, down_weight)
     most = heavy + (query_weight, output_weight)
-    spread, kept_tokens, gain_one, gain_two, query_lift, up_lift, parents, owner = stage(
+    rank = adapter_query.shape[1]
+    split_out = (shape((chips, rows, cols), f32), shape((chips, rows, cols), bf16))
+    factors = adapter_inputs[0].T
+
+    spread_tokens, kept_tokens, gain_one, gain_two, parents = spread(
         tokens,
-        (attention_gain, forward_gain),
-        (adapter_query, adapter_upper),
-        tree_parents,
-        adapter_place,
-        request_adapter,
+        (attention_gain.reshape(-1, LANES), forward_gain.reshape(-1, LANES), tree_parents),
         heavy,
         chips,
     )
-    mine = exchange(spread, "tp")
+    mine = exchange(spread_tokens, "tp")
+    mine, held = lax.optimization_barrier((mine, adapter_inputs))
     theirs = partner_2(mine, "tp", 0)
+    factors_theirs = partner_2(held, "tp", 0)[0].T
+    query_lift, up_lift, owner, cosine, sine, reach = tables(
+        request_adapter, adapter_place, (adapter_query, adapter_upper), parents, mine
+    )
     query, pair, payload = call(
         project_kernel,
         "project",
         (
             shape((rows, query_weight.shape[1]), f32),
             shape((rows, 2 * key_matrix.shape[1]), bf16),
-            shape((chips, rows, wide), bf16),
+            shape((chips, rank, cols + rows // rank * LANES), bf16),
         ),
-        (mine, theirs, gain_one),
-        (query_weight, key_matrix.T, value_matrix.T, adapter_inputs[0].T),
+        (mine, theirs, gain_one, owner, factors_theirs),
+        (query_weight, key_matrix.T, value_matrix.T, factors),
         heavy,
         [VMEM((rows, width), bf16)],
     )
-    pair_theirs = partner_2(pair, "tp", 0)
-    got = exchange(payload, "tp")
-    (piece,) = call(pick_kernel, "pick", (shape((rows, wide), bf16),), (owner, got), (), most)
-    piece_theirs = partner_2(piece, "tp", 0)
-    kept, sent = call(
+    pair_theirs, payload = lax.optimization_barrier((partner_2(pair, "tp", 0), payload))
+    kept, sent, piece = call(
         attend_kernel,
         "attend",
-        split_out,
-        (query, pair, pair_theirs, piece, piece_theirs, query_lift, parents, freq),
+        (*split_out, shape(payload.shape[1:], bf16)),
+        (
+            query, pair, pair_theirs, owner, exchange(payload, "tp"), query_lift, cosine,
+            sine, reach,
+        ),
         (output_weight,),
         heavy + (query_weight,),
     )
@@ -577,7 +614,7 @@
         hidden_kernel,
         "hidden",
         (shape((rows, cols), bf16), shape((chips, rows, wide), bf16)),
-        (exchange(chip_sum, "tp"), kept_tokens, gain_two, piece, piece_theirs),
+        (exchange(chip_sum, "tp"), kept_tokens, gain_two, piece),
         (),
         most,
     )

time: 98 us -> 92.5 us (0.944)
  blocking collectives: 69.8 us -> 66.6 us
  local copies, waits for them, and re-layouts: 1.37 us -> 0.07 us
  waiting for transfers between devices: 6.93 us -> 5.79 us
    all_to_all x5, blocking collectives: 69.8 us -> 66.6 us  [exchange(): lax.all_to_all(blocks, axis, 0, 0, axis_index_groups=core_groups(axis), t...]
    unnamed x32 -> x28, local copies, waits for them, and re-layouts: 1.37 us -> 0.07 us
    ppermute x6, waiting for transfers between devices: 6.93 us -> 5.79 us  [partner_2(): return lax.ppermute(block, axis, route)]
    pallas_call x1 -> x2, Pallas kernels: 1.83 us -> 2.13 us  [the longest x1 1.19 us: spread(): pl.pallas_call(kernel, out_shape=outs, in_specs=[FAR] * (used + len(ahead...]
    pallas_call x5 -> x4, Pallas kernels: 15.3 us -> 15.1 us  [call(): pl.pallas_call(run, out_shape=outs, in_specs=[WHOLE] * (len(args) + len(w...]
  transfers between devices with their start and end apart: 6 -> 6, of which waited for: 5 -> 5; matrix products, arithmetic and copies ran while one was open for 0% -> 0% of each run, Pallas kernels for 0% -> 1%
where the time goes in v4:
time: 92.5 us; the launch traced here: 92.2 us
  blocking collectives  66.6 us (72%)
  Pallas kernels  17.2 us (19%)
  waiting for transfers between devices  5.79 us (6%)
    all_to_all x5, blocking collectives, exchange(): lax.all_to_all(blocks, axis, 0, 0, axis_index_groups=core_groups(axis), t...  66.6 us
    pallas_call x4, Pallas kernels, call(): pl.pallas_call(run, out_shape=outs, in_specs=[WHOLE] * (len(args) + len(w...  15.1 us
    ppermute x6, waiting for transfers between devices, partner_2(): return lax.ppermute(block, axis, route)  5.79 us
  transfers between devices with their start and end apart: 6, of which 5 were waited for; matrix products, arithmetic and copies ran while one was open for 0% of the time, Pallas kernels for 1%

profile of v4, /device:TPU:0, one launch (start us, length us, event | category | flops | bytes accessed | tf_op | source)
XLA Modules:
  0.0 92.2 jit_solution(12210975479415547924)
XLA Ops:
  0.0 1.2 %spread.1 = (bf16[8,32,512]{2,1,0:T(8,128)(2,1)S(1)}, bf16[32,512]{1,0:T(8,128)(2,1)S(1)}, bf16[64,128]{1,0:T(8,128)(2,1)S(1)}, bf16[64,128]{1,0:T(8,128)(2,1)S(1)}, s32[1,32]{1,0:T(1,128)S(1)}) custom-call(bf16[32,512]{1,0:T(8,128)(2,1)} %refs_0_.1, bf16[64,128]{1,0:T(8,128)(2,1)} %bitcast.20, bf16[64,128]{1,0:T(8,128)(2,1)} %bitcast.21, s32[1,32]{1,0:T(1,128)} %refs_3_.1, ...), custom_call_target="tpu_custom_call" | custom-call | tf_op jit(solution)/shard_map/spread/pallas_call | solution.py:290
  1.2 16.2 %all_to_all.25.after_ref.refs_0_ = bf16[8,32,512]{2,1,0:T(8,128)(2,1)S(1)} all-to-all(bf16[8,32,512]{2,1,0:T(8,128)(2,1)S(1)} %get-tuple-element.30), channel_id=1, replica_groups={{0,2,4,6,8,10,12,14},{1,3,5,7,9,11,13,15},{16,18,20,22,24,26,28,30},{17..., dimensions={0} | all-to-all | bytes 524288 | tf_op jit(solution)/shard_map/all_to_all | solution.py:22
  17.5 0.5 collective-permute-start
  18.6 0.9 %tables.1 = (bf16[16,512]{1,0:T(8,128)(2,1)S(1)}, bf16[16,1024]{1,0:T(8,128)(2,1)S(1)}, s32[8,128]{1,0:T(8,128)S(1)}, f32[32,128]{1,0:T(8,128)S(1)}, f32[32,128]{1,0:T(8,128)S(1)}, /*index=5*/f32[32,32]{1,0:T(8,128)S(1)}) custom-call(s32[1]{0:T(128)S(6)} %copy.17.request_ref, s32[16]{0:T(128)} %place_ref.1, bf16[16,16,512]{2,1,0:T(8,128)(2,1)} %query_ref.1, ...), custom_call_target="tpu_custom_call" | custom-call | tf_op jit(solution)/shard_map/tables/pallas_call | solution.py:341
  19.6 0.2 collective-permute-done.refs_1_
  19.8 0.0 slice-start.9
  19.8 2.7 %project.1 = (f32[32,512]{1,0:T(8,128)S(1)}, bf16[32,128]{1,0:T(8,128)(2,1)S(1)}, bf16[8,16,768]{2,1,0:T(8,128)(2,1)S(1)}) custom-call(bf16[8,32,512]{2,1,0:T(8,128)(2,1)S(1)} %all_to_all.25.after_ref.refs_0_, bf16[8,32,512]{2,1,0:T(8,128)(2,1)S(1)} %collective-permute-done.refs_1_, bf16[64,128]{1,0:T(8,128)(2,1)S(1)} %get-tuple-element.32.refs_2_, ...), custom_call_target="tpu_custom_call" | custom-call | flops 352321536 | bytes 11010048 | tf_op jit(solution)/shard_map/project/pallas_call | solution.py:248
  22.4 0.2 collective-permute-start.2
  22.6 1.0 %collective-permute-done.2.refs_2_ = bf16[32,128]{1,0:T(8,128)(2,1)S(1)} collective-permute-done((bf16[32,128]{1,0:T(8,128)(2,1)S(1)}, bf16[32,128]{1,0:T(8,128)(2,1)S(1)}, u32[]{:S(2)}, u32[]{:S(2)}) %collective-permute-start.2) | collective-permute-done | bytes 8224 | tf_op jit(solution)/shard_map/ppermute | solution.py:72
  23.6 11.7 %all_to_all.26.refs_4_ = bf16[8,16,768]{2,1,0:T(8,128)(2,1)S(1)} all-to-all(bf16[8,16,768]{2,1,0:T(8,128)(2,1)S(1)} %get-tuple-element.40), channel_id=1, replica_groups={{0,2,4,6,8,10,12,14},{1,3,5,7,9,11,13,15},{16,18,20,22,24,26,28,30},{17..., dimensions={0} | all-to-all | bytes 393216 | tf_op jit(solution)/shard_map/all_to_all | solution.py:22
  35.3 2.1 %attend.1 = (f32[8,32,512]{2,1,0:T(8,128)S(1)}, bf16[8,32,512]{2,1,0:T(8,128)(2,1)S(1)}, bf16[16,768]{1,0:T(8,128)(2,1)S(1)}) custom-call(f32[32,512]{1,0:T(8,128)S(1)} %get-tuple-element.36.refs_0_, bf16[32,128]{1,0:T(8,128)(2,1)S(1)} %get-tuple-element.37.refs_1_, bf16[32,128]{1,0:T(8,128)(2,1)S(1)} %collective-permute-done.2.refs_2_, ...), custom_call_target="tpu_custom_call" | custom-call | flops 268435456 | bytes 8388608 | tf_op jit(solution)/shard_map/attend/pallas_call | solution.py:248
  37.5 1.5 %collective-permute-done.3 = bf16[8,32,512]{2,1,0:T(8,128)(2,1)S(1)} collective-permute-done((bf16[8,32,512]{2,1,0:T(8,128)(2,1)S(1)}, bf16[8,32,512]{2,1,0:T(8,128)(2,1)S(1)}, u32[]{:S(2)}, u32[]{:S(2)}) %collective-permute-start.3) | collective-permute-done | bytes 262176 | tf_op jit(solution)/shard_map/ppermute | solution.py:72
  39.0 0.1 add_convert_fusion.1
  39.1 0.0 slice-start.2
  39.1 12.4 %all_to_all.27.refs_0_ = bf16[8,32,512]{2,1,0:T(8,128)(2,1)S(1)} all-to-all(bf16[8,32,512]{2,1,0:T(8,128)(2,1)S(1)} %add_convert_fusion.1), channel_id=1, replica_groups={{0,2,4,6,8,10,12,14},{1,3,5,7,9,11,13,15},{16,18,20,22,24,26,28,30},{17..., dimensions={0} | all-to-all | bytes 524288 | tf_op jit(solution)/shard_map/all_to_all | solution.py:22
  51.6 0.2 hidden.1
  51.8 14.3 %all_to_all.28.refs_0_ = bf16[8,32,640]{2,1,0:T(8,128)(2,1)S(1)} all-to-all(bf16[8,32,640]{2,1,0:T(8,128)(2,1)S(1)} %get-tuple-element.51), channel_id=1, replica_groups={{0,2,4,6,8,10,12,14},{1,3,5,7,9,11,13,15},{16,18,20,22,24,26,28,30},{17..., dimensions={0} | all-to-all | bytes 655360 | tf_op jit(solution)/shard_map/all_to_all | solution.py:22
  66.0 1.6 %collective-permute-done.4.refs_1_ = bf16[8,32,640]{2,1,0:T(8,128)(2,1)S(1)} collective-permute-done((bf16[8,32,640]{2,1,0:T(8,128)(2,1)S(1)}, bf16[8,32,640]{2,1,0:T(8,128)(2,1)S(1)}, u32[]{:S(2)}, u32[]{:S(2)}) %collective-permute-start.4) | collective-permute-done | bytes 327712 | tf_op jit(solution)/shard_map/ppermute | solution.py:72
  67.8 10.1 %forward.1 = (f32[8,32,512]{2,1,0:T(8,128)S(1)}, bf16[8,32,512]{2,1,0:T(8,128)(2,1)S(1)}) custom-call(bf16[8,32,640]{2,1,0:T(8,128)(2,1)S(1)} %all_to_all.28.refs_0_, bf16[8,32,640]{2,1,0:T(8,128)(2,1)S(1)} %collective-permute-done.4.refs_1_, bf16[64,128]{1,0:T(8,128)(2,1)S(1)} %get-tuple-element.48.refs_2_, bf16[16,1024]{1,0:T(8,128)(2,1)S(1)} %get-tuple-element.52.refs_3_, ...), custom_call_target="tpu_custom_call" | custom-call | flops 1610612736 | bytes 50331648 | tf_op jit(solution)/shard_map/forward/pallas_call | solution.py:248
  77.8 0.2 collective-permute-start.5
  78.0 1.4 %collective-permute-done.5 = bf16[8,32,512]{2,1,0:T(8,128)(2,1)S(1)} collective-permute-done((bf16[8,32,512]{2,1,0:T(8,128)(2,1)S(1)}, bf16[8,32,512]{2,1,0:T(8,128)(2,1)S(1)}, u32[]{:S(2)}, u32[]{:S(2)}) %collective-permute-start.5) | collective-permute-done | bytes 262176 | tf_op jit(solution)/shard_map/ppermute | solution.py:72
  79.4 0.1 add_convert_fusion
  79.5 12.0 %all_to_all.29 = bf16[8,32,512]{2,1,0:T(8,128)(2,1)S(1)} all-to-all(bf16[8,32,512]{2,1,0:T(8,128)(2,1)S(1)} %add_convert_fusion), channel_id=1, replica_groups={{0,2,4,6,8,10,12,14},{1,3,5,7,9,11,13,15},{16,18,20,22,24,26,28,30},{17..., dimensions={0} | all-to-all | bytes 524288 | tf_op jit(solution)/shard_map/all_to_all | solution.py:22
  91.5 0.6 add_convert_fusion.2
  (34 shorter events, 0.1 us)
Async XLA Ops:
  0.0 17.5 %copy-start.3 = (bf16[1,8192,32]{1,2,0:T(8,128)(2,1)S(1)}, bf16[1,8192,32]{1,2,0:T(8,128)(2,1)}, u32[]{:S(2)}) copy-start(bf16[1,8192,32]{1,2,0:T(8,128)(2,1)} %param.26) | copy-start | bytes 1572868
  0.0 19.8 %copy-start = (bf16[8192,512]{1,0:T(8,128)(2,1)S(1)}, bf16[8192,512]{1,0:T(8,128)(2,1)}, u32[]{:S(2)}) copy-start(bf16[8192,512]{1,0:T(8,128)(2,1)} %refs_7_.3) | copy-start | bytes 25165828
  0.0 19.8 %copy-start.1 = (bf16[8192,64]{0,1:T(8,128)(2,1)S(1)}, bf16[8192,64]{0,1:T(8,128)(2,1)}, u32[]{:S(2)}) copy-start(bf16[8192,64]{0,1:T(8,128)(2,1)} %param.20) | copy-start | bytes 3145732
  0.0 19.8 %copy-start.2 = (bf16[8192,64]{0,1:T(8,128)(2,1)S(1)}, bf16[8192,64]{0,1:T(8,128)(2,1)}, u32[]{:S(2)}) copy-start(bf16[8192,64]{0,1:T(8,128)(2,1)} %param.21) | copy-start | bytes 3145732
  1.2 34.1 %slice-start.8 = ((s8[8388608]{0:T(1024)(128)(4,1)}), s8[4194304]{0:T(1024)(128)(4,1)S(1)}, s32[]{:S(2)}) async-start(s8[8388608]{0:T(1024)(128)(4,1)} %bitcast.14), calls=%async_computation.13 | async-start | bytes 8388608
  17.5 2.3 %collective-permute-start.1 = (bf16[1,8192,32]{1,2,0:T(8,128)(2,1)S(1)}, bf16[1,8192,32]{1,2,0:T(8,128)(2,1)S(1)}, u32[]{:S(2)}, u32[]{:S(2)}) collective-permute-start(bf16[1,8192,32]{1,2,0:T(8,128)(2,1)S(1)} %copy-done.3), channel_id=1, source_target_pairs={{0,1},{1,0},{2,3},{3,2},{4,5},{5,4},{6,7},{7,6},{8,9},{9,8},{10,11... | collective-permute-start | bytes 1572872 | tf_op jit(solution)/shard_map/ppermute | solution.py:72
  17.5 2.3 %collective-permute-start = (bf16[8,32,512]{2,1,0:T(8,128)(2,1)S(1)}, bf16[8,32,512]{2,1,0:T(8,128)(2,1)S(1)}, u32[]{:S(2)}, u32[]{:S(2)}) collective-permute-start(bf16[8,32,512]{2,1,0:T(8,128)(2,1)S(1)} %all_to_all.25.after_ref.refs_0_), channel_id=1, source_target_pairs={{0,1},{1,0},{2,3},{3,2},{4,5},{5,4},{6,7},{7,6},{8,9},{9,8},{10,11... | collective-permute-start | bytes 786440 | tf_op jit(solution)/shard_map/ppermute | solution.py:72
  19.8 15.5 %slice-start.9 = ((s8[8388608]{0:T(1024)(128)(4,1)}), s8[4194304]{0:T(1024)(128)(4,1)S(1)}, s32[]{:S(2)}) async-start(s8[8388608]{0:T(1024)(128)(4,1)} %bitcast.14), calls=%async_computation.14 | async-start | bytes 8388608
  22.4 1.2 %collective-permute-start.2 = (bf16[32,128]{1,0:T(8,128)(2,1)S(1)}, bf16[32,128]{1,0:T(8,128)(2,1)S(1)}, u32[]{:S(2)}, u32[]{:S(2)}) collective-permute-start(bf16[32,128]{1,0:T(8,128)(2,1)S(1)} %get-tuple-element.37.refs_1_), channel_id=1, source_target_pairs={{0,1},{1,0},{2,3},{3,2},{4,5},{5,4},{6,7},{7,6},{8,9},{9,8},{10,11... | collective-permute-start | bytes 24584 | tf_op jit(solution)/shard_map/ppermute | solution.py:72
  35.3 32.4 %slice-start = ((s8[16777216]{0:T(1024)(128)(4,1)}), s8[4194304]{0:T(1024)(128)(4,1)S(1)}, s32[]{:S(2)}) async-start(s8[16777216]{0:T(1024)(128)(4,1)} %bitcast.10), calls=%async_computation.5 | async-start | bytes 8388608
  35.3 32.4 %slice-start.1 = ((s8[16777216]{0:T(1024)(128)(4,1)}), s8[4194304]{0:T(1024)(128)(4,1)S(1)}, s32[]{:S(2)}) async-start(s8[16777216]{0:T(1024)(128)(4,1)} %bitcast.10), calls=%async_computation.6 | async-start | bytes 8388608
  35.3 32.4 %slice-start.4 = ((s8[16777216]{0:T(1024)(128)(4,1)}), s8[4194304]{0:T(1024)(128)(4,1)S(1)}, s32[]{:S(2)}) async-start(s8[16777216]{0:T(1024)(128)(4,1)} %bitcast.12), calls=%async_computation.9 | async-start | bytes 8388608
  35.3 32.4 %slice-start.5 = ((s8[16777216]{0:T(1024)(128)(4,1)}), s8[4194304]{0:T(1024)(128)(4,1)S(1)}, s32[]{:S(2)}) async-start(s8[16777216]{0:T(1024)(128)(4,1)} %bitcast.12), calls=%async_computation.10 | async-start | bytes 8388608
  37.5 1.5 %collective-permute-start.3 = (bf16[8,32,512]{2,1,0:T(8,128)(2,1)S(1)}, bf16[8,32,512]{2,1,0:T(8,128)(2,1)S(1)}, u32[]{:S(2)}, u32[]{:S(2)}) collective-permute-start(bf16[8,32,512]{2,1,0:T(8,128)(2,1)S(1)} %get-tuple-element.46), channel_id=1, source_target_pairs={{0,1},{1,0},{2,3},{3,2},{4,5},{5,4},{6,7},{7,6},{8,9},{9,8},{10,11... | collective-permute-start | bytes 786440 | tf_op jit(solution)/shard_map/ppermute | solution.py:72
  39.1 28.6 %slice-start.2 = ((s8[16777216]{0:T(1024)(128)(4,1)}), s8[4194304]{0:T(1024)(128)(4,1)S(1)}, s32[]{:S(2)}) async-start(s8[16777216]{0:T(1024)(128)(4,1)} %bitcast.10), calls=%async_computation.7 | async-start | bytes 8388608
  39.1 28.6 %slice-start.6 = ((s8[16777216]{0:T(1024)(128)(4,1)}), s8[4194304]{0:T(1024)(128)(4,1)S(1)}, s32[]{:S(2)}) async-start(s8[16777216]{0:T(1024)(128)(4,1)} %bitcast.12), calls=%async_computation.11 | async-start | bytes 8388608
  51.6 16.1 %slice-start.3 = ((s8[16777216]{0:T(1024)(128)(4,1)}), s8[4194304]{0:T(1024)(128)(4,1)S(1)}, s32[]{:S(2)}) async-start(s8[16777216]{0:T(1024)(128)(4,1)} %bitcast.10), calls=%async_computation.8 | async-start | bytes 8388608
  51.6 16.2 %slice-start.7 = ((s8[16777216]{0:T(1024)(128)(4,1)}), s8[4194304]{0:T(1024)(128)(4,1)S(1)}, s32[]{:S(2)}) async-start(s8[16777216]{0:T(1024)(128)(4,1)} %bitcast.12), calls=%async_computation.12 | async-start | bytes 8388608
  66.0 1.6 %collective-permute-start.4 = (bf16[8,32,640]{2,1,0:T(8,128)(2,1)S(1)}, bf16[8,32,640]{2,1,0:T(8,128)(2,1)S(1)}, u32[]{:S(2)}, u32[]{:S(2)}) collective-permute-start(bf16[8,32,640]{2,1,0:T(8,128)(2,1)S(1)} %all_to_all.28.refs_0_), channel_id=1, source_target_pairs={{0,1},{1,0},{2,3},{3,2},{4,5},{5,4},{6,7},{7,6},{8,9},{9,8},{10,11... | collective-permute-start | bytes 983048 | tf_op jit(solution)/shard_map/ppermute | solution.py:72
  77.8 1.6 %collective-permute-start.5 = (bf16[8,32,512]{2,1,0:T(8,128)(2,1)S(1)}, bf16[8,32,512]{2,1,0:T(8,128)(2,1)S(1)}, u32[]{:S(2)}, u32[]{:S(2)}) collective-permute-start(bf16[8,32,512]{2,1,0:T(8,128)(2,1)S(1)} %get-tuple-element.54), channel_id=1, source_target_pairs={{0,1},{1,0},{2,3},{3,2},{4,5},{5,4},{6,7},{7,6},{8,9},{9,8},{10,11... | collective-permute-start | bytes 786440 | tf_op jit(solution)/shard_map/ppermute | solution.py:72

commit v5 on v4

--- a/solution.py
+++ b/solution.py
@@ -397,19 +397,18 @@
 
 
 def project_kernel(
-    mine_ref, theirs_ref, gain_ref, owner_ref, other_ref, query_ref, key_ref, value_ref,
-    factor_ref, query_out, pair_out, payload_out, scratch,
+    mine_ref, theirs_ref, gain_ref, owner_ref, other_ref, key_ref, value_ref, factor_ref,
+    normed_out, pair_out, payload_out,
 ):
     chips, rows, cols = mine_ref.shape
     core = core_index()
-    norm_blocks(mine_ref, theirs_ref, gain_ref, scratch, cols)
-    normed = scratch[...]
+    norm_blocks(mine_ref, theirs_ref, gain_ref, normed_out, cols)
+    normed = normed_out[...]
     rank = factor_ref.shape[0] // 2
     here = (owner_ref[:1, :1] & 1) == core
     low = jnp.where(
         here, dot_rows(normed, factor_ref[:rank, :]), dot_rows(normed, other_ref[:rank, :])
     )
-    query_out[...] = dot_chunks(normed, query_ref)
     half = key_ref.shape[0]
     pair_out[:, :half] = dot_rows(normed, key_ref[...]).astype(jnp.bfloat16)
     pair_out[:, half:] = dot_rows(normed, value_ref[...]).astype(jnp.bfloat16)
@@ -426,22 +425,23 @@
             payload_out[chip, :, lanes] = padded[part * rank : (part + 1) * rank]
 
 
-def split_product(left, weight_ref, mine_out, theirs_out):
-    chips, _, cols = mine_out.shape
-    core = core_index()
+def query_kernel(normed_ref, query_ref, query_out):
+    query_out[...] = dot_chunks(normed_ref[...], query_ref)
+
+
+def side_product(left, weight_ref, side, out):
+    chips, _, cols = out.shape
     for chip in range(chips):
-        at = pl.multiple_of((2 * chip + 1 - core) * cols, cols)
-        theirs_out[chip] = dot(left, weight_ref[:, pl.ds(at, cols)]).astype(jnp.bfloat16)
-        at = pl.multiple_of((2 * chip + core) * cols, cols)
-        mine_out[chip] = dot(left, weight_ref[:, pl.ds(at, cols)])
+        at = pl.multiple_of((2 * chip + side) * cols, cols)
+        out[chip] = dot(left, weight_ref[:, pl.ds(at, cols)]).astype(out.dtype)
 
 
 def attend_kernel(
     query_ref, pair_mine, pair_theirs, owner_ref, got_ref, lift_ref, cosine_ref, sine_ref,
-    reach_ref, output_ref, mine_out, theirs_out, piece_out,
+    reach_ref, output_ref, mixed_out, theirs_out, piece_out,
 ):
     rows, query_cols = query_ref.shape
-    chips, _, cols = mine_out.shape
+    chips, _, cols = theirs_out.shape
     head = HEAD_SIZE
     heads = query_cols // head
     half = head // 2
@@ -476,7 +476,12 @@
     probs = (weights / jnp.sum(weights, axis=-1, keepdims=True)).astype(jnp.bfloat16)
     mixed = dot(probs, value).astype(jnp.bfloat16)
     mixed = jnp.concatenate([mixed[h * rows : (h + 1) * rows] for h in range(heads)], axis=1)
-    split_product(mixed, output_ref, mine_out, theirs_out)
+    mixed_out[...] = mixed
+    side_product(mixed, output_ref, 1 - core_index(), theirs_out)
+
+
+def rest_kernel(mixed_ref, output_ref, mine_out):
+    side_product(mixed_ref[...], output_ref, core_index(), mine_out)
 
 
 def hidden_kernel(
@@ -505,40 +510,58 @@
         payload_out[chip, :, cols:] = padded
 
 
+def down_copies(down_ref, held, sem, side):
+    chips, _, cols = held.shape
+
+    def copy(chip):
+        part = pl.ds(pl.multiple_of((2 * chip + side) * cols, LANES), cols)
+        return pltpu.make_async_copy(down_ref.at[:, part], held.at[chip], sem.at[chip])
+
+    return copy
+
+
 def forward_kernel(
     mine_ref, theirs_ref, gain_ref, lift_ref, gate_ref, up_ref, down_ref,
-    mine_out, theirs_out, scratch, active, held, sem,
+    active_out, theirs_out, held_out, scratch, held, sem, sem_out,
 ):
-    chips = mine_ref.shape[0]
-    cols = mine_ref.shape[2] - LANES
-
-    def down_copy(chip):
-        part = pl.ds(pl.multiple_of(2 * cols * chip, 2 * cols), 2 * cols)
-        return pltpu.make_async_copy(down_ref.at[:, part], held.at[:, part], sem.at[chip])
+    chips, rows, cols = theirs_out.shape
+    core = core_index()
+    rank = lift_ref.shape[0]
+    first = down_copies(down_ref, held, sem, 1 - core)
+    second = down_copies(down_ref, held_out, sem_out, core)
 
     @pl.loop(0, chips)
     def _(chip):
-        down_copy(chip).start()
-
-    rank = lift_ref.shape[0]
+        first(chip).start()
+
+    @pl.loop(0, chips)
+    def _(chip):
+        second(chip).start()
+
     scale = norm_blocks(mine_ref, theirs_ref, gain_ref, scratch, cols)
-    low = jnp.zeros((mine_ref.shape[1], LANES), jnp.float32)
-    for chip in range(mine_ref.shape[0]):
+    low = jnp.zeros((rows, LANES), jnp.float32)
+    for chip in range(chips):
         for ref in (mine_ref, theirs_ref):
             low = low + ref[chip, :, cols:].astype(jnp.float32)
     low = (low * scale)[:, :rank].astype(jnp.bfloat16)
     normed = scratch[...]
     gate = dot_chunks(normed, gate_ref)
     upper = dot_chunks(normed, up_ref) + dot(low, lift_ref[...])
-    active[...] = (gate * jax.nn.sigmoid(gate) * upper).astype(jnp.bfloat16)
-    core = core_index()
+    active_out[...] = (gate * jax.nn.sigmoid(gate) * upper).astype(jnp.bfloat16)
 
     @pl.loop(0, chips)
     def _(chip):
-        down_copy(chip).wait()
-        for side, out in ((1 - core, theirs_out), (core, mine_out)):
-            at = pl.multiple_of((2 * chip + side) * cols, cols)
-            out[chip] = dot(active[...], held[:, pl.ds(at, cols)]).astype(out.dtype)
+        first(chip).wait()
+        theirs_out[chip] = dot(active_out[...], held[chip]).astype(theirs_out.dtype)
+
+    @pl.loop(0, chips)
+    def _(chip):
+        second(chip).wait()
+
+
+def last_kernel(active_ref, held_ref, mine_out):
+    for chip in range(mine_out.shape[0]):
+        mine_out[chip] = dot(active_ref[...], held_ref[chip])
 
 
 def fast_body(
@@ -568,7 +591,6 @@
     heavy = (gate_weight, up_weight, down_weight)
     most = heavy + (query_weight, output_weight)
     rank = adapter_query.shape[1]
-    split_out = (shape((chips, rows, cols), f32), shape((chips, rows, cols), bf16))
     factors = adapter_inputs[0].T
 
     spread_tokens, kept_tokens, gain_one, gain_two, parents = spread(
@@ -584,24 +606,35 @@
     query_lift, up_lift, owner, cosine, sine, reach = tables(
         request_adapter, adapter_place, (adapter_query, adapter_upper), parents, mine
     )
-    query, pair, payload = call(
+    normed, pair, payload = call(
         project_kernel,
         "project",
         (
-            shape((rows, query_weight.shape[1]), f32),
+            shape((rows, width), bf16),
             shape((rows, 2 * key_matrix.shape[1]), bf16),
             shape((chips, rank, cols + rows // rank * LANES), bf16),
         ),
         (mine, theirs, gain_one, owner, factors_theirs),
-        (query_weight, key_matrix.T, value_matrix.T, factors),
+        (key_matrix.T, value_matrix.T, factors),
+    )
+    pair_theirs = partner_2(pair, "tp", 0)
+    (query,) = call(
+        query_kernel,
+        "query",
+        (shape((rows, query_weight.shape[1]), f32),),
+        (normed,),
+        (query_weight,),
         heavy,
-        [VMEM((rows, width), bf16)],
-    )
-    pair_theirs, payload = lax.optimization_barrier((partner_2(pair, "tp", 0), payload))
-    kept, sent, piece = call(
+    )
+    pair_theirs, query, payload = lax.optimization_barrier((pair_theirs, query, payload))
+    mixed, sent, piece = call(
         attend_kernel,
         "attend",
-        (*split_out, shape(payload.shape[1:], bf16)),
+        (
+            shape((rows, query_weight.shape[1]), bf16),
+            shape((chips, rows, cols), bf16),
+            shape(payload.shape[1:], bf16),
+        ),
         (
             query, pair, pair_theirs, owner, exchange(payload, "tp"), query_lift, cosine,
             sine, reach,
@@ -609,7 +642,11 @@
         (output_weight,),
         heavy + (query_weight,),
     )
-    chip_sum = (kept + partner_2(sent, "tp", 0).astype(f32)).astype(bf16)
+    sent_theirs = partner_2(sent, "tp", 0)
+    (kept,) = call(
+        rest_kernel, "rest", (shape((chips, rows, cols), f32),), (mixed,), (output_weight,)
+    )
+    chip_sum = (kept + sent_theirs.astype(f32)).astype(bf16)
     hidden, payload = call(
         hidden_kernel,
         "hidden",
@@ -620,23 +657,32 @@
     )
     mine = exchange(payload, "tp")
     theirs = partner_2(mine, "tp", 0)
-    kept, sent = call(
+    held = shape((chips, down_weight.shape[0], cols), bf16)
+    active, sent, held_mine = call(
         forward_kernel,
         "forward",
-        split_out,
+        (
+            shape((rows, gate_weight.shape[1]), bf16),
+            shape((chips, rows, cols), bf16),
+            held,
+        ),
         (mine, theirs, gain_two, up_lift),
         (gate_weight, up_weight),
         (query_weight, output_weight),
         [
             VMEM((rows, width), bf16),
-            VMEM((rows, gate_weight.shape[1]), bf16),
-            VMEM(down_weight.shape, bf16),
+            VMEM(held.shape, bf16),
+            pltpu.SemaphoreType.DMA((chips,)),
             pltpu.SemaphoreType.DMA((chips,)),
         ],
         far=(down_weight,),
-        limit=18,
-    )
-    chip_sum = (kept + partner_2(sent, "tp", 0).astype(f32)).astype(bf16)
+        limit=10,
+    )
+    sent_theirs = partner_2(sent, "tp", 0)
+    (kept,) = call(
+        last_kernel, "last", (shape((chips, rows, cols), f32),), (active, held_mine)
+    )
+    chip_sum = (kept + sent_theirs.astype(f32)).astype(bf16)
     added = jnp.sum(exchange(chip_sum, "tp").astype(f32), axis=0)
     return (hidden.astype(f32) + added).astype(bf16)
 

time: 92.5 us -> 90 us (0.973)
  waiting for transfers between devices: 5.79 us -> 2.48 us
    ppermute x6, waiting for transfers between devices: 5.79 us -> 2.48 us  [partner_2(): return lax.ppermute(block, axis, route)]
    pallas_call x4 -> x7, Pallas kernels: 15.1 us -> 15.5 us  [call(): pl.pallas_call(run, out_shape=outs, in_specs=[WHOLE] * (len(args) + len(w...]
  transfers between devices with their start and end apart: 6 -> 6, of which waited for: 5 -> 3; matrix products, arithmetic and copies ran while one was open for 0% -> 0% of each run, Pallas kernels for 1% -> 5%
where the time goes in v5:
time: 90 us; the launch traced here: 89.8 us
  blocking collectives  67 us (74%)
  Pallas kernels  17.6 us (20%)
  waiting for transfers between devices  2.48 us (3%)
  starting transfers between devices  0.9 us (1%)
    all_to_all x5, blocking collectives, exchange(): lax.all_to_all(blocks, axis, 0, 0, axis_index_groups=core_groups(axis), t...  67 us
    pallas_call x7, Pallas kernels, call(): pl.pallas_call(run, out_shape=outs, in_specs=[WHOLE] * (len(args) + len(w...  15.5 us
    ppermute x6, waiting for transfers between devices, partner_2(): return lax.ppermute(block, axis, route)  2.48 us
  transfers between devices with their start and end apart: 6, of which 3 were waited for; matrix products, arithmetic and copies ran while one was open for 0% of the time, Pallas kernels for 5%

profile of v5, /device:TPU:0, one launch (start us, length us, event | category | flops | bytes accessed | tf_op | source)
XLA Modules:
  0.0 89.8 jit_solution(2620206327928247366)
XLA Ops:
  0.0 1.2 %spread.1 = (bf16[8,32,512]{2,1,0:T(8,128)(2,1)S(1)}, bf16[32,512]{1,0:T(8,128)(2,1)S(1)}, bf16[64,128]{1,0:T(8,128)(2,1)S(1)}, bf16[64,128]{1,0:T(8,128)(2,1)S(1)}, s32[1,32]{1,0:T(1,128)S(1)}) custom-call(bf16[32,512]{1,0:T(8,128)(2,1)} %refs_0_.1, bf16[64,128]{1,0:T(8,128)(2,1)} %bitcast.20, bf16[64,128]{1,0:T(8,128)(2,1)} %bitcast.21, s32[1,32]{1,0:T(1,128)} %refs_3_.2, ...), custom_call_target="tpu_custom_call" | custom-call | tf_op jit(solution)/shard_map/spread/pallas_call | solution.py:290
  1.2 16.2 %all_to_all.25.after_ref.refs_0_ = bf16[8,32,512]{2,1,0:T(8,128)(2,1)S(1)} all-to-all(bf16[8,32,512]{2,1,0:T(8,128)(2,1)S(1)} %get-tuple-element.32), channel_id=1, replica_groups={{0,2,4,6,8,10,12,14},{1,3,5,7,9,11,13,15},{16,18,20,22,24,26,28,30},{17..., dimensions={0} | all-to-all | bytes 524288 | tf_op jit(solution)/shard_map/all_to_all | solution.py:22
  17.5 0.5 collective-permute-start
  18.6 0.9 %tables.1 = (bf16[16,512]{1,0:T(8,128)(2,1)S(1)}, bf16[16,1024]{1,0:T(8,128)(2,1)S(1)}, s32[8,128]{1,0:T(8,128)S(1)}, f32[32,128]{1,0:T(8,128)S(1)}, f32[32,128]{1,0:T(8,128)S(1)}, /*index=5*/f32[32,32]{1,0:T(8,128)S(1)}) custom-call(s32[1]{0:T(128)S(6)} %copy.17.request_ref, s32[16]{0:T(128)} %place_ref.1, bf16[16,16,512]{2,1,0:T(8,128)(2,1)} %query_ref.1, ...), custom_call_target="tpu_custom_call" | custom-call | tf_op jit(solution)/shard_map/tables/pallas_call | solution.py:341
  19.6 0.2 collective-permute-done.refs_1_
  19.8 1.3 %project.1 = (bf16[32,8192]{1,0:T(8,128)(2,1)S(1)}, bf16[32,128]{1,0:T(8,128)(2,1)S(1)}, bf16[8,16,768]{2,1,0:T(8,128)(2,1)S(1)}) custom-call(bf16[8,32,512]{2,1,0:T(8,128)(2,1)S(1)} %all_to_all.25.after_ref.refs_0_, bf16[8,32,512]{2,1,0:T(8,128)(2,1)S(1)} %collective-permute-done.refs_1_, bf16[64,128]{1,0:T(8,128)(2,1)S(1)} %get-tuple-element.34.refs_2_, ...), custom_call_target="tpu_custom_call" | custom-call | flops 83886080 | bytes 2621440 | tf_op jit(solution)/shard_map/project/pallas_call | solution.py:248
  21.0 0.1 collective-permute-start.2
  21.2 1.5 %query.1.refs_0_ = f32[32,512]{1,0:T(8,128)S(1)} custom-call(bf16[32,8192]{1,0:T(8,128)(2,1)S(1)} %get-tuple-element.39.refs_0_, bf16[8192,512]{1,0:T(8,128)(2,1)S(1)} %copy-done, bf16[8192,1024]{1,0:T(8,128)(2,1)} %refs_4_.7, bf16[8192,1024]{1,0:T(8,128)(2,1)} %refs_5_.5, bf16[1024,8192]{1,0:T(8,128)(2,1)} %refs_6_.5), custom_call_target="tpu_custom_call" | custom-call | flops 268435456 | bytes 8388608 | tf_op jit(solution)/shard_map/query/pallas_call | solution.py:248
  22.7 11.9 %all_to_all.26.refs_4_ = bf16[8,16,768]{2,1,0:T(8,128)(2,1)S(1)} all-to-all(bf16[8,16,768]{2,1,0:T(8,128)(2,1)S(1)} %get-tuple-element.43), channel_id=1, replica_groups={{0,2,4,6,8,10,12,14},{1,3,5,7,9,11,13,15},{16,18,20,22,24,26,28,30},{17..., dimensions={0} | all-to-all | bytes 393216 | tf_op jit(solution)/shard_map/all_to_all | solution.py:22
  34.6 1.4 %attend.1 = (bf16[32,512]{1,0:T(8,128)(2,1)S(1)}, bf16[8,32,512]{2,1,0:T(8,128)(2,1)S(1)}, bf16[16,768]{1,0:T(8,128)(2,1)S(1)}) custom-call(f32[32,512]{1,0:T(8,128)S(1)} %query.1.refs_0_, bf16[32,128]{1,0:T(8,128)(2,1)S(1)} %get-tuple-element.38.refs_1_, bf16[32,128]{1,0:T(8,128)(2,1)S(1)} %collective-permute-done.2.refs_2_, ...), custom_call_target="tpu_custom_call" | custom-call | flops 268435456 | bytes 8388608 | tf_op jit(solution)/shard_map/attend/pallas_call | solution.py:248
  36.0 0.0 collective-permute-start.3
  36.1 0.8 rest.1
  36.9 0.7 collective-permute-done.3
  37.6 0.1 add_convert_fusion.1
  37.7 12.4 %all_to_all.27.refs_0_ = bf16[8,32,512]{2,1,0:T(8,128)(2,1)S(1)} all-to-all(bf16[8,32,512]{2,1,0:T(8,128)(2,1)S(1)} %add_convert_fusion.1), channel_id=1, replica_groups={{0,2,4,6,8,10,12,14},{1,3,5,7,9,11,13,15},{16,18,20,22,24,26,28,30},{17..., dimensions={0} | all-to-all | bytes 524288 | tf_op jit(solution)/shard_map/all_to_all | solution.py:22
  50.1 0.2 hidden.1
  50.3 14.3 %all_to_all.28.refs_0_ = bf16[8,32,640]{2,1,0:T(8,128)(2,1)S(1)} all-to-all(bf16[8,32,640]{2,1,0:T(8,128)(2,1)S(1)} %get-tuple-element.54), channel_id=1, replica_groups={{0,2,4,6,8,10,12,14},{1,3,5,7,9,11,13,15},{16,18,20,22,24,26,28,30},{17..., dimensions={0} | all-to-all | bytes 655360 | tf_op jit(solution)/shard_map/all_to_all | solution.py:22
  64.6 1.6 %collective-permute-done.4.refs_1_ = bf16[8,32,640]{2,1,0:T(8,128)(2,1)S(1)} collective-permute-done((bf16[8,32,640]{2,1,0:T(8,128)(2,1)S(1)}, bf16[8,32,640]{2,1,0:T(8,128)(2,1)S(1)}, u32[]{:S(2)}, u32[]{:S(2)}) %collective-permute-start.4) | collective-permute-done | bytes 327712 | tf_op jit(solution)/shard_map/ppermute | solution.py:72
  66.3 8.7 %forward.1 = (bf16[32,1024]{1,0:T(8,128)(2,1)S(1)}, bf16[8,32,512]{2,1,0:T(8,128)(2,1)S(1)}, bf16[8,1024,512]{2,1,0:T(8,128)(2,1)S(1)}) custom-call(bf16[8,32,640]{2,1,0:T(8,128)(2,1)S(1)} %all_to_all.28.refs_0_, bf16[8,32,640]{2,1,0:T(8,128)(2,1)S(1)} %collective-permute-done.4.refs_1_, bf16[64,128]{1,0:T(8,128)(2,1)S(1)} %get-tuple-element.51.refs_2_, ...), custom_call_target="tpu_custom_call" | custom-call | flops 1610612736 | bytes 50331648 | tf_op jit(solution)/shard_map/forward/pallas_call | solution.py:248
  75.1 0.2 collective-permute-start.5
  75.2 1.5 %last.1 = f32[8,32,512]{2,1,0:T(8,128)S(1)} custom-call(bf16[32,1024]{1,0:T(8,128)(2,1)S(1)} %get-tuple-element.56.refs_0_, bf16[8,1024,512]{2,1,0:T(8,128)(2,1)S(1)} %get-tuple-element.57.refs_1_), custom_call_target="tpu_custom_call" | custom-call | tf_op jit(solution)/shard_map/last/pallas_call | solution.py:248
  76.8 0.1 add_convert_fusion
  76.9 12.2 %all_to_all.29 = bf16[8,32,512]{2,1,0:T(8,128)(2,1)S(1)} all-to-all(bf16[8,32,512]{2,1,0:T(8,128)(2,1)S(1)} %add_convert_fusion), channel_id=1, replica_groups={{0,2,4,6,8,10,12,14},{1,3,5,7,9,11,13,15},{16,18,20,22,24,26,28,30},{17..., dimensions={0} | all-to-all | bytes 524288 | tf_op jit(solution)/shard_map/all_to_all | solution.py:22
  89.1 0.6 add_convert_fusion.2
  (37 shorter events, 0.1 us)
Async XLA Ops:
  0.0 17.5 %copy-start.3 = (bf16[1,8192,32]{1,2,0:T(8,128)(2,1)S(1)}, bf16[1,8192,32]{1,2,0:T(8,128)(2,1)}, u32[]{:S(2)}) copy-start(bf16[1,8192,32]{1,2,0:T(8,128)(2,1)} %param.26) | copy-start | bytes 1572868
  0.0 19.7 %copy-start.1 = (bf16[8192,64]{0,1:T(8,128)(2,1)S(1)}, bf16[8192,64]{0,1:T(8,128)(2,1)}, u32[]{:S(2)}) copy-start(bf16[8192,64]{0,1:T(8,128)(2,1)} %param.20) | copy-start | bytes 3145732
  0.0 19.8 %copy-start.2 = (bf16[8192,64]{0,1:T(8,128)(2,1)S(1)}, bf16[8192,64]{0,1:T(8,128)(2,1)}, u32[]{:S(2)}) copy-start(bf16[8192,64]{0,1:T(8,128)(2,1)} %param.21) | copy-start | bytes 3145732
  0.0 21.2 %copy-start = (bf16[8192,512]{1,0:T(8,128)(2,1)S(1)}, bf16[8192,512]{1,0:T(8,128)(2,1)}, u32[]{:S(2)}) copy-start(bf16[8192,512]{1,0:T(8,128)(2,1)} %refs_7_.3) | copy-start | bytes 25165828
  17.5 2.3 %collective-permute-start.1 = (bf16[1,8192,32]{1,2,0:T(8,128)(2,1)S(1)}, bf16[1,8192,32]{1,2,0:T(8,128)(2,1)S(1)}, u32[]{:S(2)}, u32[]{:S(2)}) collective-permute-start(bf16[1,8192,32]{1,2,0:T(8,128)(2,1)S(1)} %copy-done.3), channel_id=1, source_target_pairs={{0,1},{1,0},{2,3},{3,2},{4,5},{5,4},{6,7},{7,6},{8,9},{9,8},{10,11... | collective-permute-start | bytes 1572872 | tf_op jit(solution)/shard_map/ppermute | solution.py:72
  17.5 2.3 %collective-permute-start = (bf16[8,32,512]{2,1,0:T(8,128)(2,1)S(1)}, bf16[8,32,512]{2,1,0:T(8,128)(2,1)S(1)}, u32[]{:S(2)}, u32[]{:S(2)}) collective-permute-start(bf16[8,32,512]{2,1,0:T(8,128)(2,1)S(1)} %all_to_all.25.after_ref.refs_0_), channel_id=1, source_target_pairs={{0,1},{1,0},{2,3},{3,2},{4,5},{5,4},{6,7},{7,6},{8,9},{9,8},{10,11... | collective-permute-start | bytes 786440 | tf_op jit(solution)/shard_map/ppermute | solution.py:72
  19.8 14.9 %slice-start.8 = ((s8[8388608]{0:T(1024)(128)(4,1)}), s8[4194304]{0:T(1024)(128)(4,1)S(1)}, s32[]{:S(2)}) async-start(s8[8388608]{0:T(1024)(128)(4,1)} %bitcast.14), calls=%async_computation.13 | async-start | bytes 8388608
  21.0 1.7 %collective-permute-start.2 = (bf16[32,128]{1,0:T(8,128)(2,1)S(1)}, bf16[32,128]{1,0:T(8,128)(2,1)S(1)}, u32[]{:S(2)}, u32[]{:S(2)}) collective-permute-start(bf16[32,128]{1,0:T(8,128)(2,1)S(1)} %get-tuple-element.38.refs_1_), channel_id=1, source_target_pairs={{0,1},{1,0},{2,3},{3,2},{4,5},{5,4},{6,7},{7,6},{8,9},{9,8},{10,11... | collective-permute-start | bytes 24584 | tf_op jit(solution)/shard_map/ppermute | solution.py:72
  21.2 13.4 %slice-start.9 = ((s8[8388608]{0:T(1024)(128)(4,1)}), s8[4194304]{0:T(1024)(128)(4,1)S(1)}, s32[]{:S(2)}) async-start(s8[8388608]{0:T(1024)(128)(4,1)} %bitcast.14), calls=%async_computation.14 | async-start | bytes 8388608
  36.0 1.6 %collective-permute-start.3 = (bf16[8,32,512]{2,1,0:T(8,128)(2,1)S(1)}, bf16[8,32,512]{2,1,0:T(8,128)(2,1)S(1)}, u32[]{:S(2)}, u32[]{:S(2)}) collective-permute-start(bf16[8,32,512]{2,1,0:T(8,128)(2,1)S(1)} %get-tuple-element.49), channel_id=1, source_target_pairs={{0,1},{1,0},{2,3},{3,2},{4,5},{5,4},{6,7},{7,6},{8,9},{9,8},{10,11... | collective-permute-start | bytes 786440 | tf_op jit(solution)/shard_map/ppermute | solution.py:72
  36.1 30.2 %slice-start = ((s8[16777216]{0:T(1024)(128)(4,1)}), s8[4194304]{0:T(1024)(128)(4,1)S(1)}, s32[]{:S(2)}) async-start(s8[16777216]{0:T(1024)(128)(4,1)} %bitcast.10), calls=%async_computation.5 | async-start | bytes 8388608
  36.1 30.2 %slice-start.4 = ((s8[16777216]{0:T(1024)(128)(4,1)}), s8[4194304]{0:T(1024)(128)(4,1)S(1)}, s32[]{:S(2)}) async-start(s8[16777216]{0:T(1024)(128)(4,1)} %bitcast.12), calls=%async_computation.9 | async-start | bytes 8388608
  50.1 16.1 %slice-start.1 = ((s8[16777216]{0:T(1024)(128)(4,1)}), s8[4194304]{0:T(1024)(128)(4,1)S(1)}, s32[]{:S(2)}) async-start(s8[16777216]{0:T(1024)(128)(4,1)} %bitcast.10), calls=%async_computation.6 | async-start | bytes 8388608
  50.1 16.1 %slice-start.2 = ((s8[16777216]{0:T(1024)(128)(4,1)}), s8[4194304]{0:T(1024)(128)(4,1)S(1)}, s32[]{:S(2)}) async-start(s8[16777216]{0:T(1024)(128)(4,1)} %bitcast.10), calls=%async_computation.7 | async-start | bytes 8388608
  50.1 16.1 %slice-start.3 = ((s8[16777216]{0:T(1024)(128)(4,1)}), s8[4194304]{0:T(1024)(128)(4,1)S(1)}, s32[]{:S(2)}) async-start(s8[16777216]{0:T(1024)(128)(4,1)} %bitcast.10), calls=%async_computation.8 | async-start | bytes 8388608
  50.1 16.2 %slice-start.5 = ((s8[16777216]{0:T(1024)(128)(4,1)}), s8[4194304]{0:T(1024)(128)(4,1)S(1)}, s32[]{:S(2)}) async-start(s8[16777216]{0:T(1024)(128)(4,1)} %bitcast.12), calls=%async_computation.10 | async-start | bytes 8388608
  50.1 16.2 %slice-start.6 = ((s8[16777216]{0:T(1024)(128)(4,1)}), s8[4194304]{0:T(1024)(128)(4,1)S(1)}, s32[]{:S(2)}) async-start(s8[16777216]{0:T(1024)(128)(4,1)} %bitcast.12), calls=%async_computation.11 | async-start | bytes 8388608
  50.1 16.2 %slice-start.7 = ((s8[16777216]{0:T(1024)(128)(4,1)}), s8[4194304]{0:T(1024)(128)(4,1)S(1)}, s32[]{:S(2)}) async-start(s8[16777216]{0:T(1024)(128)(4,1)} %bitcast.12), calls=%async_computation.12 | async-start | bytes 8388608
  64.6 1.6 %collective-permute-start.4 = (bf16[8,32,640]{2,1,0:T(8,128)(2,1)S(1)}, bf16[8,32,640]{2,1,0:T(8,128)(2,1)S(1)}, u32[]{:S(2)}, u32[]{:S(2)}) collective-permute-start(bf16[8,32,640]{2,1,0:T(8,128)(2,1)S(1)} %all_to_all.28.refs_0_), channel_id=1, source_target_pairs={{0,1},{1,0},{2,3},{3,2},{4,5},{5,4},{6,7},{7,6},{8,9},{9,8},{10,11... | collective-permute-start | bytes 983048 | tf_op jit(solution)/shard_map/ppermute | solution.py:72
  75.1 1.7 %collective-permute-start.5 = (bf16[8,32,512]{2,1,0:T(8,128)(2,1)S(1)}, bf16[8,32,512]{2,1,0:T(8,128)(2,1)S(1)}, u32[]{:S(2)}, u32[]{:S(2)}) collective-permute-start(bf16[8,32,512]{2,1,0:T(8,128)(2,1)S(1)} %get-tuple-element.58), channel_id=1, source_target_pairs={{0,1},{1,0},{2,3},{3,2},{4,5},{5,4},{6,7},{7,6},{8,9},{9,8},{10,11... | collective-permute-start | bytes 786440 | tf_op jit(solution)/shard_map/ppermute | solution.py:72

commit v6 on v5

--- a/solution.py
+++ b/solution.py
@@ -377,18 +377,40 @@
     return jnp.where(flag, mine, theirs), jnp.where(flag, theirs, mine)
 
 
+def fold(low):
+    rows, rank = low.shape
+    padded = jnp.concatenate([low, jnp.zeros((rows, LANES - rank), jnp.float32)], axis=1)
+    return (padded[:rank] + pltpu.roll(padded[rank:], LANES // 2, 1)).astype(jnp.bfloat16)
+
+
+def unfold(folded):
+    rank = folded.shape[0]
+    low = jnp.concatenate([folded, pltpu.roll(folded, LANES // 2, 1)], axis=0)
+    return low[:, :rank]
+
+
+def features(ref, chip, rows, cols):
+    if ref.shape[2] == cols:
+        return ref[chip].astype(jnp.float32)
+    lanes = ref.shape[2]
+    blocks = [ref[chip, j * rows : (j + 1) * rows, :] for j in range(cols // lanes)]
+    return jnp.concatenate(blocks, axis=1).astype(jnp.float32)
+
+
 def norm_blocks(mine_ref, theirs_ref, gain_ref, scratch, cols):
     chips = mine_ref.shape[0]
     first = core_index() == 0
-    squares = jnp.zeros((mine_ref.shape[1], cols), jnp.float32)
+    rows = scratch.shape[0]
+    squares = jnp.zeros((rows, cols), jnp.float32)
     for chip in range(chips):
         for ref in (mine_ref, theirs_ref):
-            wide = ref[chip, :, :cols].astype(jnp.float32)
+            wide = features(ref, chip, rows, cols)
             squares = squares + wide * wide
     mean_sq = jnp.sum(squares, axis=-1, keepdims=True) / (2 * chips * cols)
     scale = lax.rsqrt(mean_sq + EPS)
     for chip in range(chips):
-        pair = in_order(mine_ref[chip, :, :cols], theirs_ref[chip, :, :cols], first)
+        mine = features(mine_ref, chip, rows, cols)
+        pair = in_order(mine, features(theirs_ref, chip, rows, cols), first)
         for side in range(2):
             low = (2 * chip + side) * cols
             gain = gain_block(gain_ref, 2 * chip + side, cols)
@@ -412,17 +434,13 @@
     half = key_ref.shape[0]
     pair_out[:, :half] = dot_rows(normed, key_ref[...]).astype(jnp.bfloat16)
     pair_out[:, half:] = dot_rows(normed, value_ref[...]).astype(jnp.bfloat16)
-    parts = rows // rank
-    padded = jnp.concatenate([low, jnp.zeros((rows, LANES - rank), jnp.float32)], axis=1)
-    padded = padded.astype(jnp.bfloat16)
+    folded = fold(low)
     for chip in range(chips):
         at = pl.multiple_of((2 * chip + core) * cols, cols)
         own = factor_ref[rank:, pl.ds(at, cols)].astype(jnp.float32)
         other = other_ref[rank:, pl.ds(at, cols)].astype(jnp.float32)
         payload_out[chip, :, :cols] = jnp.where(here, own, other).astype(jnp.bfloat16)
-        for part in range(parts):
-            lanes = slice(cols + part * LANES, cols + (part + 1) * LANES)
-            payload_out[chip, :, lanes] = padded[part * rank : (part + 1) * rank]
+        payload_out[chip, :, cols:] = folded
 
 
 def query_kernel(normed_ref, query_ref, query_out):
@@ -445,16 +463,13 @@
     head = HEAD_SIZE
     heads = query_cols // head
     half = head // 2
-    rank = lift_ref.shape[0]
     owner = owner_ref[:1, :1]
     piece = jnp.zeros(got_ref.shape[1:], jnp.float32)
     for chip in range(chips):
         sent = got_ref[chip].astype(jnp.float32)
         piece = piece + jnp.where((owner >> 1) == chip, sent, 0.0)
     piece_out[...] = piece.astype(jnp.bfloat16)
-    low = jnp.concatenate(
-        [piece[:, at : at + LANES] for at in range(cols, piece.shape[1], LANES)], axis=0
-    )
+    low = unfold(piece[:, cols:])
     lane = lax.broadcasted_iota(jnp.int32, (rows, head), 1)
     cosine = cosine_ref[...]
     sine = sine_ref[...]
@@ -466,7 +481,7 @@
     even, odd = in_order(pair_mine[...], pair_theirs[...], first)
     key = rotate(jnp.where(lane < half, even, pltpu.roll(odd, half, 1)))
     value = jnp.where(lane < half, pltpu.roll(even, half, 1), odd).astype(jnp.bfloat16)
-    query = query_ref[...] + dot(low[:, :rank].astype(jnp.bfloat16), lift_ref[...])
+    query = query_ref[...] + dot(low.astype(jnp.bfloat16), lift_ref[...])
     query = query.astype(jnp.bfloat16).astype(jnp.float32)
     stacked = jnp.concatenate(
         [rotate(query[:, h * head : (h + 1) * head]) for h in range(heads)], axis=0
@@ -503,11 +518,12 @@
         gain = jnp.where(device == index, gain_block(gain_ref, index, cols), gain)
     gained = hidden.astype(jnp.float32) * gain
     low = dot_rows(gained.astype(jnp.bfloat16), factor)
-    padded = jnp.concatenate([low, jnp.zeros((rows, LANES - rank), jnp.float32)], axis=1)
-    padded = padded.astype(jnp.bfloat16)
+    folded = fold(low)
     for chip in range(chips):
-        payload_out[chip, :, :cols] = hidden
-        payload_out[chip, :, cols:] = padded
+        for j in range(cols // LANES):
+            part = hidden[:, j * LANES : (j + 1) * LANES]
+            payload_out[chip, j * rows : (j + 1) * rows, :] = part
+        payload_out[chip, -rank:, :] = folded
 
 
 def down_copies(down_ref, held, sem, side):
@@ -539,11 +555,11 @@
         second(chip).start()
 
     scale = norm_blocks(mine_ref, theirs_ref, gain_ref, scratch, cols)
-    low = jnp.zeros((rows, LANES), jnp.float32)
+    folded = jnp.zeros((rank, LANES), jnp.float32)
     for chip in range(chips):
         for ref in (mine_ref, theirs_ref):
-            low = low + ref[chip, :, cols:].astype(jnp.float32)
-    low = (low * scale)[:, :rank].astype(jnp.bfloat16)
+            folded = folded + ref[chip, -rank:, :].astype(jnp.float32)
+    low = (unfold(folded) * scale).astype(jnp.bfloat16)
     normed = scratch[...]
     gate = dot_chunks(normed, gate_ref)
     upper = dot_chunks(normed, up_ref) + dot(low, lift_ref[...])
@@ -587,7 +603,7 @@
     width = query_weight.shape[0]
     shape = jax.ShapeDtypeStruct
     bf16, f32 = jnp.bfloat16, jnp.float32
-    wide = cols + LANES
+    tall = rows * cols // LANES + adapter_query.shape[1]
     heavy = (gate_weight, up_weight, down_weight)
     most = heavy + (query_weight, output_weight)
     rank = adapter_query.shape[1]
@@ -612,7 +628,7 @@
         (
             shape((rows, width), bf16),
             shape((rows, 2 * key_matrix.shape[1]), bf16),
-            shape((chips, rank, cols + rows // rank * LANES), bf16),
+            shape((chips, rank, cols + LANES), bf16),
         ),
         (mine, theirs, gain_one, owner, factors_theirs),
         (key_matrix.T, value_matrix.T, factors),
@@ -650,7 +666,7 @@
     hidden, payload = call(
         hidden_kernel,
         "hidden",
-        (shape((rows, cols), bf16), shape((chips, rows, wide), bf16)),
+        (shape((rows, cols), bf16), shape((chips, tall, LANES), bf16)),
         (exchange(chip_sum, "tp"), kept_tokens, gain_two, piece),
         (),
         most,

time: 90 us -> 88.7 us (0.986)
  blocking collectives: 67 us -> 65.7 us
    all_to_all x5, blocking collectives: 67 us -> 65.7 us  [exchange(): lax.all_to_all(blocks, axis, 0, 0, axis_index_groups=core_groups(axis), t...]
where the time goes in v6:
time: 88.7 us; the launch traced here: 88.4 us
  blocking collectives  65.7 us (74%)
  Pallas kernels  17.6 us (20%)
  waiting for transfers between devices  2.43 us (3%)
  starting transfers between devices  0.9 us (1%)
    all_to_all x5, blocking collectives, exchange(): lax.all_to_all(blocks, axis, 0, 0, axis_index_groups=core_groups(axis), t...  65.7 us
    pallas_call x7, Pallas kernels, call(): pl.pallas_call(run, out_shape=outs, in_specs=[WHOLE] * (len(args) + len(w...  15.5 us
    ppermute x6, waiting for transfers between devices, partner_2(): return lax.ppermute(block, axis, route)  2.43 us
  transfers between devices with their start and end apart: 6, of which 3 were waited for; matrix products, arithmetic and copies ran while one was open for 0% of the time, Pallas kernels for 5%

profile of v6, /device:TPU:0, one launch (start us, length us, event | category | flops | bytes accessed | tf_op | source)
XLA Modules:
  0.0 88.4 jit_solution(3688410311695542486)
XLA Ops:
  0.0 1.2 %spread.1 = (bf16[8,32,512]{2,1,0:T(8,128)(2,1)S(1)}, bf16[32,512]{1,0:T(8,128)(2,1)S(1)}, bf16[64,128]{1,0:T(8,128)(2,1)S(1)}, bf16[64,128]{1,0:T(8,128)(2,1)S(1)}, s32[1,32]{1,0:T(1,128)S(1)}) custom-call(bf16[32,512]{1,0:T(8,128)(2,1)} %refs_0_.1, bf16[64,128]{1,0:T(8,128)(2,1)} %bitcast.20, bf16[64,128]{1,0:T(8,128)(2,1)} %bitcast.21, s32[1,32]{1,0:T(1,128)} %refs_3_.2, ...), custom_call_target="tpu_custom_call" | custom-call | tf_op jit(solution)/shard_map/spread/pallas_call | solution.py:290
  1.2 16.2 %all_to_all.25.after_ref.refs_0_ = bf16[8,32,512]{2,1,0:T(8,128)(2,1)S(1)} all-to-all(bf16[8,32,512]{2,1,0:T(8,128)(2,1)S(1)} %get-tuple-element.32), channel_id=1, replica_groups={{0,2,4,6,8,10,12,14},{1,3,5,7,9,11,13,15},{16,18,20,22,24,26,28,30},{17..., dimensions={0} | all-to-all | bytes 524288 | tf_op jit(solution)/shard_map/all_to_all | solution.py:22
  17.5 0.5 collective-permute-start
  18.6 0.9 %tables.1 = (bf16[16,512]{1,0:T(8,128)(2,1)S(1)}, bf16[16,1024]{1,0:T(8,128)(2,1)S(1)}, s32[8,128]{1,0:T(8,128)S(1)}, f32[32,128]{1,0:T(8,128)S(1)}, f32[32,128]{1,0:T(8,128)S(1)}, /*index=5*/f32[32,32]{1,0:T(8,128)S(1)}) custom-call(s32[1]{0:T(128)S(6)} %copy.17.request_ref, s32[16]{0:T(128)} %place_ref.1, bf16[16,16,512]{2,1,0:T(8,128)(2,1)} %query_ref.1, ...), custom_call_target="tpu_custom_call" | custom-call | tf_op jit(solution)/shard_map/tables/pallas_call | solution.py:341
  19.6 0.2 collective-permute-done.refs_1_
  19.8 1.3 %project.1 = (bf16[32,8192]{1,0:T(8,128)(2,1)S(1)}, bf16[32,128]{1,0:T(8,128)(2,1)S(1)}, bf16[8,16,640]{2,1,0:T(8,128)(2,1)S(1)}) custom-call(bf16[8,32,512]{2,1,0:T(8,128)(2,1)S(1)} %all_to_all.25.after_ref.refs_0_, bf16[8,32,512]{2,1,0:T(8,128)(2,1)S(1)} %collective-permute-done.refs_1_, bf16[64,128]{1,0:T(8,128)(2,1)S(1)} %get-tuple-element.34.refs_2_, ...), custom_call_target="tpu_custom_call" | custom-call | flops 83886080 | bytes 2621440 | tf_op jit(solution)/shard_map/project/pallas_call | solution.py:248
  21.0 0.2 collective-permute-start.2
  21.2 1.5 %query.1.refs_0_ = f32[32,512]{1,0:T(8,128)S(1)} custom-call(bf16[32,8192]{1,0:T(8,128)(2,1)S(1)} %get-tuple-element.39.refs_0_, bf16[8192,512]{1,0:T(8,128)(2,1)S(1)} %copy-done, bf16[8192,1024]{1,0:T(8,128)(2,1)} %refs_4_.7, bf16[8192,1024]{1,0:T(8,128)(2,1)} %refs_5_.5, bf16[1024,8192]{1,0:T(8,128)(2,1)} %refs_6_.5), custom_call_target="tpu_custom_call" | custom-call | flops 268435456 | bytes 8388608 | tf_op jit(solution)/shard_map/query/pallas_call | solution.py:248
  22.7 11.4 %all_to_all.26.refs_4_ = bf16[8,16,640]{2,1,0:T(8,128)(2,1)S(1)} all-to-all(bf16[8,16,640]{2,1,0:T(8,128)(2,1)S(1)} %get-tuple-element.43), channel_id=1, replica_groups={{0,2,4,6,8,10,12,14},{1,3,5,7,9,11,13,15},{16,18,20,22,24,26,28,30},{17..., dimensions={0} | all-to-all | bytes 327680 | tf_op jit(solution)/shard_map/all_to_all | solution.py:22
  34.1 1.5 %attend.1 = (bf16[32,512]{1,0:T(8,128)(2,1)S(1)}, bf16[8,32,512]{2,1,0:T(8,128)(2,1)S(1)}, bf16[16,640]{1,0:T(8,128)(2,1)S(1)}) custom-call(f32[32,512]{1,0:T(8,128)S(1)} %query.1.refs_0_, bf16[32,128]{1,0:T(8,128)(2,1)S(1)} %get-tuple-element.38.refs_1_, bf16[32,128]{1,0:T(8,128)(2,1)S(1)} %collective-permute-done.2.refs_2_, ...), custom_call_target="tpu_custom_call" | custom-call | flops 268435456 | bytes 8388608 | tf_op jit(solution)/shard_map/attend/pallas_call | solution.py:248
  35.6 0.0 collective-permute-start.3
  35.7 0.8 rest.1
  36.5 0.7 collective-permute-done.3
  37.2 0.1 add_convert_fusion.1
  37.2 12.2 %all_to_all.27.refs_0_ = bf16[8,32,512]{2,1,0:T(8,128)(2,1)S(1)} all-to-all(bf16[8,32,512]{2,1,0:T(8,128)(2,1)S(1)} %add_convert_fusion.1), channel_id=1, replica_groups={{0,2,4,6,8,10,12,14},{1,3,5,7,9,11,13,15},{16,18,20,22,24,26,28,30},{17..., dimensions={0} | all-to-all | bytes 524288 | tf_op jit(solution)/shard_map/all_to_all | solution.py:22
  49.5 0.3 hidden.1
  49.8 13.7 %all_to_all.28.refs_0_ = bf16[8,144,128]{2,1,0:T(8,128)(2,1)S(1)} all-to-all(bf16[8,144,128]{2,1,0:T(8,128)(2,1)S(1)} %get-tuple-element.54), channel_id=1, replica_groups={{0,2,4,6,8,10,12,14},{1,3,5,7,9,11,13,15},{16,18,20,22,24,26,28,30},{17..., dimensions={0} | all-to-all | bytes 589824 | tf_op jit(solution)/shard_map/all_to_all | solution.py:22
  63.4 1.6 %collective-permute-done.4.refs_1_ = bf16[8,144,128]{2,1,0:T(8,128)(2,1)S(1)} collective-permute-done((bf16[8,144,128]{2,1,0:T(8,128)(2,1)S(1)}, bf16[8,144,128]{2,1,0:T(8,128)(2,1)S(1)}, u32[]{:S(2)}, u32[]{:S(2)}) %collective-permute-start.4) | collective-permute-done | bytes 294944 | tf_op jit(solution)/shard_map/ppermute | solution.py:72
  65.1 8.6 %forward.1 = (bf16[32,1024]{1,0:T(8,128)(2,1)S(1)}, bf16[8,32,512]{2,1,0:T(8,128)(2,1)S(1)}, bf16[8,1024,512]{2,1,0:T(8,128)(2,1)S(1)}) custom-call(bf16[8,144,128]{2,1,0:T(8,128)(2,1)S(1)} %all_to_all.28.refs_0_, bf16[8,144,128]{2,1,0:T(8,128)(2,1)S(1)} %collective-permute-done.4.refs_1_, bf16[64,128]{1,0:T(8,128)(2,1)S(1)} %get-tuple-element.51.refs_2_, ...), custom_call_target="tpu_custom_call" | custom-call | flops 1610612736 | bytes 50331648 | tf_op jit(solution)/shard_map/forward/pallas_call | solution.py:248
  73.7 0.2 collective-permute-start.5
  73.9 1.5 %last.1 = f32[8,32,512]{2,1,0:T(8,128)S(1)} custom-call(bf16[32,1024]{1,0:T(8,128)(2,1)S(1)} %get-tuple-element.56.refs_0_, bf16[8,1024,512]{2,1,0:T(8,128)(2,1)S(1)} %get-tuple-element.57.refs_1_), custom_call_target="tpu_custom_call" | custom-call | tf_op jit(solution)/shard_map/last/pallas_call | solution.py:248
  75.4 0.1 add_convert_fusion
  75.5 12.2 %all_to_all.29 = bf16[8,32,512]{2,1,0:T(8,128)(2,1)S(1)} all-to-all(bf16[8,32,512]{2,1,0:T(8,128)(2,1)S(1)} %add_convert_fusion), channel_id=1, replica_groups={{0,2,4,6,8,10,12,14},{1,3,5,7,9,11,13,15},{16,18,20,22,24,26,28,30},{17..., dimensions={0} | all-to-all | bytes 524288 | tf_op jit(solution)/shard_map/all_to_all | solution.py:22
  87.7 0.6 add_convert_fusion.2
  (37 shorter events, 0.1 us)
Async XLA Ops:
  0.0 17.5 %copy-start.3 = (bf16[1,8192,32]{1,2,0:T(8,128)(2,1)S(1)}, bf16[1,8192,32]{1,2,0:T(8,128)(2,1)}, u32[]{:S(2)}) copy-start(bf16[1,8192,32]{1,2,0:T(8,128)(2,1)} %param.26) | copy-start | bytes 1572868
  0.0 19.7 %copy-start.1 = (bf16[8192,64]{0,1:T(8,128)(2,1)S(1)}, bf16[8192,64]{0,1:T(8,128)(2,1)}, u32[]{:S(2)}) copy-start(bf16[8192,64]{0,1:T(8,128)(2,1)} %param.20) | copy-start | bytes 3145732
  0.0 19.8 %copy-start.2 = (bf16[8192,64]{0,1:T(8,128)(2,1)S(1)}, bf16[8192,64]{0,1:T(8,128)(2,1)}, u32[]{:S(2)}) copy-start(bf16[8192,64]{0,1:T(8,128)(2,1)} %param.21) | copy-start | bytes 3145732
  0.0 21.2 %copy-start = (bf16[8192,512]{1,0:T(8,128)(2,1)S(1)}, bf16[8192,512]{1,0:T(8,128)(2,1)}, u32[]{:S(2)}) copy-start(bf16[8192,512]{1,0:T(8,128)(2,1)} %refs_7_.3) | copy-start | bytes 25165828
  17.5 2.3 %collective-permute-start.1 = (bf16[1,8192,32]{1,2,0:T(8,128)(2,1)S(1)}, bf16[1,8192,32]{1,2,0:T(8,128)(2,1)S(1)}, u32[]{:S(2)}, u32[]{:S(2)}) collective-permute-start(bf16[1,8192,32]{1,2,0:T(8,128)(2,1)S(1)} %copy-done.3), channel_id=1, source_target_pairs={{0,1},{1,0},{2,3},{3,2},{4,5},{5,4},{6,7},{7,6},{8,9},{9,8},{10,11... | collective-permute-start | bytes 1572872 | tf_op jit(solution)/shard_map/ppermute | solution.py:72
  17.5 2.3 %collective-permute-start = (bf16[8,32,512]{2,1,0:T(8,128)(2,1)S(1)}, bf16[8,32,512]{2,1,0:T(8,128)(2,1)S(1)}, u32[]{:S(2)}, u32[]{:S(2)}) collective-permute-start(bf16[8,32,512]{2,1,0:T(8,128)(2,1)S(1)} %all_to_all.25.after_ref.refs_0_), channel_id=1, source_target_pairs={{0,1},{1,0},{2,3},{3,2},{4,5},{5,4},{6,7},{7,6},{8,9},{9,8},{10,11... | collective-permute-start | bytes 786440 | tf_op jit(solution)/shard_map/ppermute | solution.py:72
  19.8 14.4 %slice-start.8 = ((s8[8388608]{0:T(1024)(128)(4,1)}), s8[4194304]{0:T(1024)(128)(4,1)S(1)}, s32[]{:S(2)}) async-start(s8[8388608]{0:T(1024)(128)(4,1)} %bitcast.14), calls=%async_computation.13 | async-start | bytes 8388608
  21.0 1.7 %collective-permute-start.2 = (bf16[32,128]{1,0:T(8,128)(2,1)S(1)}, bf16[32,128]{1,0:T(8,128)(2,1)S(1)}, u32[]{:S(2)}, u32[]{:S(2)}) collective-permute-start(bf16[32,128]{1,0:T(8,128)(2,1)S(1)} %get-tuple-element.38.refs_1_), channel_id=1, source_target_pairs={{0,1},{1,0},{2,3},{3,2},{4,5},{5,4},{6,7},{7,6},{8,9},{9,8},{10,11... | collective-permute-start | bytes 24584 | tf_op jit(solution)/shard_map/ppermute | solution.py:72
  21.2 12.9 %slice-start.9 = ((s8[8388608]{0:T(1024)(128)(4,1)}), s8[4194304]{0:T(1024)(128)(4,1)S(1)}, s32[]{:S(2)}) async-start(s8[8388608]{0:T(1024)(128)(4,1)} %bitcast.14), calls=%async_computation.14 | async-start | bytes 8388608
  35.6 1.6 %collective-permute-start.3 = (bf16[8,32,512]{2,1,0:T(8,128)(2,1)S(1)}, bf16[8,32,512]{2,1,0:T(8,128)(2,1)S(1)}, u32[]{:S(2)}, u32[]{:S(2)}) collective-permute-start(bf16[8,32,512]{2,1,0:T(8,128)(2,1)S(1)} %get-tuple-element.49), channel_id=1, source_target_pairs={{0,1},{1,0},{2,3},{3,2},{4,5},{5,4},{6,7},{7,6},{8,9},{9,8},{10,11... | collective-permute-start | bytes 786440 | tf_op jit(solution)/shard_map/ppermute | solution.py:72
  35.6 29.4 %slice-start = ((s8[16777216]{0:T(1024)(128)(4,1)}), s8[4194304]{0:T(1024)(128)(4,1)S(1)}, s32[]{:S(2)}) async-start(s8[16777216]{0:T(1024)(128)(4,1)} %bitcast.10), calls=%async_computation.5 | async-start | bytes 8388608
  35.7 29.4 %slice-start.4 = ((s8[16777216]{0:T(1024)(128)(4,1)}), s8[4194304]{0:T(1024)(128)(4,1)S(1)}, s32[]{:S(2)}) async-start(s8[16777216]{0:T(1024)(128)(4,1)} %bitcast.12), calls=%async_computation.9 | async-start | bytes 8388608
  49.5 15.6 %slice-start.1 = ((s8[16777216]{0:T(1024)(128)(4,1)}), s8[4194304]{0:T(1024)(128)(4,1)S(1)}, s32[]{:S(2)}) async-start(s8[16777216]{0:T(1024)(128)(4,1)} %bitcast.10), calls=%async_computation.6 | async-start | bytes 8388608
  49.5 15.6 %slice-start.2 = ((s8[16777216]{0:T(1024)(128)(4,1)}), s8[4194304]{0:T(1024)(128)(4,1)S(1)}, s32[]{:S(2)}) async-start(s8[16777216]{0:T(1024)(128)(4,1)} %bitcast.10), calls=%async_computation.7 | async-start | bytes 8388608
  49.5 15.6 %slice-start.3 = ((s8[16777216]{0:T(1024)(128)(4,1)}), s8[4194304]{0:T(1024)(128)(4,1)S(1)}, s32[]{:S(2)}) async-start(s8[16777216]{0:T(1024)(128)(4,1)} %bitcast.10), calls=%async_computation.8 | async-start | bytes 8388608
  49.5 15.6 %slice-start.5 = ((s8[16777216]{0:T(1024)(128)(4,1)}), s8[4194304]{0:T(1024)(128)(4,1)S(1)}, s32[]{:S(2)}) async-start(s8[16777216]{0:T(1024)(128)(4,1)} %bitcast.12), calls=%async_computation.10 | async-start | bytes 8388608
  49.5 15.6 %slice-start.6 = ((s8[16777216]{0:T(1024)(128)(4,1)}), s8[4194304]{0:T(1024)(128)(4,1)S(1)}, s32[]{:S(2)}) async-start(s8[16777216]{0:T(1024)(128)(4,1)} %bitcast.12), calls=%async_computation.11 | async-start | bytes 8388608
  49.5 15.6 %slice-start.7 = ((s8[16777216]{0:T(1024)(128)(4,1)}), s8[4194304]{0:T(1024)(128)(4,1)S(1)}, s32[]{:S(2)}) async-start(s8[16777216]{0:T(1024)(128)(4,1)} %bitcast.12), calls=%async_computation.12 | async-start | bytes 8388608
  63.4 1.6 %collective-permute-start.4 = (bf16[8,144,128]{2,1,0:T(8,128)(2,1)S(1)}, bf16[8,144,128]{2,1,0:T(8,128)(2,1)S(1)}, u32[]{:S(2)}, u32[]{:S(2)}) collective-permute-start(bf16[8,144,128]{2,1,0:T(8,128)(2,1)S(1)} %all_to_all.28.refs_0_), channel_id=1, source_target_pairs={{0,1},{1,0},{2,3},{3,2},{4,5},{5,4},{6,7},{7,6},{8,9},{9,8},{10,11... | collective-permute-start | bytes 884744 | tf_op jit(solution)/shard_map/ppermute | solution.py:72
  73.7 1.7 %collective-permute-start.5 = (bf16[8,32,512]{2,1,0:T(8,128)(2,1)S(1)}, bf16[8,32,512]{2,1,0:T(8,128)(2,1)S(1)}, u32[]{:S(2)}, u32[]{:S(2)}) collective-permute-start(bf16[8,32,512]{2,1,0:T(8,128)(2,1)S(1)} %get-tuple-element.58), channel_id=1, source_target_pairs={{0,1},{1,0},{2,3},{3,2},{4,5},{5,4},{6,7},{7,6},{8,9},{9,8},{10,11... | collective-permute-start | bytes 786440 | tf_op jit(solution)/shard_map/ppermute | solution.py:72

commit v7 on v6

--- a/solution.py
+++ b/solution.py
@@ -526,53 +526,99 @@
         payload_out[chip, -rank:, :] = folded
 
 
-def down_copies(down_ref, held, sem, side):
-    chips, _, cols = held.shape
-
-    def copy(chip):
-        part = pl.ds(pl.multiple_of((2 * chip + side) * cols, LANES), cols)
-        return pltpu.make_async_copy(down_ref.at[:, part], held.at[chip], sem.at[chip])
+def down_copies(down_ref, held, sem, side, start=0):
+    cols = held.shape[2]
+
+    def copy(k):
+        part = pl.ds(pl.multiple_of((2 * (k + start) + side) * cols, LANES), cols)
+        return pltpu.make_async_copy(down_ref.at[:, part], held.at[k], sem.at[k])
 
     return copy
 
 
+def half_products(block_ref, gain_ref, gate_ref, up_ref, side, rows, cols):
+    gate = up = None
+    for chip in range(block_ref.shape[0]):
+        gain = jnp.where(
+            side == 0, gain_block(gain_ref, 2 * chip, cols), gain_block(gain_ref, 2 * chip + 1, cols)
+        )
+        left = (features(block_ref, chip, rows, cols) * gain).astype(jnp.bfloat16)
+        part = pl.ds(pl.multiple_of((2 * chip + side) * cols, cols), cols)
+        gate_part = dot(left, gate_ref[part, :])
+        up_part = dot(left, up_ref[part, :])
+        gate = gate_part if gate is None else gate + gate_part
+        up = up_part if up is None else up + up_part
+    return gate, up
+
+
+def near_kernel(
+    mine_ref, gain_ref, gate_ref, up_ref, down_ref, gate_out, up_out, held_out, sem
+):
+    core = core_index()
+    count, _, cols = held_out.shape
+    copy = down_copies(down_ref, held_out, sem, 1 - core)
+
+    @pl.loop(0, count)
+    def _(k):
+        copy(k).start()
+
+    gate, up = half_products(
+        mine_ref, gain_ref, gate_ref, up_ref, core, gate_out.shape[0], cols
+    )
+    gate_out[...] = gate
+    up_out[...] = up
+
+    @pl.loop(0, count)
+    def _(k):
+        copy(k).wait()
+
+
 def forward_kernel(
-    mine_ref, theirs_ref, gain_ref, lift_ref, gate_ref, up_ref, down_ref,
-    active_out, theirs_out, held_out, scratch, held, sem, sem_out,
+    mine_ref, theirs_ref, gain_ref, lift_ref, gate_part, up_part, early_ref, gate_ref, up_ref,
+    down_ref, active_out, theirs_out, held_out, held, sem, sem_out,
 ):
     chips, rows, cols = theirs_out.shape
     core = core_index()
     rank = lift_ref.shape[0]
-    first = down_copies(down_ref, held, sem, 1 - core)
+    early = early_ref.shape[0]
+    first = down_copies(down_ref, held, sem, 1 - core, early)
     second = down_copies(down_ref, held_out, sem_out, core)
 
+    @pl.loop(0, chips - early)
+    def _(k):
+        first(k).start()
+
     @pl.loop(0, chips)
-    def _(chip):
-        first(chip).start()
-
-    @pl.loop(0, chips)
-    def _(chip):
-        second(chip).start()
-
-    scale = norm_blocks(mine_ref, theirs_ref, gain_ref, scratch, cols)
+    def _(k):
+        second(k).start()
+
+    gate, up = half_products(theirs_ref, gain_ref, gate_ref, up_ref, 1 - core, rows, cols)
+    squares = jnp.zeros((rows, cols), jnp.float32)
     folded = jnp.zeros((rank, LANES), jnp.float32)
     for chip in range(chips):
         for ref in (mine_ref, theirs_ref):
+            wide = features(ref, chip, rows, cols)
+            squares = squares + wide * wide
             folded = folded + ref[chip, -rank:, :].astype(jnp.float32)
+    mean_sq = jnp.sum(squares, axis=-1, keepdims=True) / (2 * chips * cols)
+    scale = lax.rsqrt(mean_sq + EPS)
     low = (unfold(folded) * scale).astype(jnp.bfloat16)
-    normed = scratch[...]
-    gate = dot_chunks(normed, gate_ref)
-    upper = dot_chunks(normed, up_ref) + dot(low, lift_ref[...])
+    gate = (gate + gate_part[...]) * scale
+    upper = (up + up_part[...]) * scale + dot(low, lift_ref[...])
     active_out[...] = (gate * jax.nn.sigmoid(gate) * upper).astype(jnp.bfloat16)
 
+    @pl.loop(0, early)
+    def _(k):
+        theirs_out[k] = dot(active_out[...], early_ref[k]).astype(theirs_out.dtype)
+
+    @pl.loop(0, chips - early)
+    def _(k):
+        first(k).wait()
+        theirs_out[k + early] = dot(active_out[...], held[k]).astype(theirs_out.dtype)
+
     @pl.loop(0, chips)
-    def _(chip):
-        first(chip).wait()
-        theirs_out[chip] = dot(active_out[...], held[chip]).astype(theirs_out.dtype)
-
-    @pl.loop(0, chips)
-    def _(chip):
-        second(chip).wait()
+    def _(k):
+        second(k).wait()
 
 
 def last_kernel(active_ref, held_ref, mine_out):
@@ -674,25 +720,33 @@
     mine = exchange(payload, "tp")
     theirs = partner_2(mine, "tp", 0)
     held = shape((chips, down_weight.shape[0], cols), bf16)
+    half = chips // 2
+    part = shape((rows, gate_weight.shape[1]), f32)
+    gate_part, up_part, early = call(
+        near_kernel,
+        "near",
+        (part, part, shape((half, *held.shape[1:]), bf16)),
+        (mine, gain_two),
+        (gate_weight, up_weight),
+        (),
+        [pltpu.SemaphoreType.DMA((half,))],
+        far=(down_weight,),
+        limit=8,
+    )
     active, sent, held_mine = call(
         forward_kernel,
         "forward",
-        (
-            shape((rows, gate_weight.shape[1]), bf16),
-            shape((chips, rows, cols), bf16),
-            held,
-        ),
-        (mine, theirs, gain_two, up_lift),
+        (shape(part.shape, bf16), shape((chips, rows, cols), bf16), held),
+        (mine, theirs, gain_two, up_lift, gate_part, up_part, early),
         (gate_weight, up_weight),
-        (query_weight, output_weight),
+        (),
         [
-            VMEM((rows, width), bf16),
-            VMEM(held.shape, bf16),
-            pltpu.SemaphoreType.DMA((chips,)),
+            VMEM((chips - half, *held.shape[1:]), bf16),
+            pltpu.SemaphoreType.DMA((chips - half,)),
             pltpu.SemaphoreType.DMA((chips,)),
         ],
         far=(down_weight,),
-        limit=10,
+        limit=8,
     )
     sent_theirs = partner_2(sent, "tp", 0)
     (kept,) = call(

time: 88.7 us -> 86.9 us (0.980)
  waiting for transfers between devices: 2.43 us -> 0.88 us
    ppermute x6, waiting for transfers between devices: 2.43 us -> 0.88 us  [partner_2(): return lax.ppermute(block, axis, route)]
    pallas_call x7 -> x8, Pallas kernels: 15.5 us -> 15.6 us  [call(): pl.pallas_call(run, out_shape=outs, in_specs=[WHOLE] * (len(args) + len(w...]
  transfers between devices with their start and end apart: 6 -> 6, of which waited for: 3 -> 2; matrix products, arithmetic and copies ran while one was open for 0% -> 0% of each run, Pallas kernels for 5% -> 9%
where the time goes in v7:
time: 86.9 us; the launch traced here: 86.6 us
  blocking collectives  65.1 us (75%)
  Pallas kernels  17.7 us (20%)
  starting transfers between devices  1.27 us (1%)
  waiting for transfers between devices  0.88 us (1%)
    all_to_all x5, blocking collectives, exchange(): lax.all_to_all(blocks, axis, 0, 0, axis_index_groups=core_groups(axis), t...  65.1 us
    pallas_call x8, Pallas kernels, call(): pl.pallas_call(run, out_shape=outs, in_specs=[WHOLE] * (len(args) + len(w...  15.6 us
  transfers between devices with their start and end apart: 6, of which 2 were waited for; matrix products, arithmetic and copies ran while one was open for 0% of the time, Pallas kernels for 9%

profile of v7, /device:TPU:0, one launch (start us, length us, event | category | flops | bytes accessed | tf_op | source)
XLA Modules:
  0.0 86.6 jit_solution(7696242162504955710)
XLA Ops:
  0.0 1.2 %spread.1 = (bf16[8,32,512]{2,1,0:T(8,128)(2,1)S(1)}, bf16[32,512]{1,0:T(8,128)(2,1)S(1)}, bf16[64,128]{1,0:T(8,128)(2,1)S(1)}, bf16[64,128]{1,0:T(8,128)(2,1)S(1)}, s32[1,32]{1,0:T(1,128)S(1)}) custom-call(bf16[32,512]{1,0:T(8,128)(2,1)} %refs_0_.1, bf16[64,128]{1,0:T(8,128)(2,1)} %bitcast.22, bf16[64,128]{1,0:T(8,128)(2,1)} %bitcast.23, s32[1,32]{1,0:T(1,128)} %refs_3_.3, ...), custom_call_target="tpu_custom_call" | custom-call | tf_op jit(solution)/shard_map/spread/pallas_call | solution.py:290
  1.2 16.2 %all_to_all.25.after_ref.refs_0_ = bf16[8,32,512]{2,1,0:T(8,128)(2,1)S(1)} all-to-all(bf16[8,32,512]{2,1,0:T(8,128)(2,1)S(1)} %get-tuple-element.35), channel_id=1, replica_groups={{0,2,4,6,8,10,12,14},{1,3,5,7,9,11,13,15},{16,18,20,22,24,26,28,30},{17..., dimensions={0} | all-to-all | bytes 524288 | tf_op jit(solution)/shard_map/all_to_all | solution.py:22
  17.5 0.5 collective-permute-start
  18.6 0.9 %tables.1 = (bf16[16,512]{1,0:T(8,128)(2,1)S(1)}, bf16[16,1024]{1,0:T(8,128)(2,1)S(1)}, s32[8,128]{1,0:T(8,128)S(1)}, f32[32,128]{1,0:T(8,128)S(1)}, f32[32,128]{1,0:T(8,128)S(1)}, /*index=5*/f32[32,32]{1,0:T(8,128)S(1)}) custom-call(s32[1]{0:T(128)S(6)} %copy.17.request_ref, s32[16]{0:T(128)} %place_ref.1, bf16[16,16,512]{2,1,0:T(8,128)(2,1)} %query_ref.1, ...), custom_call_target="tpu_custom_call" | custom-call | tf_op jit(solution)/shard_map/tables/pallas_call | solution.py:341
  19.6 0.2 collective-permute-done.refs_1_
  19.8 1.3 %project.1 = (bf16[32,8192]{1,0:T(8,128)(2,1)S(1)}, bf16[32,128]{1,0:T(8,128)(2,1)S(1)}, bf16[8,16,640]{2,1,0:T(8,128)(2,1)S(1)}) custom-call(bf16[8,32,512]{2,1,0:T(8,128)(2,1)S(1)} %all_to_all.25.after_ref.refs_0_, bf16[8,32,512]{2,1,0:T(8,128)(2,1)S(1)} %collective-permute-done.refs_1_, bf16[64,128]{1,0:T(8,128)(2,1)S(1)} %get-tuple-element.37.refs_2_, ...), custom_call_target="tpu_custom_call" | custom-call | flops 83886080 | bytes 2621440 | tf_op jit(solution)/shard_map/project/pallas_call | solution.py:248
  21.0 0.2 collective-permute-start.2
  21.2 1.5 %query.1.refs_0_ = f32[32,512]{1,0:T(8,128)S(1)} custom-call(bf16[32,8192]{1,0:T(8,128)(2,1)S(1)} %get-tuple-element.42.refs_0_, bf16[8192,512]{1,0:T(8,128)(2,1)S(1)} %bitcast.17, bf16[8192,1024]{1,0:T(8,128)(2,1)} %refs_7_.3, bf16[8192,1024]{1,0:T(8,128)(2,1)} %refs_8_.3, bf16[1024,8192]{1,0:T(8,128)(2,1)} %refs_9_.3), custom_call_target="tpu_custom_call" | custom-call | flops 268435456 | bytes 8388608 | tf_op jit(solution)/shard_map/query/pallas_call | solution.py:248
  22.7 11.4 %all_to_all.26.refs_4_ = bf16[8,16,640]{2,1,0:T(8,128)(2,1)S(1)} all-to-all(bf16[8,16,640]{2,1,0:T(8,128)(2,1)S(1)} %get-tuple-element.46), channel_id=1, replica_groups={{0,2,4,6,8,10,12,14},{1,3,5,7,9,11,13,15},{16,18,20,22,24,26,28,30},{17..., dimensions={0} | all-to-all | bytes 327680 | tf_op jit(solution)/shard_map/all_to_all | solution.py:22
  34.1 1.5 %attend.1 = (bf16[32,512]{1,0:T(8,128)(2,1)S(1)}, bf16[8,32,512]{2,1,0:T(8,128)(2,1)S(1)}, bf16[16,640]{1,0:T(8,128)(2,1)S(1)}) custom-call(f32[32,512]{1,0:T(8,128)S(1)} %query.1.refs_0_, bf16[32,128]{1,0:T(8,128)(2,1)S(1)} %get-tuple-element.41.refs_1_, bf16[32,128]{1,0:T(8,128)(2,1)S(1)} %collective-permute-done.2.refs_2_, ...), custom_call_target="tpu_custom_call" | custom-call | flops 268435456 | bytes 8388608 | tf_op jit(solution)/shard_map/attend/pallas_call | solution.py:248
  35.6 0.0 collective-permute-start.3
  35.6 0.8 rest.1
  36.5 0.7 collective-permute-done.3
  37.2 0.1 add_convert_fusion.1
  37.2 11.9 %all_to_all.27.refs_0_ = bf16[8,32,512]{2,1,0:T(8,128)(2,1)S(1)} all-to-all(bf16[8,32,512]{2,1,0:T(8,128)(2,1)S(1)} %add_convert_fusion.1), channel_id=1, replica_groups={{0,2,4,6,8,10,12,14},{1,3,5,7,9,11,13,15},{16,18,20,22,24,26,28,30},{17..., dimensions={0} | all-to-all | bytes 524288 | tf_op jit(solution)/shard_map/all_to_all | solution.py:22
  49.3 0.3 hidden.1
  49.5 13.7 %all_to_all.28.refs_0_ = bf16[8,144,128]{2,1,0:T(8,128)(2,1)S(1)} all-to-all(bf16[8,144,128]{2,1,0:T(8,128)(2,1)S(1)} %get-tuple-element.57), channel_id=1, replica_groups={{0,2,4,6,8,10,12,14},{1,3,5,7,9,11,13,15},{16,18,20,22,24,26,28,30},{17..., dimensions={0} | all-to-all | bytes 589824 | tf_op jit(solution)/shard_map/all_to_all | solution.py:22
  63.3 3.1 %near.1 = (f32[32,1024]{1,0:T(8,128)S(1)}, f32[32,1024]{1,0:T(8,128)S(1)}, bf16[4,1024,512]{2,1,0:T(8,128)(2,1)S(1)}) custom-call(bf16[8,144,128]{2,1,0:T(8,128)(2,1)S(1)} %all_to_all.28.refs_0_, bf16[64,128]{1,0:T(8,128)(2,1)S(1)} %get-tuple-element.54.refs_2_.refs_1_, bf16[8192,1024]{1,0:T(8,128)(2,1)S(1)} %bitcast.11, bf16[8192,1024]{1,0:T(8,128)(2,1)S(1)} %bitcast.13, ...), custom_call_target="tpu_custom_call" | custom-call | flops 1610612736 | bytes 50331648 | tf_op jit(solution)/shard_map/near/pallas_call | solution.py:248
  66.4 5.6 %forward.1 = (bf16[32,1024]{1,0:T(8,128)(2,1)S(1)}, bf16[8,32,512]{2,1,0:T(8,128)(2,1)S(1)}, bf16[8,1024,512]{2,1,0:T(8,128)(2,1)S(1)}) custom-call(bf16[8,144,128]{2,1,0:T(8,128)(2,1)S(1)} %all_to_all.28.refs_0_, bf16[8,144,128]{2,1,0:T(8,128)(2,1)S(1)} %collective-permute-done.4.refs_1_, bf16[64,128]{1,0:T(8,128)(2,1)S(1)} %get-tuple-element.54.refs_2_.refs_1_, ...), custom_call_target="tpu_custom_call" | custom-call | flops 1610612736 | bytes 50331648 | tf_op jit(solution)/shard_map/forward/pallas_call | solution.py:248
  72.0 0.6 collective-permute-start.5
  72.5 1.5 %last.1 = f32[8,32,512]{2,1,0:T(8,128)S(1)} custom-call(bf16[32,1024]{1,0:T(8,128)(2,1)S(1)} %get-tuple-element.62.refs_0_, bf16[8,1024,512]{2,1,0:T(8,128)(2,1)S(1)} %get-tuple-element.63.refs_1_), custom_call_target="tpu_custom_call" | custom-call | tf_op jit(solution)/shard_map/last/pallas_call | solution.py:248
  74.1 0.1 add_convert_fusion
  74.2 11.8 %all_to_all.29 = bf16[8,32,512]{2,1,0:T(8,128)(2,1)S(1)} all-to-all(bf16[8,32,512]{2,1,0:T(8,128)(2,1)S(1)} %add_convert_fusion), channel_id=1, replica_groups={{0,2,4,6,8,10,12,14},{1,3,5,7,9,11,13,15},{16,18,20,22,24,26,28,30},{17..., dimensions={0} | all-to-all | bytes 524288 | tf_op jit(solution)/shard_map/all_to_all | solution.py:22
  86.0 0.6 add_convert_fusion.2
  (41 shorter events, 0.1 us)
Async XLA Ops:
  0.0 21.2 %slice-start.10 = ((s8[8388608]{0:T(1024)(128)(4,1)}), s8[4194304]{0:T(1024)(128)(4,1)S(1)}, s32[]{:S(2)}) async-start(s8[8388608]{0:T(1024)(128)(4,1)} %bitcast.16), calls=%async_computation.15 | async-start | bytes 8388608
  0.0 17.5 %copy-start.2 = (bf16[1,8192,32]{1,2,0:T(8,128)(2,1)S(1)}, bf16[1,8192,32]{1,2,0:T(8,128)(2,1)}, u32[]{:S(2)}) copy-start(bf16[1,8192,32]{1,2,0:T(8,128)(2,1)} %param.26) | copy-start | bytes 1572868
  0.0 19.8 %copy-start = (bf16[8192,64]{0,1:T(8,128)(2,1)S(1)}, bf16[8192,64]{0,1:T(8,128)(2,1)}, u32[]{:S(2)}) copy-start(bf16[8192,64]{0,1:T(8,128)(2,1)} %param.20) | copy-start | bytes 3145732
  0.0 19.8 %copy-start.1 = (bf16[8192,64]{0,1:T(8,128)(2,1)S(1)}, bf16[8192,64]{0,1:T(8,128)(2,1)}, u32[]{:S(2)}) copy-start(bf16[8192,64]{0,1:T(8,128)(2,1)} %param.21) | copy-start | bytes 3145732
  0.0 21.2 %slice-start.11 = ((s8[8388608]{0:T(1024)(128)(4,1)}), s8[4194304]{0:T(1024)(128)(4,1)S(1)}, s32[]{:S(2)}) async-start(s8[8388608]{0:T(1024)(128)(4,1)} %bitcast.16), calls=%async_computation.16 | async-start | bytes 8388608
  17.5 2.3 %collective-permute-start.1 = (bf16[1,8192,32]{1,2,0:T(8,128)(2,1)S(1)}, bf16[1,8192,32]{1,2,0:T(8,128)(2,1)S(1)}, u32[]{:S(2)}, u32[]{:S(2)}) collective-permute-start(bf16[1,8192,32]{1,2,0:T(8,128)(2,1)S(1)} %copy-done.2), channel_id=1, source_target_pairs={{0,1},{1,0},{2,3},{3,2},{4,5},{5,4},{6,7},{7,6},{8,9},{9,8},{10,11... | collective-permute-start | bytes 1572872 | tf_op jit(solution)/shard_map/ppermute | solution.py:72
  17.5 2.3 %collective-permute-start = (bf16[8,32,512]{2,1,0:T(8,128)(2,1)S(1)}, bf16[8,32,512]{2,1,0:T(8,128)(2,1)S(1)}, u32[]{:S(2)}, u32[]{:S(2)}) collective-permute-start(bf16[8,32,512]{2,1,0:T(8,128)(2,1)S(1)} %all_to_all.25.after_ref.refs_0_), channel_id=1, source_target_pairs={{0,1},{1,0},{2,3},{3,2},{4,5},{5,4},{6,7},{7,6},{8,9},{9,8},{10,11... | collective-permute-start | bytes 786440 | tf_op jit(solution)/shard_map/ppermute | solution.py:72
  19.8 14.4 %slice-start.8 = ((s8[8388608]{0:T(1024)(128)(4,1)}), s8[4194304]{0:T(1024)(128)(4,1)S(1)}, s32[]{:S(2)}) async-start(s8[8388608]{0:T(1024)(128)(4,1)} %bitcast.14), calls=%async_computation.13 | async-start | bytes 8388608
  21.0 1.7 %collective-permute-start.2 = (bf16[32,128]{1,0:T(8,128)(2,1)S(1)}, bf16[32,128]{1,0:T(8,128)(2,1)S(1)}, u32[]{:S(2)}, u32[]{:S(2)}) collective-permute-start(bf16[32,128]{1,0:T(8,128)(2,1)S(1)} %get-tuple-element.41.refs_1_), channel_id=1, source_target_pairs={{0,1},{1,0},{2,3},{3,2},{4,5},{5,4},{6,7},{7,6},{8,9},{9,8},{10,11... | collective-permute-start | bytes 24584 | tf_op jit(solution)/shard_map/ppermute | solution.py:72
  21.2 12.9 %slice-start.9 = ((s8[8388608]{0:T(1024)(128)(4,1)}), s8[4194304]{0:T(1024)(128)(4,1)S(1)}, s32[]{:S(2)}) async-start(s8[8388608]{0:T(1024)(128)(4,1)} %bitcast.14), calls=%async_computation.14 | async-start | bytes 8388608
  35.6 1.6 %collective-permute-start.3 = (bf16[8,32,512]{2,1,0:T(8,128)(2,1)S(1)}, bf16[8,32,512]{2,1,0:T(8,128)(2,1)S(1)}, u32[]{:S(2)}, u32[]{:S(2)}) collective-permute-start(bf16[8,32,512]{2,1,0:T(8,128)(2,1)S(1)} %get-tuple-element.52), channel_id=1, source_target_pairs={{0,1},{1,0},{2,3},{3,2},{4,5},{5,4},{6,7},{7,6},{8,9},{9,8},{10,11... | collective-permute-start | bytes 786440 | tf_op jit(solution)/shard_map/ppermute | solution.py:72
  49.2 14.0 %slice-start = ((s8[16777216]{0:T(1024)(128)(4,1)}), s8[4194304]{0:T(1024)(128)(4,1)S(1)}, s32[]{:S(2)}) async-start(s8[16777216]{0:T(1024)(128)(4,1)} %bitcast.10), calls=%async_computation.5 | async-start | bytes 8388608
  49.2 14.0 %slice-start.4 = ((s8[16777216]{0:T(1024)(128)(4,1)}), s8[4194304]{0:T(1024)(128)(4,1)S(1)}, s32[]{:S(2)}) async-start(s8[16777216]{0:T(1024)(128)(4,1)} %bitcast.12), calls=%async_computation.9 | async-start | bytes 8388608
  49.2 14.0 %slice-start.1 = ((s8[16777216]{0:T(1024)(128)(4,1)}), s8[4194304]{0:T(1024)(128)(4,1)S(1)}, s32[]{:S(2)}) async-start(s8[16777216]{0:T(1024)(128)(4,1)} %bitcast.10), calls=%async_computation.6 | async-start | bytes 8388608
  49.2 14.0 %slice-start.2 = ((s8[16777216]{0:T(1024)(128)(4,1)}), s8[4194304]{0:T(1024)(128)(4,1)S(1)}, s32[]{:S(2)}) async-start(s8[16777216]{0:T(1024)(128)(4,1)} %bitcast.10), calls=%async_computation.7 | async-start | bytes 8388608
  49.2 14.0 %slice-start.3 = ((s8[16777216]{0:T(1024)(128)(4,1)}), s8[4194304]{0:T(1024)(128)(4,1)S(1)}, s32[]{:S(2)}) async-start(s8[16777216]{0:T(1024)(128)(4,1)} %bitcast.10), calls=%async_computation.8 | async-start | bytes 8388608
  49.2 14.0 %slice-start.5 = ((s8[16777216]{0:T(1024)(128)(4,1)}), s8[4194304]{0:T(1024)(128)(4,1)S(1)}, s32[]{:S(2)}) async-start(s8[16777216]{0:T(1024)(128)(4,1)} %bitcast.12), calls=%async_computation.10 | async-start | bytes 8388608
  49.2 14.0 %slice-start.6 = ((s8[16777216]{0:T(1024)(128)(4,1)}), s8[4194304]{0:T(1024)(128)(4,1)S(1)}, s32[]{:S(2)}) async-start(s8[16777216]{0:T(1024)(128)(4,1)} %bitcast.12), calls=%async_computation.11 | async-start | bytes 8388608
  49.2 14.0 %slice-start.7 = ((s8[16777216]{0:T(1024)(128)(4,1)}), s8[4194304]{0:T(1024)(128)(4,1)S(1)}, s32[]{:S(2)}) async-start(s8[16777216]{0:T(1024)(128)(4,1)} %bitcast.12), calls=%async_computation.12 | async-start | bytes 8388608
  63.2 3.2 %collective-permute-start.4 = (bf16[8,144,128]{2,1,0:T(8,128)(2,1)S(1)}, bf16[8,144,128]{2,1,0:T(8,128)(2,1)S(1)}, u32[]{:S(2)}, u32[]{:S(2)}) collective-permute-start(bf16[8,144,128]{2,1,0:T(8,128)(2,1)S(1)} %all_to_all.28.refs_0_), channel_id=1, source_target_pairs={{0,1},{1,0},{2,3},{3,2},{4,5},{5,4},{6,7},{7,6},{8,9},{9,8},{10,11... | collective-permute-start | bytes 884744 | tf_op jit(solution)/shard_map/ppermute | solution.py:72
  72.0 2.1 %collective-permute-start.5 = (bf16[8,32,512]{2,1,0:T(8,128)(2,1)S(1)}, bf16[8,32,512]{2,1,0:T(8,128)(2,1)S(1)}, u32[]{:S(2)}, u32[]{:S(2)}) collective-permute-start(bf16[8,32,512]{2,1,0:T(8,128)(2,1)S(1)} %get-tuple-element.64), channel_id=1, source_target_pairs={{0,1},{1,0},{2,3},{3,2},{4,5},{5,4},{6,7},{7,6},{8,9},{9,8},{10,11... | collective-permute-start | bytes 786440 | tf_op jit(solution)/shard_map/ppermute | solution.py:72

commit v8 on v7

--- a/solution.py
+++ b/solution.py
@@ -607,13 +607,14 @@
     upper = (up + up_part[...]) * scale + dot(low, lift_ref[...])
     active_out[...] = (gate * jax.nn.sigmoid(gate) * upper).astype(jnp.bfloat16)
 
-    @pl.loop(0, early)
-    def _(k):
+    for k in range(early):
         theirs_out[k] = dot(active_out[...], early_ref[k]).astype(theirs_out.dtype)
 
     @pl.loop(0, chips - early)
     def _(k):
         first(k).wait()
+
+    for k in range(chips - early):
         theirs_out[k + early] = dot(active_out[...], held[k]).astype(theirs_out.dtype)
 
     @pl.loop(0, chips)

time: 86.9 us -> 86.2 us (level)
  no operation moved by 1% of the time
where the time goes in v8:
time: 86.2 us; the launch traced here: 85.9 us
  blocking collectives  65.1 us (76%)
  Pallas kernels  17 us (20%)
  starting transfers between devices  1.27 us (1%)
  waiting for transfers between devices  0.88 us (1%)
    all_to_all x5, blocking collectives, exchange(): lax.all_to_all(blocks, axis, 0, 0, axis_index_groups=core_groups(axis), t...  65.1 us
    pallas_call x8, Pallas kernels, call(): pl.pallas_call(run, out_shape=outs, in_specs=[WHOLE] * (len(args) + len(w...  14.9 us
  transfers between devices with their start and end apart: 6, of which 2 were waited for; matrix products, arithmetic and copies ran while one was open for 0% of the time, Pallas kernels for 9%

profile of v8, /device:TPU:0, one launch (start us, length us, event | category | flops | bytes accessed | tf_op | source)
XLA Modules:
  0.0 85.9 jit_solution(1248822115922713565)
XLA Ops:
  0.0 1.2 %spread.1 = (bf16[8,32,512]{2,1,0:T(8,128)(2,1)S(1)}, bf16[32,512]{1,0:T(8,128)(2,1)S(1)}, bf16[64,128]{1,0:T(8,128)(2,1)S(1)}, bf16[64,128]{1,0:T(8,128)(2,1)S(1)}, s32[1,32]{1,0:T(1,128)S(1)}) custom-call(bf16[32,512]{1,0:T(8,128)(2,1)} %refs_0_.1, bf16[64,128]{1,0:T(8,128)(2,1)} %bitcast.22, bf16[64,128]{1,0:T(8,128)(2,1)} %bitcast.23, s32[1,32]{1,0:T(1,128)} %refs_3_.3, ...), custom_call_target="tpu_custom_call" | custom-call | tf_op jit(solution)/shard_map/spread/pallas_call | solution.py:290
  1.2 16.2 %all_to_all.25.after_ref.refs_0_ = bf16[8,32,512]{2,1,0:T(8,128)(2,1)S(1)} all-to-all(bf16[8,32,512]{2,1,0:T(8,128)(2,1)S(1)} %get-tuple-element.35), channel_id=1, replica_groups={{0,2,4,6,8,10,12,14},{1,3,5,7,9,11,13,15},{16,18,20,22,24,26,28,30},{17..., dimensions={0} | all-to-all | bytes 524288 | tf_op jit(solution)/shard_map/all_to_all | solution.py:22
  17.5 0.5 collective-permute-start
  18.6 0.9 %tables.1 = (bf16[16,512]{1,0:T(8,128)(2,1)S(1)}, bf16[16,1024]{1,0:T(8,128)(2,1)S(1)}, s32[8,128]{1,0:T(8,128)S(1)}, f32[32,128]{1,0:T(8,128)S(1)}, f32[32,128]{1,0:T(8,128)S(1)}, /*index=5*/f32[32,32]{1,0:T(8,128)S(1)}) custom-call(s32[1]{0:T(128)S(6)} %copy.17.request_ref, s32[16]{0:T(128)} %place_ref.1, bf16[16,16,512]{2,1,0:T(8,128)(2,1)} %query_ref.1, ...), custom_call_target="tpu_custom_call" | custom-call | tf_op jit(solution)/shard_map/tables/pallas_call | solution.py:341
  19.6 0.2 collective-permute-done.refs_1_
  19.8 1.3 %project.1 = (bf16[32,8192]{1,0:T(8,128)(2,1)S(1)}, bf16[32,128]{1,0:T(8,128)(2,1)S(1)}, bf16[8,16,640]{2,1,0:T(8,128)(2,1)S(1)}) custom-call(bf16[8,32,512]{2,1,0:T(8,128)(2,1)S(1)} %all_to_all.25.after_ref.refs_0_, bf16[8,32,512]{2,1,0:T(8,128)(2,1)S(1)} %collective-permute-done.refs_1_, bf16[64,128]{1,0:T(8,128)(2,1)S(1)} %get-tuple-element.37.refs_2_, ...), custom_call_target="tpu_custom_call" | custom-call | flops 83886080 | bytes 2621440 | tf_op jit(solution)/shard_map/project/pallas_call | solution.py:248
  21.0 0.2 collective-permute-start.2
  21.2 1.5 %query.1.refs_0_ = f32[32,512]{1,0:T(8,128)S(1)} custom-call(bf16[32,8192]{1,0:T(8,128)(2,1)S(1)} %get-tuple-element.42.refs_0_, bf16[8192,512]{1,0:T(8,128)(2,1)S(1)} %bitcast.17, bf16[8192,1024]{1,0:T(8,128)(2,1)} %refs_7_.3, bf16[8192,1024]{1,0:T(8,128)(2,1)} %refs_8_.3, bf16[1024,8192]{1,0:T(8,128)(2,1)} %refs_9_.3), custom_call_target="tpu_custom_call" | custom-call | flops 268435456 | bytes 8388608 | tf_op jit(solution)/shard_map/query/pallas_call | solution.py:248
  22.7 11.4 %all_to_all.26.refs_4_ = bf16[8,16,640]{2,1,0:T(8,128)(2,1)S(1)} all-to-all(bf16[8,16,640]{2,1,0:T(8,128)(2,1)S(1)} %get-tuple-element.46), channel_id=1, replica_groups={{0,2,4,6,8,10,12,14},{1,3,5,7,9,11,13,15},{16,18,20,22,24,26,28,30},{17..., dimensions={0} | all-to-all | bytes 327680 | tf_op jit(solution)/shard_map/all_to_all | solution.py:22
  34.1 1.5 %attend.1 = (bf16[32,512]{1,0:T(8,128)(2,1)S(1)}, bf16[8,32,512]{2,1,0:T(8,128)(2,1)S(1)}, bf16[16,640]{1,0:T(8,128)(2,1)S(1)}) custom-call(f32[32,512]{1,0:T(8,128)S(1)} %query.1.refs_0_, bf16[32,128]{1,0:T(8,128)(2,1)S(1)} %get-tuple-element.41.refs_1_, bf16[32,128]{1,0:T(8,128)(2,1)S(1)} %collective-permute-done.2.refs_2_, ...), custom_call_target="tpu_custom_call" | custom-call | flops 268435456 | bytes 8388608 | tf_op jit(solution)/shard_map/attend/pallas_call | solution.py:248
  35.6 0.0 collective-permute-start.3
  35.6 0.8 rest.1
  36.5 0.7 collective-permute-done.3
  37.2 0.1 add_convert_fusion.1
  37.2 11.9 %all_to_all.27.refs_0_ = bf16[8,32,512]{2,1,0:T(8,128)(2,1)S(1)} all-to-all(bf16[8,32,512]{2,1,0:T(8,128)(2,1)S(1)} %add_convert_fusion.1), channel_id=1, replica_groups={{0,2,4,6,8,10,12,14},{1,3,5,7,9,11,13,15},{16,18,20,22,24,26,28,30},{17..., dimensions={0} | all-to-all | bytes 524288 | tf_op jit(solution)/shard_map/all_to_all | solution.py:22
  49.3 0.3 hidden.1
  49.5 13.7 %all_to_all.28.refs_0_ = bf16[8,144,128]{2,1,0:T(8,128)(2,1)S(1)} all-to-all(bf16[8,144,128]{2,1,0:T(8,128)(2,1)S(1)} %get-tuple-element.57), channel_id=1, replica_groups={{0,2,4,6,8,10,12,14},{1,3,5,7,9,11,13,15},{16,18,20,22,24,26,28,30},{17..., dimensions={0} | all-to-all | bytes 589824 | tf_op jit(solution)/shard_map/all_to_all | solution.py:22
  63.3 3.1 %near.1 = (f32[32,1024]{1,0:T(8,128)S(1)}, f32[32,1024]{1,0:T(8,128)S(1)}, bf16[4,1024,512]{2,1,0:T(8,128)(2,1)S(1)}) custom-call(bf16[8,144,128]{2,1,0:T(8,128)(2,1)S(1)} %all_to_all.28.refs_0_, bf16[64,128]{1,0:T(8,128)(2,1)S(1)} %get-tuple-element.54.refs_2_.refs_1_, bf16[8192,1024]{1,0:T(8,128)(2,1)S(1)} %bitcast.11, bf16[8192,1024]{1,0:T(8,128)(2,1)S(1)} %bitcast.13, ...), custom_call_target="tpu_custom_call" | custom-call | flops 1610612736 | bytes 50331648 | tf_op jit(solution)/shard_map/near/pallas_call | solution.py:248
  66.4 4.9 %forward.1 = (bf16[32,1024]{1,0:T(8,128)(2,1)S(1)}, bf16[8,32,512]{2,1,0:T(8,128)(2,1)S(1)}, bf16[8,1024,512]{2,1,0:T(8,128)(2,1)S(1)}) custom-call(bf16[8,144,128]{2,1,0:T(8,128)(2,1)S(1)} %all_to_all.28.refs_0_, bf16[8,144,128]{2,1,0:T(8,128)(2,1)S(1)} %collective-permute-done.4.refs_1_, bf16[64,128]{1,0:T(8,128)(2,1)S(1)} %get-tuple-element.54.refs_2_.refs_1_, ...), custom_call_target="tpu_custom_call" | custom-call | flops 1610612736 | bytes 50331648 | tf_op jit(solution)/shard_map/forward/pallas_call | solution.py:248
  71.3 0.6 collective-permute-start.5
  71.8 1.5 %last.1 = f32[8,32,512]{2,1,0:T(8,128)S(1)} custom-call(bf16[32,1024]{1,0:T(8,128)(2,1)S(1)} %get-tuple-element.62.refs_0_, bf16[8,1024,512]{2,1,0:T(8,128)(2,1)S(1)} %get-tuple-element.63.refs_1_), custom_call_target="tpu_custom_call" | custom-call | tf_op jit(solution)/shard_map/last/pallas_call | solution.py:248
  73.4 0.1 add_convert_fusion
  73.5 11.8 %all_to_all.29 = bf16[8,32,512]{2,1,0:T(8,128)(2,1)S(1)} all-to-all(bf16[8,32,512]{2,1,0:T(8,128)(2,1)S(1)} %add_convert_fusion), channel_id=1, replica_groups={{0,2,4,6,8,10,12,14},{1,3,5,7,9,11,13,15},{16,18,20,22,24,26,28,30},{17..., dimensions={0} | all-to-all | bytes 524288 | tf_op jit(solution)/shard_map/all_to_all | solution.py:22
  85.3 0.6 add_convert_fusion.2
  (41 shorter events, 0.1 us)
Async XLA Ops:
  0.0 21.2 %slice-start.10 = ((s8[8388608]{0:T(1024)(128)(4,1)}), s8[4194304]{0:T(1024)(128)(4,1)S(1)}, s32[]{:S(2)}) async-start(s8[8388608]{0:T(1024)(128)(4,1)} %bitcast.16), calls=%async_computation.15 | async-start | bytes 8388608
  0.0 17.5 %copy-start.2 = (bf16[1,8192,32]{1,2,0:T(8,128)(2,1)S(1)}, bf16[1,8192,32]{1,2,0:T(8,128)(2,1)}, u32[]{:S(2)}) copy-start(bf16[1,8192,32]{1,2,0:T(8,128)(2,1)} %param.26) | copy-start | bytes 1572868
  0.0 19.8 %copy-start = (bf16[8192,64]{0,1:T(8,128)(2,1)S(1)}, bf16[8192,64]{0,1:T(8,128)(2,1)}, u32[]{:S(2)}) copy-start(bf16[8192,64]{0,1:T(8,128)(2,1)} %param.20) | copy-start | bytes 3145732
  0.0 19.8 %copy-start.1 = (bf16[8192,64]{0,1:T(8,128)(2,1)S(1)}, bf16[8192,64]{0,1:T(8,128)(2,1)}, u32[]{:S(2)}) copy-start(bf16[8192,64]{0,1:T(8,128)(2,1)} %param.21) | copy-start | bytes 3145732
  0.0 21.2 %slice-start.11 = ((s8[8388608]{0:T(1024)(128)(4,1)}), s8[4194304]{0:T(1024)(128)(4,1)S(1)}, s32[]{:S(2)}) async-start(s8[8388608]{0:T(1024)(128)(4,1)} %bitcast.16), calls=%async_computation.16 | async-start | bytes 8388608
  17.5 2.3 %collective-permute-start.1 = (bf16[1,8192,32]{1,2,0:T(8,128)(2,1)S(1)}, bf16[1,8192,32]{1,2,0:T(8,128)(2,1)S(1)}, u32[]{:S(2)}, u32[]{:S(2)}) collective-permute-start(bf16[1,8192,32]{1,2,0:T(8,128)(2,1)S(1)} %copy-done.2), channel_id=1, source_target_pairs={{0,1},{1,0},{2,3},{3,2},{4,5},{5,4},{6,7},{7,6},{8,9},{9,8},{10,11... | collective-permute-start | bytes 1572872 | tf_op jit(solution)/shard_map/ppermute | solution.py:72
  17.5 2.3 %collective-permute-start = (bf16[8,32,512]{2,1,0:T(8,128)(2,1)S(1)}, bf16[8,32,512]{2,1,0:T(8,128)(2,1)S(1)}, u32[]{:S(2)}, u32[]{:S(2)}) collective-permute-start(bf16[8,32,512]{2,1,0:T(8,128)(2,1)S(1)} %all_to_all.25.after_ref.refs_0_), channel_id=1, source_target_pairs={{0,1},{1,0},{2,3},{3,2},{4,5},{5,4},{6,7},{7,6},{8,9},{9,8},{10,11... | collective-permute-start | bytes 786440 | tf_op jit(solution)/shard_map/ppermute | solution.py:72
  19.8 14.4 %slice-start.8 = ((s8[8388608]{0:T(1024)(128)(4,1)}), s8[4194304]{0:T(1024)(128)(4,1)S(1)}, s32[]{:S(2)}) async-start(s8[8388608]{0:T(1024)(128)(4,1)} %bitcast.14), calls=%async_computation.13 | async-start | bytes 8388608
  21.0 1.7 %collective-permute-start.2 = (bf16[32,128]{1,0:T(8,128)(2,1)S(1)}, bf16[32,128]{1,0:T(8,128)(2,1)S(1)}, u32[]{:S(2)}, u32[]{:S(2)}) collective-permute-start(bf16[32,128]{1,0:T(8,128)(2,1)S(1)} %get-tuple-element.41.refs_1_), channel_id=1, source_target_pairs={{0,1},{1,0},{2,3},{3,2},{4,5},{5,4},{6,7},{7,6},{8,9},{9,8},{10,11... | collective-permute-start | bytes 24584 | tf_op jit(solution)/shard_map/ppermute | solution.py:72
  21.2 12.9 %slice-start.9 = ((s8[8388608]{0:T(1024)(128)(4,1)}), s8[4194304]{0:T(1024)(128)(4,1)S(1)}, s32[]{:S(2)}) async-start(s8[8388608]{0:T(1024)(128)(4,1)} %bitcast.14), calls=%async_computation.14 | async-start | bytes 8388608
  35.6 1.6 %collective-permute-start.3 = (bf16[8,32,512]{2,1,0:T(8,128)(2,1)S(1)}, bf16[8,32,512]{2,1,0:T(8,128)(2,1)S(1)}, u32[]{:S(2)}, u32[]{:S(2)}) collective-permute-start(bf16[8,32,512]{2,1,0:T(8,128)(2,1)S(1)} %get-tuple-element.52), channel_id=1, source_target_pairs={{0,1},{1,0},{2,3},{3,2},{4,5},{5,4},{6,7},{7,6},{8,9},{9,8},{10,11... | collective-permute-start | bytes 786440 | tf_op jit(solution)/shard_map/ppermute | solution.py:72
  49.2 14.0 %slice-start = ((s8[16777216]{0:T(1024)(128)(4,1)}), s8[4194304]{0:T(1024)(128)(4,1)S(1)}, s32[]{:S(2)}) async-start(s8[16777216]{0:T(1024)(128)(4,1)} %bitcast.10), calls=%async_computation.5 | async-start | bytes 8388608
  49.2 14.0 %slice-start.4 = ((s8[16777216]{0:T(1024)(128)(4,1)}), s8[4194304]{0:T(1024)(128)(4,1)S(1)}, s32[]{:S(2)}) async-start(s8[16777216]{0:T(1024)(128)(4,1)} %bitcast.12), calls=%async_computation.9 | async-start | bytes 8388608
  49.2 14.0 %slice-start.1 = ((s8[16777216]{0:T(1024)(128)(4,1)}), s8[4194304]{0:T(1024)(128)(4,1)S(1)}, s32[]{:S(2)}) async-start(s8[16777216]{0:T(1024)(128)(4,1)} %bitcast.10), calls=%async_computation.6 | async-start | bytes 8388608
  49.2 14.0 %slice-start.2 = ((s8[16777216]{0:T(1024)(128)(4,1)}), s8[4194304]{0:T(1024)(128)(4,1)S(1)}, s32[]{:S(2)}) async-start(s8[16777216]{0:T(1024)(128)(4,1)} %bitcast.10), calls=%async_computation.7 | async-start | bytes 8388608
  49.2 14.0 %slice-start.3 = ((s8[16777216]{0:T(1024)(128)(4,1)}), s8[4194304]{0:T(1024)(128)(4,1)S(1)}, s32[]{:S(2)}) async-start(s8[16777216]{0:T(1024)(128)(4,1)} %bitcast.10), calls=%async_computation.8 | async-start | bytes 8388608
  49.2 14.0 %slice-start.5 = ((s8[16777216]{0:T(1024)(128)(4,1)}), s8[4194304]{0:T(1024)(128)(4,1)S(1)}, s32[]{:S(2)}) async-start(s8[16777216]{0:T(1024)(128)(4,1)} %bitcast.12), calls=%async_computation.10 | async-start | bytes 8388608
  49.2 14.0 %slice-start.6 = ((s8[16777216]{0:T(1024)(128)(4,1)}), s8[4194304]{0:T(1024)(128)(4,1)S(1)}, s32[]{:S(2)}) async-start(s8[16777216]{0:T(1024)(128)(4,1)} %bitcast.12), calls=%async_computation.11 | async-start | bytes 8388608
  49.2 14.0 %slice-start.7 = ((s8[16777216]{0:T(1024)(128)(4,1)}), s8[4194304]{0:T(1024)(128)(4,1)S(1)}, s32[]{:S(2)}) async-start(s8[16777216]{0:T(1024)(128)(4,1)} %bitcast.12), calls=%async_computation.12 | async-start | bytes 8388608
  63.2 3.2 %collective-permute-start.4 = (bf16[8,144,128]{2,1,0:T(8,128)(2,1)S(1)}, bf16[8,144,128]{2,1,0:T(8,128)(2,1)S(1)}, u32[]{:S(2)}, u32[]{:S(2)}) collective-permute-start(bf16[8,144,128]{2,1,0:T(8,128)(2,1)S(1)} %all_to_all.28.refs_0_), channel_id=1, source_target_pairs={{0,1},{1,0},{2,3},{3,2},{4,5},{5,4},{6,7},{7,6},{8,9},{9,8},{10,11... | collective-permute-start | bytes 884744 | tf_op jit(solution)/shard_map/ppermute | solution.py:72
  71.3 2.1 %collective-permute-start.5 = (bf16[8,32,512]{2,1,0:T(8,128)(2,1)S(1)}, bf16[8,32,512]{2,1,0:T(8,128)(2,1)S(1)}, u32[]{:S(2)}, u32[]{:S(2)}) collective-permute-start(bf16[8,32,512]{2,1,0:T(8,128)(2,1)S(1)} %get-tuple-element.64), channel_id=1, source_target_pairs={{0,1},{1,0},{2,3},{3,2},{4,5},{5,4},{6,7},{7,6},{8,9},{9,8},{10,11... | collective-permute-start | bytes 786440 | tf_op jit(solution)/shard_map/ppermute | solution.py:72

commit v9 on v8

--- a/solution.py
+++ b/solution.py
@@ -432,8 +432,8 @@
         here, dot_rows(normed, factor_ref[:rank, :]), dot_rows(normed, other_ref[:rank, :])
     )
     half = key_ref.shape[0]
-    pair_out[:, :half] = dot_rows(normed, key_ref[...]).astype(jnp.bfloat16)
-    pair_out[:, half:] = dot_rows(normed, value_ref[...]).astype(jnp.bfloat16)
+    turned = [dot_rows(ref[...], normed) for ref in (key_ref, value_ref)]
+    pair_out[...] = jnp.concatenate(turned, axis=0).T.astype(jnp.bfloat16)
     folded = fold(low)
     for chip in range(chips):
         at = pl.multiple_of((2 * chip + core) * cols, cols)
@@ -454,9 +454,17 @@
         out[chip] = dot(left, weight_ref[:, pl.ds(at, cols)]).astype(out.dtype)
 
 
+def owner_part(owner, got_ref, lanes):
+    part = jnp.zeros((got_ref.shape[1], lanes.stop - lanes.start), jnp.float32)
+    for chip in range(got_ref.shape[0]):
+        sent = got_ref[chip, :, lanes].astype(jnp.float32)
+        part = part + jnp.where((owner >> 1) == chip, sent, 0.0)
+    return part
+
+
 def attend_kernel(
     query_ref, pair_mine, pair_theirs, owner_ref, got_ref, lift_ref, cosine_ref, sine_ref,
-    reach_ref, output_ref, mixed_out, theirs_out, piece_out,
+    reach_ref, output_ref, mixed_out, theirs_out,
 ):
     rows, query_cols = query_ref.shape
     chips, _, cols = theirs_out.shape
@@ -464,12 +472,7 @@
     heads = query_cols // head
     half = head // 2
     owner = owner_ref[:1, :1]
-    piece = jnp.zeros(got_ref.shape[1:], jnp.float32)
-    for chip in range(chips):
-        sent = got_ref[chip].astype(jnp.float32)
-        piece = piece + jnp.where((owner >> 1) == chip, sent, 0.0)
-    piece_out[...] = piece.astype(jnp.bfloat16)
-    low = unfold(piece[:, cols:])
+    low = unfold(owner_part(owner, got_ref, slice(cols, cols + LANES)))
     lane = lax.broadcasted_iota(jnp.int32, (rows, head), 1)
     cosine = cosine_ref[...]
     sine = sine_ref[...]
@@ -495,7 +498,9 @@
     side_product(mixed, output_ref, 1 - core_index(), theirs_out)
 
 
-def rest_kernel(mixed_ref, output_ref, mine_out):
+def rest_kernel(mixed_ref, owner_ref, got_ref, output_ref, mine_out, piece_out):
+    part = owner_part(owner_ref[:1, :1], got_ref, slice(0, piece_out.shape[1]))
+    piece_out[...] = part.astype(jnp.bfloat16)
     side_product(mixed_ref[...], output_ref, core_index(), mine_out)
 
 
@@ -690,24 +695,28 @@
         heavy,
     )
     pair_theirs, query, payload = lax.optimization_barrier((pair_theirs, query, payload))
-    mixed, sent, piece = call(
+    got = exchange(payload, "tp")
+    mixed, sent = call(
         attend_kernel,
         "attend",
         (
             shape((rows, query_weight.shape[1]), bf16),
             shape((chips, rows, cols), bf16),
-            shape(payload.shape[1:], bf16),
         ),
         (
-            query, pair, pair_theirs, owner, exchange(payload, "tp"), query_lift, cosine,
+            query, pair, pair_theirs, owner, got, query_lift, cosine,
             sine, reach,
         ),
         (output_weight,),
         heavy + (query_weight,),
     )
     sent_theirs = partner_2(sent, "tp", 0)
-    (kept,) = call(
-        rest_kernel, "rest", (shape((chips, rows, cols), f32),), (mixed,), (output_weight,)
+    kept, piece = call(
+        rest_kernel,
+        "rest",
+        (shape((chips, rows, cols), f32), shape((rank, cols), bf16)),
+        (mixed, owner, got),
+        (output_weight,),
     )
     chip_sum = (kept + sent_theirs.astype(f32)).astype(bf16)
     hidden, payload = call(

time: 86.2 us -> 86.2 us (level)
  no operation moved by 1% of the time
where the time goes in v9:
time: 86.2 us; the launch traced here: 85.9 us
  blocking collectives  65.1 us (76%)
  Pallas kernels  16.9 us (20%)
  starting transfers between devices  1.28 us (1%)
    all_to_all x5, blocking collectives, exchange(): lax.all_to_all(blocks, axis, 0, 0, axis_index_groups=core_groups(axis), t...  65.1 us
    pallas_call x8, Pallas kernels, call(): pl.pallas_call(run, out_shape=outs, in_specs=[WHOLE] * (len(args) + len(w...  14.8 us
  transfers between devices with their start and end apart: 6, of which 2 were waited for; matrix products, arithmetic and copies ran while one was open for 0% of the time, Pallas kernels for 9%

profile of v9, /device:TPU:0, one launch (start us, length us, event | category | flops | bytes accessed | tf_op | source)
XLA Modules:
  0.0 85.9 jit_solution(14874058083277694785)
XLA Ops:
  0.0 1.2 %spread.1 = (bf16[8,32,512]{2,1,0:T(8,128)(2,1)S(1)}, bf16[32,512]{1,0:T(8,128)(2,1)S(1)}, bf16[64,128]{1,0:T(8,128)(2,1)S(1)}, bf16[64,128]{1,0:T(8,128)(2,1)S(1)}, s32[1,32]{1,0:T(1,128)S(1)}) custom-call(bf16[32,512]{1,0:T(8,128)(2,1)} %refs_0_.1, bf16[64,128]{1,0:T(8,128)(2,1)} %bitcast.22, bf16[64,128]{1,0:T(8,128)(2,1)} %bitcast.23, s32[1,32]{1,0:T(1,128)} %refs_3_.4, ...), custom_call_target="tpu_custom_call" | custom-call | tf_op jit(solution)/shard_map/spread/pallas_call | solution.py:290
  1.2 16.2 %all_to_all.25.after_ref.refs_0_ = bf16[8,32,512]{2,1,0:T(8,128)(2,1)S(1)} all-to-all(bf16[8,32,512]{2,1,0:T(8,128)(2,1)S(1)} %get-tuple-element.36), channel_id=1, replica_groups={{0,2,4,6,8,10,12,14},{1,3,5,7,9,11,13,15},{16,18,20,22,24,26,28,30},{17..., dimensions={0} | all-to-all | bytes 524288 | tf_op jit(solution)/shard_map/all_to_all | solution.py:22
  17.5 0.5 collective-permute-start
  18.6 0.9 %tables.1 = (bf16[16,512]{1,0:T(8,128)(2,1)S(1)}, bf16[16,1024]{1,0:T(8,128)(2,1)S(1)}, s32[8,128]{1,0:T(8,128)S(1)}, f32[32,128]{1,0:T(8,128)S(1)}, f32[32,128]{1,0:T(8,128)S(1)}, /*index=5*/f32[32,32]{1,0:T(8,128)S(1)}) custom-call(s32[1]{0:T(128)S(6)} %copy.17.request_ref, s32[16]{0:T(128)} %place_ref.1, bf16[16,16,512]{2,1,0:T(8,128)(2,1)} %query_ref.1, ...), custom_call_target="tpu_custom_call" | custom-call | tf_op jit(solution)/shard_map/tables/pallas_call | solution.py:341
  19.6 0.2 collective-permute-done.refs_1_
  19.8 1.2 %project.1 = (bf16[32,8192]{1,0:T(8,128)(2,1)S(1)}, bf16[32,128]{1,0:T(8,128)(2,1)S(1)}, bf16[8,16,640]{2,1,0:T(8,128)(2,1)S(1)}) custom-call(bf16[8,32,512]{2,1,0:T(8,128)(2,1)S(1)} %all_to_all.25.after_ref.refs_0_, bf16[8,32,512]{2,1,0:T(8,128)(2,1)S(1)} %collective-permute-done.refs_1_, bf16[64,128]{1,0:T(8,128)(2,1)S(1)} %get-tuple-element.38.refs_2_, ...), custom_call_target="tpu_custom_call" | custom-call | flops 83886080 | bytes 2621440 | tf_op jit(solution)/shard_map/project/pallas_call | solution.py:248
  21.0 0.2 collective-permute-start.2
  21.2 1.5 %query.1.refs_0_ = f32[32,512]{1,0:T(8,128)S(1)} custom-call(bf16[32,8192]{1,0:T(8,128)(2,1)S(1)} %get-tuple-element.43.refs_0_, bf16[8192,512]{1,0:T(8,128)(2,1)S(1)} %bitcast.17, bf16[8192,1024]{1,0:T(8,128)(2,1)} %refs_7_.3, bf16[8192,1024]{1,0:T(8,128)(2,1)} %refs_8_.3, bf16[1024,8192]{1,0:T(8,128)(2,1)} %refs_9_.3), custom_call_target="tpu_custom_call" | custom-call | flops 268435456 | bytes 8388608 | tf_op jit(solution)/shard_map/query/pallas_call | solution.py:248
  22.7 11.4 %all_to_all.26.refs_4_.refs_2_ = bf16[8,16,640]{2,1,0:T(8,128)(2,1)S(1)} all-to-all(bf16[8,16,640]{2,1,0:T(8,128)(2,1)S(1)} %get-tuple-element.47), channel_id=1, replica_groups={{0,2,4,6,8,10,12,14},{1,3,5,7,9,11,13,15},{16,18,20,22,24,26,28,30},{17..., dimensions={0} | all-to-all | bytes 327680 | tf_op jit(solution)/shard_map/all_to_all | solution.py:22
  34.1 1.4 %attend.1 = (bf16[32,512]{1,0:T(8,128)(2,1)S(1)}, bf16[8,32,512]{2,1,0:T(8,128)(2,1)S(1)}) custom-call(f32[32,512]{1,0:T(8,128)S(1)} %query.1.refs_0_, bf16[32,128]{1,0:T(8,128)(2,1)S(1)} %get-tuple-element.42.refs_1_, bf16[32,128]{1,0:T(8,128)(2,1)S(1)} %collective-permute-done.2.refs_2_, s32[8,128]{1,0:T(8,128)S(1)} %get-tuple-element.40.refs_3_.refs_1_, ...), custom_call_target="tpu_custom_call" | custom-call | flops 268435456 | bytes 8388608 | tf_op jit(solution)/shard_map/attend/pallas_call | solution.py:248
  35.6 0.0 collective-permute-start.3
  35.6 0.8 rest.1
  36.5 0.7 collective-permute-done.3
  37.1 0.1 add_convert_fusion.1
  37.2 12.0 %all_to_all.27.refs_0_ = bf16[8,32,512]{2,1,0:T(8,128)(2,1)S(1)} all-to-all(bf16[8,32,512]{2,1,0:T(8,128)(2,1)S(1)} %add_convert_fusion.1), channel_id=1, replica_groups={{0,2,4,6,8,10,12,14},{1,3,5,7,9,11,13,15},{16,18,20,22,24,26,28,30},{17..., dimensions={0} | all-to-all | bytes 524288 | tf_op jit(solution)/shard_map/all_to_all | solution.py:22
  49.2 0.3 hidden.1
  49.5 13.7 %all_to_all.28.refs_0_ = bf16[8,144,128]{2,1,0:T(8,128)(2,1)S(1)} all-to-all(bf16[8,144,128]{2,1,0:T(8,128)(2,1)S(1)} %get-tuple-element.59), channel_id=1, replica_groups={{0,2,4,6,8,10,12,14},{1,3,5,7,9,11,13,15},{16,18,20,22,24,26,28,30},{17..., dimensions={0} | all-to-all | bytes 589824 | tf_op jit(solution)/shard_map/all_to_all | solution.py:22
  63.2 3.1 %near.1 = (f32[32,1024]{1,0:T(8,128)S(1)}, f32[32,1024]{1,0:T(8,128)S(1)}, bf16[4,1024,512]{2,1,0:T(8,128)(2,1)S(1)}) custom-call(bf16[8,144,128]{2,1,0:T(8,128)(2,1)S(1)} %all_to_all.28.refs_0_, bf16[64,128]{1,0:T(8,128)(2,1)S(1)} %get-tuple-element.56.refs_2_.refs_1_, bf16[8192,1024]{1,0:T(8,128)(2,1)S(1)} %bitcast.11, bf16[8192,1024]{1,0:T(8,128)(2,1)S(1)} %bitcast.13, ...), custom_call_target="tpu_custom_call" | custom-call | flops 1610612736 | bytes 50331648 | tf_op jit(solution)/shard_map/near/pallas_call | solution.py:248
  66.3 4.9 %forward.1 = (bf16[32,1024]{1,0:T(8,128)(2,1)S(1)}, bf16[8,32,512]{2,1,0:T(8,128)(2,1)S(1)}, bf16[8,1024,512]{2,1,0:T(8,128)(2,1)S(1)}) custom-call(bf16[8,144,128]{2,1,0:T(8,128)(2,1)S(1)} %all_to_all.28.refs_0_, bf16[8,144,128]{2,1,0:T(8,128)(2,1)S(1)} %collective-permute-done.4.refs_1_, bf16[64,128]{1,0:T(8,128)(2,1)S(1)} %get-tuple-element.56.refs_2_.refs_1_, ...), custom_call_target="tpu_custom_call" | custom-call | flops 1610612736 | bytes 50331648 | tf_op jit(solution)/shard_map/forward/pallas_call | solution.py:248
  71.2 0.6 collective-permute-start.5
  71.8 1.5 %last.1 = f32[8,32,512]{2,1,0:T(8,128)S(1)} custom-call(bf16[32,1024]{1,0:T(8,128)(2,1)S(1)} %get-tuple-element.64.refs_0_, bf16[8,1024,512]{2,1,0:T(8,128)(2,1)S(1)} %get-tuple-element.65.refs_1_), custom_call_target="tpu_custom_call" | custom-call | tf_op jit(solution)/shard_map/last/pallas_call | solution.py:248
  73.3 0.1 add_convert_fusion
  73.4 11.8 %all_to_all.29 = bf16[8,32,512]{2,1,0:T(8,128)(2,1)S(1)} all-to-all(bf16[8,32,512]{2,1,0:T(8,128)(2,1)S(1)} %add_convert_fusion), channel_id=1, replica_groups={{0,2,4,6,8,10,12,14},{1,3,5,7,9,11,13,15},{16,18,20,22,24,26,28,30},{17..., dimensions={0} | all-to-all | bytes 524288 | tf_op jit(solution)/shard_map/all_to_all | solution.py:22
  85.3 0.6 add_convert_fusion.2
  (41 shorter events, 0.1 us)
Async XLA Ops:
  0.0 21.2 %slice-start.10 = ((s8[8388608]{0:T(1024)(128)(4,1)}), s8[4194304]{0:T(1024)(128)(4,1)S(1)}, s32[]{:S(2)}) async-start(s8[8388608]{0:T(1024)(128)(4,1)} %bitcast.16), calls=%async_computation.15 | async-start | bytes 8388608
  0.0 17.5 %copy-start.2 = (bf16[1,8192,32]{1,2,0:T(8,128)(2,1)S(1)}, bf16[1,8192,32]{1,2,0:T(8,128)(2,1)}, u32[]{:S(2)}) copy-start(bf16[1,8192,32]{1,2,0:T(8,128)(2,1)} %param.26) | copy-start | bytes 1572868
  0.0 19.8 %copy-start = (bf16[8192,64]{0,1:T(8,128)(2,1)S(1)}, bf16[8192,64]{0,1:T(8,128)(2,1)}, u32[]{:S(2)}) copy-start(bf16[8192,64]{0,1:T(8,128)(2,1)} %param.20) | copy-start | bytes 3145732
  0.0 19.8 %copy-start.1 = (bf16[8192,64]{0,1:T(8,128)(2,1)S(1)}, bf16[8192,64]{0,1:T(8,128)(2,1)}, u32[]{:S(2)}) copy-start(bf16[8192,64]{0,1:T(8,128)(2,1)} %param.21) | copy-start | bytes 3145732
  0.0 21.2 %slice-start.11 = ((s8[8388608]{0:T(1024)(128)(4,1)}), s8[4194304]{0:T(1024)(128)(4,1)S(1)}, s32[]{:S(2)}) async-start(s8[8388608]{0:T(1024)(128)(4,1)} %bitcast.16), calls=%async_computation.16 | async-start | bytes 8388608
  17.5 2.3 %collective-permute-start.1 = (bf16[1,8192,32]{1,2,0:T(8,128)(2,1)S(1)}, bf16[1,8192,32]{1,2,0:T(8,128)(2,1)S(1)}, u32[]{:S(2)}, u32[]{:S(2)}) collective-permute-start(bf16[1,8192,32]{1,2,0:T(8,128)(2,1)S(1)} %copy-done.2), channel_id=1, source_target_pairs={{0,1},{1,0},{2,3},{3,2},{4,5},{5,4},{6,7},{7,6},{8,9},{9,8},{10,11... | collective-permute-start | bytes 1572872 | tf_op jit(solution)/shard_map/ppermute | solution.py:72
  17.5 2.3 %collective-permute-start = (bf16[8,32,512]{2,1,0:T(8,128)(2,1)S(1)}, bf16[8,32,512]{2,1,0:T(8,128)(2,1)S(1)}, u32[]{:S(2)}, u32[]{:S(2)}) collective-permute-start(bf16[8,32,512]{2,1,0:T(8,128)(2,1)S(1)} %all_to_all.25.after_ref.refs_0_), channel_id=1, source_target_pairs={{0,1},{1,0},{2,3},{3,2},{4,5},{5,4},{6,7},{7,6},{8,9},{9,8},{10,11... | collective-permute-start | bytes 786440 | tf_op jit(solution)/shard_map/ppermute | solution.py:72
  19.8 14.4 %slice-start.8 = ((s8[8388608]{0:T(1024)(128)(4,1)}), s8[4194304]{0:T(1024)(128)(4,1)S(1)}, s32[]{:S(2)}) async-start(s8[8388608]{0:T(1024)(128)(4,1)} %bitcast.14), calls=%async_computation.13 | async-start | bytes 8388608
  21.0 1.7 %collective-permute-start.2 = (bf16[32,128]{1,0:T(8,128)(2,1)S(1)}, bf16[32,128]{1,0:T(8,128)(2,1)S(1)}, u32[]{:S(2)}, u32[]{:S(2)}) collective-permute-start(bf16[32,128]{1,0:T(8,128)(2,1)S(1)} %get-tuple-element.42.refs_1_), channel_id=1, source_target_pairs={{0,1},{1,0},{2,3},{3,2},{4,5},{5,4},{6,7},{7,6},{8,9},{9,8},{10,11... | collective-permute-start | bytes 24584 | tf_op jit(solution)/shard_map/ppermute | solution.py:72
  21.2 12.9 %slice-start.9 = ((s8[8388608]{0:T(1024)(128)(4,1)}), s8[4194304]{0:T(1024)(128)(4,1)S(1)}, s32[]{:S(2)}) async-start(s8[8388608]{0:T(1024)(128)(4,1)} %bitcast.14), calls=%async_computation.14 | async-start | bytes 8388608
  35.6 1.6 %collective-permute-start.3 = (bf16[8,32,512]{2,1,0:T(8,128)(2,1)S(1)}, bf16[8,32,512]{2,1,0:T(8,128)(2,1)S(1)}, u32[]{:S(2)}, u32[]{:S(2)}) collective-permute-start(bf16[8,32,512]{2,1,0:T(8,128)(2,1)S(1)} %get-tuple-element.54), channel_id=1, source_target_pairs={{0,1},{1,0},{2,3},{3,2},{4,5},{5,4},{6,7},{7,6},{8,9},{9,8},{10,11... | collective-permute-start | bytes 786440 | tf_op jit(solution)/shard_map/ppermute | solution.py:72
  49.2 14.0 %slice-start = ((s8[16777216]{0:T(1024)(128)(4,1)}), s8[4194304]{0:T(1024)(128)(4,1)S(1)}, s32[]{:S(2)}) async-start(s8[16777216]{0:T(1024)(128)(4,1)} %bitcast.10), calls=%async_computation.5 | async-start | bytes 8388608
  49.2 14.0 %slice-start.4 = ((s8[16777216]{0:T(1024)(128)(4,1)}), s8[4194304]{0:T(1024)(128)(4,1)S(1)}, s32[]{:S(2)}) async-start(s8[16777216]{0:T(1024)(128)(4,1)} %bitcast.12), calls=%async_computation.9 | async-start | bytes 8388608
  49.2 14.0 %slice-start.1 = ((s8[16777216]{0:T(1024)(128)(4,1)}), s8[4194304]{0:T(1024)(128)(4,1)S(1)}, s32[]{:S(2)}) async-start(s8[16777216]{0:T(1024)(128)(4,1)} %bitcast.10), calls=%async_computation.6 | async-start | bytes 8388608
  49.2 14.0 %slice-start.2 = ((s8[16777216]{0:T(1024)(128)(4,1)}), s8[4194304]{0:T(1024)(128)(4,1)S(1)}, s32[]{:S(2)}) async-start(s8[16777216]{0:T(1024)(128)(4,1)} %bitcast.10), calls=%async_computation.7 | async-start | bytes 8388608
  49.2 14.0 %slice-start.3 = ((s8[16777216]{0:T(1024)(128)(4,1)}), s8[4194304]{0:T(1024)(128)(4,1)S(1)}, s32[]{:S(2)}) async-start(s8[16777216]{0:T(1024)(128)(4,1)} %bitcast.10), calls=%async_computation.8 | async-start | bytes 8388608
  49.2 14.0 %slice-start.5 = ((s8[16777216]{0:T(1024)(128)(4,1)}), s8[4194304]{0:T(1024)(128)(4,1)S(1)}, s32[]{:S(2)}) async-start(s8[16777216]{0:T(1024)(128)(4,1)} %bitcast.12), calls=%async_computation.10 | async-start | bytes 8388608
  49.2 14.0 %slice-start.6 = ((s8[16777216]{0:T(1024)(128)(4,1)}), s8[4194304]{0:T(1024)(128)(4,1)S(1)}, s32[]{:S(2)}) async-start(s8[16777216]{0:T(1024)(128)(4,1)} %bitcast.12), calls=%async_computation.11 | async-start | bytes 8388608
  49.2 14.0 %slice-start.7 = ((s8[16777216]{0:T(1024)(128)(4,1)}), s8[4194304]{0:T(1024)(128)(4,1)S(1)}, s32[]{:S(2)}) async-start(s8[16777216]{0:T(1024)(128)(4,1)} %bitcast.12), calls=%async_computation.12 | async-start | bytes 8388608
  63.2 3.2 %collective-permute-start.4 = (bf16[8,144,128]{2,1,0:T(8,128)(2,1)S(1)}, bf16[8,144,128]{2,1,0:T(8,128)(2,1)S(1)}, u32[]{:S(2)}, u32[]{:S(2)}) collective-permute-start(bf16[8,144,128]{2,1,0:T(8,128)(2,1)S(1)} %all_to_all.28.refs_0_), channel_id=1, source_target_pairs={{0,1},{1,0},{2,3},{3,2},{4,5},{5,4},{6,7},{7,6},{8,9},{9,8},{10,11... | collective-permute-start | bytes 884744 | tf_op jit(solution)/shard_map/ppermute | solution.py:72
  71.2 2.1 %collective-permute-start.5 = (bf16[8,32,512]{2,1,0:T(8,128)(2,1)S(1)}, bf16[8,32,512]{2,1,0:T(8,128)(2,1)S(1)}, u32[]{:S(2)}, u32[]{:S(2)}) collective-permute-start(bf16[8,32,512]{2,1,0:T(8,128)(2,1)S(1)} %get-tuple-element.66), channel_id=1, source_target_pairs={{0,1},{1,0},{2,3},{3,2},{4,5},{5,4},{6,7},{7,6},{8,9},{9,8},{10,11... | collective-permute-start | bytes 786440 | tf_op jit(solution)/shard_map/ppermute | solution.py:72
